TPU v7x, 32 devices: a whole 2x2x4 slice. The times are simulated.
32 devices in a mesh: dp: 16 (over z, x, core), seq: 2 (over y).
Axes of the slice: x: 2, y: 2, z: 4, core: 2. Of those that a mesh axis runs over, the one named last changes fastest.
Arguments:
- queries: bfloat16 [4096, 4096], P(('dp', 'seq')), may hold values from -48 to 48
- keys: bfloat16 [4096, 1024], P(('dp', 'seq')), may hold values from -6 to 6
- values: bfloat16 [4096, 1024], P(('dp', 'seq')), may hold values from -6 to 6
- out_grad: bfloat16 [4096, 4096], P(('dp', 'seq')), may hold values from -6 to 6
- normed: bfloat16 [4096, 4096], P(('dp', 'seq')), may hold values from -6 to 6
Outputs:
- query_grad: bfloat16 [4096, 4096], P(('dp', 'seq'))
- key_weight_grad: float32 [4096, 1024], P('dp', 'seq')
- value_weight_grad: float32 [4096, 1024], P('dp', 'seq')
All inputs are finite; a program needn't handle non-finite values.
Results may differ from a plain program's by a relative error of at most 0.0055.
Values may be sent and summed in bfloat16 or wider, within the bound.
No kernel may reach another device: no remote copies, remote signals or barrier semaphores. Data moves between devices by JAX's collectives and lax.ppermute only.
A program may use at most 128 MiB of HBM per device.

v0:
```python
import math

import jax
import jax.numpy as jnp
from jax import lax
from jax.sharding import PartitionSpec as P

HD = 128


def unrotate(grad, position):
    half = HD // 2
    freqs = jnp.exp(-math.log(500000.0) * (2.0 * jnp.arange(half).astype(jnp.float32) / HD))
    angle = position.astype(jnp.float32)[:, None] * freqs[None, :]
    cosine = jnp.cos(angle)[:, None, :]
    sine = jnp.sin(angle)[:, None, :]
    first = grad[..., :half]
    second = grad[..., half:]
    return jnp.concatenate(
        [first * cosine + second * sine, second * cosine - first * sine], axis=-1
    )


def local(queries, keys, values, out_grad, normed):
    head_q, head_k, head_v, head_g = (
        lax.all_to_all(queries, "seq", split_axis=1, concat_axis=0, tiled=True),
        lax.all_to_all(keys, "seq", split_axis=1, concat_axis=0, tiled=True),
        lax.all_to_all(values, "seq", split_axis=1, concat_axis=0, tiled=True),
        lax.all_to_all(out_grad, "seq", split_axis=1, concat_axis=0, tiled=True),
    )
    length = head_q.shape[0]
    heads = head_q.shape[1] // HD
    kv_heads = head_k.shape[1] // HD
    groups = heads // kv_heads
    scale = 1.0 / math.sqrt(HD)
    block = length if length <= 512 else max(512, length // 8)
    starts = list(range(0, length, block))
    query_parts = [[None] * heads for first in starts]
    key_groups = []
    value_groups = []
    for group in range(kv_heads):
        low = group * HD
        high = low + HD
        key_acc = jnp.zeros((length, HD), jnp.float32)
        value_acc = jnp.zeros((length, HD), jnp.float32)
        for number, first in enumerate(starts):
            last = first + block
            query_pos = first + jnp.arange(block)[:, None]
            key_pos = jnp.arange(last)[None, :]
            allowed = key_pos <= query_pos
            key_block = head_k[:last, low:high]
            value_block = head_v[:last, low:high]
            for member in range(groups):
                head = group * groups + member
                query_block = head_q[first:last, head * HD : (head + 1) * HD]
                grad_block = head_g[first:last, head * HD : (head + 1) * HD]
                scores = (
                    lax.dot_general(
                        query_block,
                        key_block,
                        (((1,), (1,)), ((), ())),
                        preferred_element_type=jnp.float32,
                    )
                    * scale
                )
                scores = jnp.where(allowed, scores, -jnp.inf)
                top = jnp.max(scores, axis=1, keepdims=True)
                expo = jnp.where(allowed, jnp.exp(scores - top), 0.0)
                probs = expo / jnp.sum(expo, axis=1, keepdims=True)
                probs_b = probs.astype(jnp.bfloat16)
                value_acc = value_acc.at[:last].add(
                    lax.dot_general(
                        probs_b,
                        grad_block,
                        (((0,), (0,)), ((), ())),
                        preferred_element_type=jnp.float32,
                    )
                )
                prob_grad = lax.dot_general(
                    grad_block,
                    value_block,
                    (((1,), (1,)), ((), ())),
                    preferred_element_type=jnp.float32,
                )
                delta = jnp.sum(probs * prob_grad, axis=1, keepdims=True)
                score_grad = (probs * (prob_grad - delta) * scale).astype(jnp.bfloat16)
                query_parts[number][head] = jnp.dot(
                    score_grad, key_block, preferred_element_type=jnp.float32
                ).astype(jnp.bfloat16)
                key_acc = key_acc.at[:last].add(
                    lax.dot_general(
                        score_grad,
                        query_block,
                        (((0,), (0,)), ((), ())),
                        preferred_element_type=jnp.float32,
                    )
                )
        key_groups.append(key_acc)
        value_groups.append(value_acc)
    head_query_grad = jnp.concatenate(
        [jnp.concatenate(parts, axis=1) for parts in query_parts], axis=0
    )
    rows_pos = jnp.arange(length)
    key_total = jnp.stack(key_groups, axis=1)
    key_grad = unrotate(key_total, rows_pos).reshape(length, kv_heads * HD).astype(jnp.bfloat16)
    value_grad = jnp.concatenate(value_groups, axis=1).astype(jnp.bfloat16)
    query_grad = lax.all_to_all(head_query_grad, "seq", split_axis=0, concat_axis=1, tiled=True)
    width = normed.shape[1]
    piece = lax.all_gather(normed, "seq", axis=0, tiled=True)
    key_part = lax.dot_general(
        piece, key_grad, (((0,), (0,)), ((), ())), preferred_element_type=jnp.float32
    )
    value_part = lax.dot_general(
        piece, value_grad, (((0,), (0,)), ((), ())), preferred_element_type=jnp.float32
    )
    key_full, value_full = lax.psum((key_part, value_part), "dp")
    share = width // lax.axis_size("dp")
    offset = lax.axis_index("dp") * share
    key_weight_grad = lax.dynamic_slice_in_dim(key_full, offset, share, 0)
    value_weight_grad = lax.dynamic_slice_in_dim(value_full, offset, share, 0)
    return (query_grad, key_weight_grad, value_weight_grad)


def solution(mesh):
    placed = (
        P(("dp", "seq"), None),
        P(("dp", "seq"), None),
        P(("dp", "seq"), None),
        P(("dp", "seq"), None),
        P(("dp", "seq"), None),
    )
    return jax.shard_map(
        local,
        mesh=mesh,
        in_specs=placed,
        out_specs=(P(("dp", "seq"), None), P("dp", "seq"), P("dp", "seq")),
        check_vma=False,
    )
```

profile of v0, /device:TPU:0, one launch (start us, length us, event | category | flops | bytes accessed | tf_op | source)
XLA Modules:
  0.0 419.1 jit_solution(5312784370574780921)
XLA Ops:
  7.2 1.8 copy.27
  9.0 4.2 %all-to-all-start.1 = ((bf16[128,2,512]{0,2,1:T(8,128)(2,1)}), bf16[128,2,512]{0,2,1:T(8,128)(2,1)S(1)}, u32[]{:S(2)}, u32[]{:S(2)}) async-start(bf16[128,2,512]{0,2,1:T(8,128)(2,1)} %bitcast.3), calls=%async_computation.1 | async-start | bytes 524288 | tf_op jit(solution)/shard_map/all_to_all | solution.py:27
  13.2 1.8 copy.31
  15.0 4.1 all-to-all-done.1
  19.1 3.4 all-to-all-start.3
  22.5 2.3 copy.25
  24.8 2.9 all-to-all-done.3
  27.7 3.6 all-to-all-start
  32.0 2.3 copy.29
  34.3 1.0 multiply_cosine_fusion
  36.3 7.1 %all-to-all-done = bf16[128,2,2048]{0,2,1:T(8,128)(2,1)S(1)} async-done(((bf16[128,2,2048]{0,2,1:T(8,128)(2,1)}), bf16[128,2,2048]{0,2,1:T(8,128)(2,1)S(1)}, u32[]{:S(2)}, u32[]{:S(2)}) %all-to-all-start) | async-done | bytes 1048608 | tf_op jit(solution)/shard_map/all_to_all | solution.py:26
  43.4 3.6 all-to-all-start.2
  47.6 0.9 fusion.248
  49.2 0.9 fusion.252
  50.1 0.9 fusion.253
  51.0 0.9 fusion.254
  52.1 0.9 fusion.256
  53.0 0.9 fusion.257
  53.9 0.9 fusion.258
  54.9 0.9 fusion.259
  55.7 0.9 fusion.260
  56.7 0.9 fusion.261
  57.6 0.9 fusion.262
  58.5 0.9 fusion.263
  59.4 12.5 %all-to-all-done.2 = bf16[128,2,2048]{0,2,1:T(8,128)(2,1)S(1)} async-done(((bf16[128,2,2048]{0,2,1:T(8,128)(2,1)}), bf16[128,2,2048]{0,2,1:T(8,128)(2,1)S(1)}, u32[]{:S(2)}, u32[]{:S(2)}) %all-to-all-start.2) | async-done | bytes 1048608 | tf_op jit(solution)/shard_map/all_to_all | solution.py:29
  71.9 1.3 copy.30
  73.2 1.1 fusion.72
  74.3 1.2 fusion.82
  75.5 1.3 multiply_reduce_fusion.3
  76.8 1.0 fusion.64
  77.8 1.2 multiply_reduce_fusion.7
  79.1 1.2 fusion.87
  80.3 1.1 fusion.56
  81.4 1.2 multiply_reduce_fusion.11
  82.6 1.2 fusion.92
  89.2 0.9 convolution_add_fusion.2
  91.0 1.6 fusion.23
  99.0 6.2 %convolution_bitcast_fusion.1 = f32[4096,512]{0,1:T(8,128)} fusion(bf16[256,512]{0,1:T(8,128)(2,1)S(1)} %bitcast.169, bf16[256,4096]{1,0:T(8,128)(2,1)} %all-gather.2.cloned.1.call-done), kind=kOutput, calls=%fused_computation.1 | convolution fusion | flops 1073741824 | bytes 10747904 | tf_op jit(solution)/shard_map/dot_general | solution.py:110
  105.2 4.5 %convolution_bitcast_fusion = f32[4096,512]{0,1:T(8,128)} fusion(bf16[256,4096]{1,0:T(8,128)(2,1)S(1)} %copy-done, bf16[256,128]{0,1:T(8,128)(2,1)S(1)} %copy-done.25, bf16[256,128]{0,1:T(8,128)(2,1)S(1)} %fusion.22, bf16[256,128]{0,1:T(8,128)(2,1)S(1)} %fusion.21, bf16[256,128]{0,1:T(8,128)(2,1)S(1)} %fusion.20), kind=kOutput, calls=%fused_computation | convolution fusion | flops 1074790400 | bytes 10747904 | tf_op jit(solution)/shard_map/dot_general | solution.py:113
  109.7 0.9 copy-done.21
  114.1 1.0 copy_bitcast_fusion
  115.2 3.6 all-to-all-start.4
  118.8 10.3 %all-to-all-done.4 = bf16[2,128,2048]{1,2,0:T(8,128)(2,1)S(1)} async-done(((bf16[2,128,2048]{1,2,0:T(8,128)(2,1)}), bf16[2,128,2048]{1,2,0:T(8,128)(2,1)S(1)}, u32[]{:S(2)}, u32[]{:S(2)}) %all-to-all-start.4) | async-done | bytes 1048608 | tf_op jit(solution)/shard_map/all_to_all | solution.py:107
  129.0 1.3 copy.34
  130.3 278.6 %all-reduce.3.cloned.1.call-done = (f32[4096,512]{0,1:T(8,128)}, f32[4096,512]{0,1:T(8,128)}) async-done(((f32[4096,512]{0,1:T(8,128)}, f32[4096,512]{0,1:T(8,128)}), (f32[4096,512]{0,1:T(8,128)}, f32[4096,512]{0,1:T(8,128)})) %all-reduce.3.cloned.1.call-update) | async-done | bytes 16777232 | tf_op jit(solution)/shard_map/psum | solution.py:116
  408.9 1.3 constant_dynamic-slice_fusion
  410.2 1.0 copy.35
  411.2 1.0 copy.36
  (193 shorter events, 18.7 us)
Async XLA Ops:
  9.0 10.1 %all-to-all-start.1 = ((bf16[128,2,512]{0,2,1:T(8,128)(2,1)}), bf16[128,2,512]{0,2,1:T(8,128)(2,1)S(1)}, u32[]{:S(2)}, u32[]{:S(2)}) async-start(bf16[128,2,512]{0,2,1:T(8,128)(2,1)} %bitcast.3), calls=%async_computation.1 | async-start | bytes 524288 | tf_op jit(solution)/shard_map/all_to_all | solution.py:27
  19.1 8.6 %all-to-all-start.3 = ((bf16[128,2,512]{0,2,1:T(8,128)(2,1)}), bf16[128,2,512]{0,2,1:T(8,128)(2,1)S(1)}, u32[]{:S(2)}, u32[]{:S(2)}) async-start(bf16[128,2,512]{0,2,1:T(8,128)(2,1)} %bitcast.9), calls=%async_computation.3 | async-start | bytes 524288 | tf_op jit(solution)/shard_map/all_to_all | solution.py:28
  27.7 15.7 %all-to-all-start = ((bf16[128,2,2048]{0,2,1:T(8,128)(2,1)}), bf16[128,2,2048]{0,2,1:T(8,128)(2,1)S(1)}, u32[]{:S(2)}, u32[]{:S(2)}) async-start(bf16[128,2,2048]{0,2,1:T(8,128)(2,1)} %bitcast), calls=%async_computation | async-start | bytes 2097152 | tf_op jit(solution)/shard_map/all_to_all | solution.py:26
  31.3 67.7 %all-gather.2.cloned.1.call-start = ((), (), s32[]{:S(2)}) async-start(), calls=%async_computation.5 | async-start | bytes 3145728 | tf_op jit(solution)/shard_map/all_gather | solution.py:109
  43.4 28.4 %all-to-all-start.2 = ((bf16[128,2,2048]{0,2,1:T(8,128)(2,1)}), bf16[128,2,2048]{0,2,1:T(8,128)(2,1)S(1)}, u32[]{:S(2)}, u32[]{:S(2)}) async-start(bf16[128,2,2048]{0,2,1:T(8,128)(2,1)} %bitcast.6), calls=%async_computation.2 | async-start | bytes 2097152 | tf_op jit(solution)/shard_map/all_to_all | solution.py:29
  47.0 361.9 %all-reduce.3.cloned.1.call-start = ((), (), s32[]{:S(2)}) async-start(), calls=%async_computation.6 | async-start | bytes 33554432 | tf_op jit(solution)/shard_map/psum | solution.py:116
  48.5 35.4 %copy-start.28 = (f32[256]{0:T(256)}, f32[256]{0:T(256)S(1)}, u32[]{:S(2)}) copy-start(f32[256]{0:T(256)S(1)} %get-tuple-element.661) | copy-start | bytes 3076
  48.7 44.1 %copy-start.3 = (f32[256,256]{0,1:T(8,128)}, f32[256,256]{0,1:T(8,128)S(1)}, u32[]{:S(2)}) copy-start(f32[256,256]{0,1:T(8,128)S(1)} %get-tuple-element.666) | copy-start | bytes 786436
  48.9 44.0 %copy-start.1 = (f32[256,256]{0,1:T(8,128)}, f32[256,256]{0,1:T(8,128)S(1)}, u32[]{:S(2)}) copy-start(f32[256,256]{0,1:T(8,128)S(1)} %get-tuple-element.670) | copy-start | bytes 786436
  50.1 34.1 %copy-start.44 = (f32[256]{0:T(256)}, f32[256]{0:T(256)S(1)}, u32[]{:S(2)}) copy-start(f32[256]{0:T(256)S(1)} %get-tuple-element.677) | copy-start | bytes 3076
  51.0 34.2 %copy-start.30 = (f32[256]{0:T(256)}, f32[256]{0:T(256)S(1)}, u32[]{:S(2)}) copy-start(f32[256]{0:T(256)S(1)} %get-tuple-element.681) | copy-start | bytes 3076
  51.9 33.6 %copy-start.26 = (f32[256]{0:T(256)}, f32[256]{0:T(256)S(1)}, u32[]{:S(2)}) copy-start(f32[256]{0:T(256)S(1)} %get-tuple-element.685) | copy-start | bytes 3076
  52.1 33.7 %copy-start.5 = (f32[256,256]{0,1:T(8,128)}, f32[256,256]{0,1:T(8,128)S(1)}, u32[]{:S(2)}) copy-start(f32[256,256]{0,1:T(8,128)S(1)} %get-tuple-element.690) | copy-start | bytes 786436
  53.9 32.2 %copy-start.42 = (f32[256]{0:T(256)}, f32[256]{0:T(256)S(1)}, u32[]{:S(2)}) copy-start(f32[256]{0:T(256)S(1)} %get-tuple-element.697) | copy-start | bytes 3076
  54.8 31.6 %copy-start.34 = (f32[256]{0:T(256)}, f32[256]{0:T(256)S(1)}, u32[]{:S(2)}) copy-start(f32[256]{0:T(256)S(1)} %get-tuple-element.701) | copy-start | bytes 3076
  55.7 31.0 %copy-start.32 = (f32[256]{0:T(256)}, f32[256]{0:T(256)S(1)}, u32[]{:S(2)}) copy-start(f32[256]{0:T(256)S(1)} %get-tuple-element.705) | copy-start | bytes 3076
  57.6 29.5 %copy-start.40 = (f32[256]{0:T(256)}, f32[256]{0:T(256)S(1)}, u32[]{:S(2)}) copy-start(f32[256]{0:T(256)S(1)} %get-tuple-element.713) | copy-start | bytes 3076
  58.5 28.9 %copy-start.38 = (f32[256]{0:T(256)}, f32[256]{0:T(256)S(1)}, u32[]{:S(2)}) copy-start(f32[256]{0:T(256)S(1)} %get-tuple-element.717) | copy-start | bytes 3076
  59.4 28.4 %copy-start.36 = (f32[256]{0:T(256)}, f32[256]{0:T(256)S(1)}, u32[]{:S(2)}) copy-start(f32[256]{0:T(256)S(1)} %get-tuple-element.721) | copy-start | bytes 3076
  73.2 10.7 %copy-start.8 = (f32[256,256]{0,1:T(8,128)S(1)}, f32[256,256]{0,1:T(8,128)}, u32[]{:S(2)}) copy-start(f32[256,256]{0,1:T(8,128)} %get-tuple-element.662) | copy-start | bytes 786436
  73.2 10.8 %copy-start.19 = (bf16[2,128,2048]{2,1,0:T(8,128)(2,1)S(1)}, bf16[2,128,2048]{2,1,0:T(8,128)(2,1)}, u32[]{:S(2)}) copy-start(bf16[2,128,2048]{2,1,0:T(8,128)(2,1)} %copy.30) | copy-start | bytes 3145732
  73.2 10.8 %copy-start.24 = (bf16[2,128,512]{2,1,0:T(8,128)(2,1)S(1)}, bf16[2,128,512]{2,1,0:T(8,128)(2,1)}, u32[]{:S(2)}) copy-start(bf16[2,128,512]{2,1,0:T(8,128)(2,1)} %copy.32) | copy-start | bytes 786436
  73.2 11.9 %copy-start.9 = (f32[256,256]{0,1:T(8,128)S(1)}, f32[256,256]{0,1:T(8,128)}, u32[]{:S(2)}) copy-start(f32[256,256]{0,1:T(8,128)} %get-tuple-element.682) | copy-start | bytes 786436
  74.3 11.1 %copy-start.7 = (f32[256,256]{0,1:T(8,128)S(1)}, f32[256,256]{0,1:T(8,128)}, u32[]{:S(2)}) copy-start(f32[256,256]{0,1:T(8,128)} %get-tuple-element.686) | copy-start | bytes 786436
  79.1 7.0 %copy-start.15 = (f32[256,256]{0,1:T(8,128)S(1)}, f32[256,256]{0,1:T(8,128)}, u32[]{:S(2)}) copy-start(f32[256,256]{0,1:T(8,128)} %get-tuple-element.698) | copy-start | bytes 786436
  80.3 6.0 %copy-start.11 = (f32[256,256]{0,1:T(8,128)S(1)}, f32[256,256]{0,1:T(8,128)}, u32[]{:S(2)}) copy-start(f32[256,256]{0,1:T(8,128)} %get-tuple-element.702) | copy-start | bytes 786436
  82.6 4.0 copy-start.10
  85.1 3.2 copy-start.17
  85.2 3.4 copy-start.16
  85.2 3.4 copy-start.45
  85.4 3.5 copy-start.29
  86.3 6.2 %copy-start.43 = (f32[256]{0:T(256)S(1)}, f32[256]{0:T(256)}, u32[]{:S(2)}) copy-start(f32[256]{0:T(256)} %copy-done.42) | copy-start | bytes 3076
  87.0 6.1 %copy-start.31 = (f32[256]{0:T(256)S(1)}, f32[256]{0:T(256)}, u32[]{:S(2)}) copy-start(f32[256]{0:T(256)} %copy-done.30) | copy-start | bytes 3076
  87.0 6.1 %copy-start.27 = (f32[256]{0:T(256)S(1)}, f32[256]{0:T(256)}, u32[]{:S(2)}) copy-start(f32[256]{0:T(256)} %copy-done.26) | copy-start | bytes 3076
  87.1 6.2 %copy-start.6 = (f32[256,256]{0,1:T(8,128)S(1)}, f32[256,256]{0,1:T(8,128)}, u32[]{:S(2)}) copy-start(f32[256,256]{0,1:T(8,128)} %copy-done.5) | copy-start | bytes 786436
  87.4 6.1 %copy-start.35 = (f32[256]{0:T(256)S(1)}, f32[256]{0:T(256)}, u32[]{:S(2)}) copy-start(f32[256]{0:T(256)} %copy-done.34) | copy-start | bytes 3076
  87.6 5.9 %copy-start.33 = (f32[256]{0:T(256)S(1)}, f32[256]{0:T(256)}, u32[]{:S(2)}) copy-start(f32[256]{0:T(256)} %copy-done.32) | copy-start | bytes 3076
  87.6 6.0 %copy-start.41 = (f32[256]{0:T(256)S(1)}, f32[256]{0:T(256)}, u32[]{:S(2)}) copy-start(f32[256]{0:T(256)} %copy-done.40) | copy-start | bytes 3076
  87.7 6.0 %copy-start.39 = (f32[256]{0:T(256)S(1)}, f32[256]{0:T(256)}, u32[]{:S(2)}) copy-start(f32[256]{0:T(256)} %copy-done.38) | copy-start | bytes 3076
  87.9 5.9 %copy-start.37 = (f32[256]{0:T(256)S(1)}, f32[256]{0:T(256)}, u32[]{:S(2)}) copy-start(f32[256]{0:T(256)} %copy-done.36) | copy-start | bytes 3076
  89.0 3.8 copy-start.20
  91.0 5.7 %copy-start.22 = (f32[256,64]{0,1:T(8,128)S(1)}, f32[256,64]{0,1:T(8,128)}, u32[]{:S(2)}) copy-start(f32[256,64]{0,1:T(8,128)} %get-tuple-element.659) | copy-start | bytes 196612
  91.0 5.7 %copy-start.23 = (f32[256,64]{0,1:T(8,128)S(1)}, f32[256,64]{0,1:T(8,128)}, u32[]{:S(2)}) copy-start(f32[256,64]{0,1:T(8,128)} %get-tuple-element.660) | copy-start | bytes 196612
  93.8 4.4 %copy-start.4 = (f32[256,256]{0,1:T(8,128)S(1)}, f32[256,256]{0,1:T(8,128)}, u32[]{:S(2)}) copy-start(f32[256,256]{0,1:T(8,128)} %copy-done.3) | copy-start | bytes 786436
  94.2 4.3 %copy-start.2 = (f32[256,256]{0,1:T(8,128)S(1)}, f32[256,256]{0,1:T(8,128)}, u32[]{:S(2)}) copy-start(f32[256,256]{0,1:T(8,128)} %copy-done.1) | copy-start | bytes 786436
  97.8 7.4 %copy-start.25 = (bf16[256,128]{0,1:T(8,128)(2,1)S(1)}, bf16[256,128]{0,1:T(8,128)(2,1)}, u32[]{:S(2)}) copy-start(bf16[256,128]{0,1:T(8,128)(2,1)} %fusion.23) | copy-start | bytes 196612
  99.0 6.2 %copy-start = (bf16[256,4096]{1,0:T(8,128)(2,1)S(1)}, bf16[256,4096]{1,0:T(8,128)(2,1)}, u32[]{:S(2)}) copy-start(bf16[256,4096]{1,0:T(8,128)(2,1)} %all-gather.2.cloned.1.call-done) | copy-start | bytes 6291460
  115.2 13.9 %all-to-all-start.4 = ((bf16[2,128,2048]{1,2,0:T(8,128)(2,1)}), bf16[2,128,2048]{1,2,0:T(8,128)(2,1)S(1)}, u32[]{:S(2)}, u32[]{:S(2)}) async-start(bf16[2,128,2048]{1,2,0:T(8,128)(2,1)} %copy_bitcast_fusion), calls=%async_computation.4 | async-start | bytes 2097152 | tf_op jit(solution)/shard_map/all_to_all | solution.py:107
  (5 other events, 13.1 us)
Sparse Core Ops, SparseCore 0:
  33.6 46.2 all-gather.1
  109.8 299.0 all-reduce.2
where the time goes:
time: 420 us; the launch traced here: 419 us
  waiting for transfers between devices  316 us (75%)
  matrix products  45.3 us (11%)
  starting transfers between devices  18.5 us (4%)
  local copies, waits for them, and re-layouts  17.6 us (4%)
  between operations  14.9 us (4%)
  other arithmetic  6.5 us (2%)
    psum x1, waiting for transfers between devices, local(): key_full, value_full = lax.psum((key_part, value_part), 'dp')  279 us
    all_to_all x1, waiting for transfers between devices, local(): lax.all_to_all(out_grad, 'seq', split_axis=1, concat_axis=0, tiled=True)  12.5 us
    unnamed x99, local copies, waits for them, and re-layouts  12.5 us
    dot_general x16, matrix products, local(): lax.dot_general(query_block, key_block, (((1,), (1,)), ((), ())), preferr...  11.7 us
    all_to_all x1, waiting for transfers between devices, local(): lax.all_to_all(head_query_grad, 'seq', split_axis=0, concat_axis=1, tiled...  10.3 us
    dot_general x16, matrix products, local(): lax.dot_general(probs_b, grad_block, (((0,), (0,)), ((), ())), preferred_...  9.27 us
  transfers between devices with their start and end apart: 7, of which 6 were waited for; matrix products, arithmetic and copies ran while one was open for 13% of the time, Pallas kernels for 0%

commit v1 on v0

--- a/solution.py
+++ b/solution.py
@@ -2,10 +2,17 @@
 
 import jax
 import jax.numpy as jnp
+import numpy as np
 from jax import lax
+from jax.experimental import pallas as pl
+from jax.experimental.pallas import tpu as pltpu
 from jax.sharding import PartitionSpec as P
 
 HD = 128
+NC = 2
+BF = jnp.bfloat16
+F32 = jnp.float32
+VMEM_LIMIT = 40 * 1024 * 1024
 
 
 def unrotate(grad, position):
@@ -21,7 +28,7 @@
     )
 
 
-def local(queries, keys, values, out_grad, normed):
+def general_local(queries, keys, values, out_grad, normed):
     head_q, head_k, head_v, head_g = (
         lax.all_to_all(queries, "seq", split_axis=1, concat_axis=0, tiled=True),
         lax.all_to_all(keys, "seq", split_axis=1, concat_axis=0, tiled=True),
@@ -121,18 +128,312 @@
     return (query_grad, key_weight_grad, value_weight_grad)
 
 
+CORE, XBIT, ZLOW, ZHIGH = 1, 2, 4, 8
+
+
+def flip(array, mask):
+    return lax.ppermute(array, "dp", [(i, i ^ mask) for i in range(16)])
+
+
+def swap_seq(array):
+    return lax.ppermute(array, "seq", [(0, 1), (1, 0)])
+
+
+def params():
+    return pltpu.CompilerParams(vmem_limit_bytes=VMEM_LIMIT)
+
+
+def rotary_tables(length):
+    half = HD // 2
+    freqs = np.exp(-math.log(500000.0) * (2.0 * np.arange(half, dtype=np.float64) / HD))
+    angle = np.arange(length, dtype=np.float64)[:, None] * freqs[None, :]
+    cosine = np.concatenate([np.cos(angle), np.cos(angle)], axis=1)
+    sine = np.concatenate([np.sin(angle), -np.sin(angle)], axis=1)
+    return cosine.astype(np.float32), sine.astype(np.float32)
+
+
+def pack_kv(keys, values):
+    rows = keys.shape[0]
+    wide = keys.shape[1] // (2 * NC)
+
+    def body(k_ref, v_ref, *outs):
+        for chunk, out in enumerate(outs):
+            for number, ref in enumerate((k_ref, v_ref)):
+                for half in range(2):
+                    low = (half * NC + chunk) * wide
+                    at = (number * 2 + half) * wide
+                    out[:, at : at + wide] = ref[:, low : low + wide]
+
+    return pl.pallas_call(
+        body,
+        out_shape=[jax.ShapeDtypeStruct((rows, 4 * wide), BF)] * NC,
+        compiler_params=params(),
+        name="pack_kv",
+    )(keys, values)
+
+
+def split_normed(normed, me):
+    rows, width = normed.shape
+    share = width // 16
+
+    def body(me_ref, x_ref, same_ref, other_ref):
+        mine = me_ref[0]
+        for core, out in enumerate((same_ref, other_ref)):
+            for place in range(8):
+                zlow, xbit, zhigh = place >> 2, (place >> 1) & 1, place & 1
+                mask = zhigh * ZHIGH + zlow * ZLOW + xbit * XBIT + core
+                low = pl.multiple_of((mine ^ mask) * share, share)
+                out[:, place * share : (place + 1) * share] = x_ref[:, pl.ds(low, share)]
+
+    vmem = pl.BlockSpec(memory_space=pltpu.VMEM)
+    return pl.pallas_call(
+        body,
+        out_shape=[jax.ShapeDtypeStruct((rows, width // 2), BF)] * 2,
+        in_specs=[pl.BlockSpec(memory_space=pltpu.SMEM), vmem],
+        out_specs=[vmem, vmem],
+        compiler_params=params(),
+        name="split_normed",
+    )(me, normed)
+
+
+def pack_normed(same, recv):
+    rows, width = same.shape
+    wide = width // 4
+
+    def body(a_ref, b_ref, *outs):
+        for place, out in enumerate(outs):
+            out[:rows, :] = a_ref[:, place * wide : (place + 1) * wide]
+            out[rows:, :] = b_ref[:, place * wide : (place + 1) * wide]
+
+    return pl.pallas_call(
+        body,
+        out_shape=[jax.ShapeDtypeStruct((2 * rows, wide), BF)] * 4,
+        compiler_params=params(),
+        name="pack_normed",
+    )(same, recv)
+
+
+def attention(chunk, seq_at, queries, out_grad, keys, values, kv_recv, cosine, sine, grad_so_far):
+    rows, width = queries.shape
+    wide = width // (2 * NC)
+    kv_wide = keys.shape[1] // (2 * NC)
+    kv_heads = kv_wide // HD
+    groups = wide // kv_wide
+    span = groups * rows
+    scale = 1.0 / math.sqrt(HD)
+
+    def rotate(grad, cos, sin):
+        return grad * cos + pltpu.roll(grad, HD // 2, 1) * sin
+
+    def nt(a, b):
+        return lax.dot_general(a, b, (((1,), (1,)), ((), ())), preferred_element_type=F32)
+
+    def tn(a, b):
+        return lax.dot_general(a, b, (((0,), (0,)), ((), ())), preferred_element_type=F32)
+
+    def body(at_ref, q_ref, g_ref, k_ref, v_ref, ko_ref, vo_ref, cos_ref, sin_ref, *rest):
+        qg_ref, keep_a, keep_b, send = rest[-4:]
+        other = pl.program_id(0)
+        late = at_ref[0]
+
+        def stack(ref, head):
+            return jnp.concatenate(
+                [
+                    ref[:, (head * groups + m) * HD : (head * groups + m + 1) * HD]
+                    for m in range(groups)
+                ],
+                axis=0,
+            )
+
+        def one_head(head, is_late):
+            cols = slice(head * HD, (head + 1) * HD)
+            qs = stack(q_ref, head)
+            gs = stack(g_ref, head)
+            ks = k_ref[:, cols]
+            vs = v_ref[:, cols]
+            if is_late:
+                ks = jnp.concatenate([ko_ref[:, cols], ks], axis=0)
+                vs = jnp.concatenate([vo_ref[:, cols], vs], axis=0)
+            count = ks.shape[0]
+            scores = nt(ks, qs) * scale
+            key_pos = lax.broadcasted_iota(jnp.int32, (count, span), 0) - (count - rows)
+            query_pos = lax.broadcasted_iota(jnp.int32, (count, span), 1) % rows
+            scores = jnp.where(key_pos <= query_pos, scores, -1e30)
+            top = jnp.max(scores, axis=0, keepdims=True)
+            expo = jnp.exp(scores - top)
+            probs = expo * (1.0 / jnp.sum(expo, axis=0, keepdims=True))
+            value_grad = jnp.dot(probs.astype(BF), gs, preferred_element_type=F32)
+            prob_grad = nt(vs, gs)
+            delta = jnp.sum(probs * prob_grad, axis=0, keepdims=True)
+            score_grad = (probs * (prob_grad - delta) * scale).astype(BF)
+            key_grad = jnp.dot(score_grad, qs, preferred_element_type=F32)
+            query_grad = tn(score_grad, ks).astype(BF)
+            for m in range(groups):
+                low = (head * groups + m) * HD
+                qg_ref[:, low : low + HD] = query_grad[m * rows : (m + 1) * rows]
+            first = (rotate(key_grad[:rows], cos_ref[:rows], sin_ref[:rows]), value_grad[:rows])
+            second = None
+            if is_late:
+                second = (
+                    rotate(key_grad[rows:], cos_ref[rows:], sin_ref[rows:]),
+                    value_grad[rows:],
+                )
+            return first, second
+
+        def all_heads(is_late):
+            parts = [one_head(head, is_late) for head in range(kv_heads)]
+
+            def write(first_ref, second_ref, second_at):
+                for head, (first, second) in enumerate(parts):
+                    for number in range(2):
+                        at = slice(number * kv_wide + head * HD, number * kv_wide + (head + 1) * HD)
+                        first_ref[:rows, at] = first[number].astype(first_ref.dtype)
+                        later = jnp.zeros((rows, HD), BF) if second is None else second[number].astype(BF)
+                        second_ref[second_at : second_at + rows, at] = later
+
+            @pl.when(other == 0)
+            def _():
+                write(keep_a, keep_b, 0)
+
+            @pl.when(other == 1)
+            def _():
+                write(send, send, rows)
+
+        @pl.when(late == 1)
+        def _():
+            all_heads(True)
+
+        @pl.when(late == 0)
+        def _():
+            all_heads(False)
+
+    def block(j, at):
+        return (at[0] ^ j) * NC + chunk
+
+    whole = lambda j, at: (0, 0)
+    mine = lambda j, at: (0, block(j, at))
+    specs = [
+        pl.BlockSpec((rows, wide), mine),
+        pl.BlockSpec((rows, wide), mine),
+        pl.BlockSpec((rows, kv_wide), mine),
+        pl.BlockSpec((rows, kv_wide), mine),
+        pl.BlockSpec((rows, kv_wide), lambda j, at: (0, at[0] ^ j)),
+        pl.BlockSpec((rows, kv_wide), lambda j, at: (0, 2 + (at[0] ^ j))),
+        pl.BlockSpec((2 * rows, HD), whole),
+        pl.BlockSpec((2 * rows, HD), whole),
+    ]
+    operands = [queries, out_grad, keys, values, kv_recv, kv_recv, cosine, sine]
+    aliases = {}
+    if grad_so_far is not None:
+        specs.append(pl.BlockSpec(memory_space=pl.ANY))
+        operands.append(grad_so_far)
+        aliases = {9: 0}
+    return pl.pallas_call(
+        body,
+        out_shape=[
+            jax.ShapeDtypeStruct((rows, width), BF),
+            jax.ShapeDtypeStruct((rows, 2 * kv_wide), F32),
+            jax.ShapeDtypeStruct((rows, 2 * kv_wide), BF),
+            jax.ShapeDtypeStruct((2 * rows, 2 * kv_wide), BF),
+        ],
+        grid_spec=pltpu.PrefetchScalarGridSpec(
+            num_scalar_prefetch=1,
+            grid=(2,),
+            in_specs=specs,
+            out_specs=[
+                pl.BlockSpec((rows, wide), mine),
+                pl.BlockSpec((rows, 2 * kv_wide), whole),
+                pl.BlockSpec((rows, 2 * kv_wide), whole),
+                pl.BlockSpec((2 * rows, 2 * kv_wide), whole),
+            ],
+        ),
+        input_output_aliases=aliases,
+        compiler_params=params(),
+        name="attention",
+    )(seq_at, *operands)
+
+
+def project(normed_parts, grads):
+    rows = grads[0].shape[0] // 2
+    wide = grads[0].shape[1]
+    share = normed_parts[0].shape[1] // 2
+
+    def body(*refs):
+        xs, ys = refs[:8], refs[8:16]
+        keep, send = refs[16:]
+        left = jnp.concatenate([ref[...] for ref in xs], axis=0)
+        right = jnp.concatenate(
+            [
+                ys[place * 2 + core][seq * rows : (seq + 1) * rows, :]
+                for place in range(4)
+                for seq in range(2)
+                for core in range(2)
+            ],
+            axis=0,
+        )
+        total = lax.dot_general(
+            left, right, (((0,), (0,)), ((), ())), preferred_element_type=F32
+        )
+        keep[...] = total[:share]
+        send[...] = total[share:].astype(BF)
+
+    return pl.pallas_call(
+        body,
+        out_shape=[
+            jax.ShapeDtypeStruct((share, wide), F32),
+            jax.ShapeDtypeStruct((share, wide), BF),
+        ],
+        compiler_params=params(),
+        name="project",
+    )(*normed_parts, *grads)
+
+
+def cube_local(queries, keys, values, out_grad, normed):
+    seq = lax.axis_index("seq")
+    seq_at = jnp.reshape(seq, (1,)).astype(jnp.int32)
+    me = jnp.reshape(lax.axis_index("dp"), (1,)).astype(jnp.int32)
+    rows = queries.shape[0]
+    cosine, sine = (jnp.asarray(table) for table in rotary_tables(2 * rows))
+
+    kv_recv = [lax.ppermute(part, "seq", [(0, 1)]) for part in pack_kv(keys, values)]
+    same, other = split_normed(normed, me)
+    places = pack_normed(same, flip(other, CORE))
+    places = [places[0]] + [flip(places[n], mask) for n, mask in ((1, XBIT), (2, ZLOW), (3, XBIT | ZLOW))]
+
+    query_grad = None
+    kept, sent = [], []
+    normed_parts = None
+    for chunk in range(NC):
+        query_grad, keep_a, keep_b, send = attention(
+            chunk, seq_at, queries, out_grad, keys, values, kv_recv[chunk], cosine, sine, query_grad
+        )
+        recv = swap_seq(send)
+        early = (keep_a + recv[:rows].astype(F32)).astype(BF)
+        later = jnp.where(seq == 1, keep_b, recv[rows:])
+        mine = jnp.concatenate(
+            [jnp.where(seq == 1, later, early), jnp.where(seq == 1, early, later)], axis=0
+        )
+        gathered = [mine] + [flip(mine, mask) for mask in (XBIT, ZLOW, XBIT | ZLOW)]
+        grads = [part for one in gathered for part in (one, flip(one, CORE))]
+        if normed_parts is None:
+            normed_parts = [part for one in places for part in (one, swap_seq(one))]
+        keep, send = project(normed_parts, grads)
+        kept.append(keep)
+        sent.append(flip(send, ZHIGH))
+    totals = [keep + recv.astype(F32) for keep, recv in zip(kept, sent)]
+    half = totals[0].shape[1] // 2
+    key_weight_grad = jnp.concatenate([one[:, :half] for one in totals], axis=1)
+    value_weight_grad = jnp.concatenate([one[:, half:] for one in totals], axis=1)
+    return (query_grad, key_weight_grad, value_weight_grad)
+
+
 def solution(mesh):
-    placed = (
-        P(("dp", "seq"), None),
-        P(("dp", "seq"), None),
-        P(("dp", "seq"), None),
-        P(("dp", "seq"), None),
-        P(("dp", "seq"), None),
-    )
+    spread = P(("dp", "seq"), None)
+    cube = dict(mesh.shape) == {"dp": 16, "seq": 2}
     return jax.shard_map(
-        local,
+        cube_local if cube else general_local,
         mesh=mesh,
-        in_specs=placed,
-        out_specs=(P(("dp", "seq"), None), P("dp", "seq"), P("dp", "seq")),
+        in_specs=(spread,) * 5,
+        out_specs=(spread, P("dp", "seq"), P("dp", "seq")),
         check_vma=False,
     )

time: 420 us -> 108 us (0.26)
  waiting for transfers between devices: 316 us -> 52.5 us
  matrix products: 45.3 us -> 0 us
  between operations: 14.9 us -> 0.83 us
  starting transfers between devices: 18.5 us -> 31.4 us
  Pallas kernels: 0 us -> 12.4 us
  local copies, waits for them, and re-layouts: 17.6 us -> 7.73 us
    psum x1 -> x0, waiting for transfers between devices: 279 us -> none  [local(): key_full, value_full = lax.psum((key_part, value_part), 'dp')]
    ppermute x0 -> x28, waiting for transfers between devices: none -> 52.5 us  [the longest x20 44.4 us: flip(): return lax.ppermute(array, 'dp', [(i, i ^ mask) for i in range(16)])]
    dot_general x82 -> x0, matrix products: 45.3 us -> none  [the longest x16 11.7 us: local(): lax.dot_general(query_block, key_block, (((1,), (1,)), ((), ())), preferr...]
    all_to_all x5 -> x0, waiting for transfers between devices: 36.9 us -> none  [the longest x1 12.5 us: local(): lax.all_to_all(out_grad, 'seq', split_axis=1, concat_axis=0, tiled=True)]
    ppermute x0 -> x28, starting transfers between devices: none -> 31.4 us  [the longest x20 17.7 us: flip(): return lax.ppermute(array, 'dp', [(i, i ^ mask) for i in range(16)])]
    all_to_all x5 -> x0, starting transfers between devices: 18.4 us -> none  [the longest x1 4.23 us: local(): lax.all_to_all(keys, 'seq', split_axis=1, concat_axis=0, tiled=True)]
    pallas_call x0 -> x7, Pallas kernels: none -> 12.4 us  [the longest x2 7.06 us: attention(): pl.pallas_call(body, out_shape=[jax.ShapeDtypeStruct((rows, width), BF),...]
    unnamed x99 -> x32, local copies, waits for them, and re-layouts: 12.5 us -> 7.66 us
  transfers between devices with their start and end apart: 7 -> 28, of which waited for: 6 -> 9; matrix products, arithmetic and copies ran while one was open for 13% -> 1% of each run, Pallas kernels for 0% -> 11%
where the time goes in v1:
time: 108 us; the launch traced here: 107 us
  waiting for transfers between devices  52.5 us (49%)
  starting transfers between devices  31.4 us (29%)
  Pallas kernels  12.4 us (11%)
  local copies, waits for them, and re-layouts  7.73 us (7%)
  other arithmetic  2.35 us (2%)
    ppermute x20, waiting for transfers between devices, flip(): return lax.ppermute(array, 'dp', [(i, i ^ mask) for i in range(16)])  44.4 us
    ppermute x20, starting transfers between devices, flip(): return lax.ppermute(array, 'dp', [(i, i ^ mask) for i in range(16)])  17.7 us
    unnamed x32, local copies, waits for them, and re-layouts  7.66 us
    ppermute x6, starting transfers between devices, swap_seq(): return lax.ppermute(array, 'seq', [(0, 1), (1, 0)])  7.48 us
    pallas_call x2, Pallas kernels, attention(): pl.pallas_call(body, out_shape=[jax.ShapeDtypeStruct((rows, width), BF),...  7.06 us
    ppermute x6, waiting for transfers between devices, swap_seq(): return lax.ppermute(array, 'seq', [(0, 1), (1, 0)])  6.73 us
    ppermute x2, starting transfers between devices, cube_local(): lax.ppermute(part, 'seq', [(0, 1)])  6.17 us
    pallas_call x2, Pallas kernels, project(): pl.pallas_call(body, out_shape=[jax.ShapeDtypeStruct((share, wide), F32),...  2.54 us
  transfers between devices with their start and end apart: 28, of which 9 were waited for; matrix products, arithmetic and copies ran while one was open for 1% of the time, Pallas kernels for 11%

profile of v1, /device:TPU:0, one launch (start us, length us, event | category | flops | bytes accessed | tf_op | source)
XLA Modules:
  0.0 107.2 jit_solution(4932648093311900974)
XLA Ops:
  0.6 0.9 copy-done.3
  1.6 0.9 copy-done.5
  2.5 0.7 pack_kv.1
  3.3 4.9 %collective-permute-start.1 = (bf16[128,1024]{1,0:T(8,128)(2,1)S(1)}, bf16[128,1024]{1,0:T(8,128)(2,1)S(1)}, u32[]{:S(2)}, u32[]{:S(2)}) collective-permute-start(bf16[128,1024]{1,0:T(8,128)(2,1)S(1)} %get-tuple-element.24), channel_id=1, source_target_pairs={{0,1},{2,3},{4,5},{6,7},{8,9},{10,11},{12,13},{14,15},{16,17},{18,... | collective-permute-start | bytes 786440 | tf_op jit(solution)/shard_map/ppermute | solution.py:398
  8.2 1.2 %copy-done.7 = bf16[128,4096]{1,0:T(8,128)(2,1)S(1)} copy-done((bf16[128,4096]{1,0:T(8,128)(2,1)S(1)}, bf16[128,4096]{1,0:T(8,128)(2,1)}, u32[]{:S(2)}) %copy-start.7) | copy-done | bytes 1048600
  9.4 0.9 split_normed.1
  10.3 0.8 copy-done.12
  11.1 1.3 %collective-permute-start = (bf16[128,1024]{1,0:T(8,128)(2,1)}, bf16[128,1024]{1,0:T(8,128)(2,1)S(1)}, u32[]{:S(2)}, u32[]{:S(2)}) collective-permute-start(bf16[128,1024]{1,0:T(8,128)(2,1)} %get-tuple-element.23), channel_id=1, source_target_pairs={{0,1},{2,3},{4,5},{6,7},{8,9},{10,11},{12,13},{14,15},{16,17},{18,... | collective-permute-start | bytes 786440 | tf_op jit(solution)/shard_map/ppermute | solution.py:398
  12.4 1.3 %collective-permute-done.1.ko_ref.vo_ref = bf16[128,1024]{1,0:T(8,128)(2,1)S(1)} collective-permute-done((bf16[128,1024]{1,0:T(8,128)(2,1)S(1)}, bf16[128,1024]{1,0:T(8,128)(2,1)S(1)}, u32[]{:S(2)}, u32[]{:S(2)}) %collective-permute-start.1) | collective-permute-done | bytes 262176 | tf_op jit(solution)/shard_map/ppermute | solution.py:398
  13.8 1.2 %copy-done.1 = bf16[128,4096]{1,0:T(8,128)(2,1)S(1)} copy-done((bf16[128,4096]{1,0:T(8,128)(2,1)S(1)}, bf16[128,4096]{1,0:T(8,128)(2,1)}, u32[]{:S(2)}) %copy-start.1) | copy-done | bytes 1048600
  15.0 0.9 copy-done.8
  15.9 0.9 copy-done.10
  16.8 3.6 %attention.2 = (bf16[128,4096]{1,0:T(8,128)(2,1)}, f32[128,512]{1,0:T(8,128)S(1)}, bf16[128,512]{1,0:T(8,128)(2,1)S(1)}, bf16[256,512]{1,0:T(8,128)(2,1)}) custom-call(s32[1]{0:T(128)} %bitcast.at_ref, bf16[128,4096]{1,0:T(8,128)(2,1)S(1)} %copy-done, bf16[128,4096]{1,0:T(8,128)(2,1)S(1)} %copy-done.1, bf16[128,1024]{1,0:T(8,128)(2,1)S(1)} %copy-done.4, ...), custom_call_target="tpu_custom_call" | custom-call | tf_op jit(solution)/shard_map/attention/pallas_call | solution.py:331
  20.4 0.7 copy-done.14
  21.1 3.4 %collective-permute-start.10 = (bf16[256,512]{1,0:T(8,128)(2,1)}, bf16[256,512]{1,0:T(8,128)(2,1)}, u32[]{:S(2)}, u32[]{:S(2)}) collective-permute-start(bf16[256,512]{1,0:T(8,128)(2,1)} %get-tuple-element.34), channel_id=1, source_target_pairs={{0,1},{1,0},{2,3},{3,2},{4,5},{5,4},{6,7},{7,6},{8,9},{9,8},{10,11... | collective-permute-start | bytes 786440 | tf_op jit(solution)/shard_map/ppermute | solution.py:139
  24.5 3.5 %attention.3 = (bf16[128,4096]{1,0:T(8,128)(2,1)}, f32[128,512]{1,0:T(8,128)S(1)}, bf16[128,512]{1,0:T(8,128)(2,1)S(1)}, bf16[256,512]{1,0:T(8,128)(2,1)S(1)}) custom-call(s32[1]{0:T(128)} %bitcast.at_ref, bf16[128,4096]{1,0:T(8,128)(2,1)S(1)} %copy-done, bf16[128,4096]{1,0:T(8,128)(2,1)S(1)} %copy-done.2, ...), custom_call_target="tpu_custom_call", output_to_operand_aliasing={{0}: (9, {})} | custom-call | tf_op jit(solution)/shard_map/attention/pallas_call | solution.py:331
  28.0 0.9 collective-permute-start.19
  28.9 1.2 %pack_normed.1 = (bf16[256,512]{1,0:T(8,128)(2,1)S(1)}, bf16[256,512]{1,0:T(8,128)(2,1)S(1)}, bf16[256,512]{1,0:T(8,128)(2,1)S(1)}, bf16[256,512]{1,0:T(8,128)(2,1)S(1)}) custom-call(bf16[128,2048]{1,0:T(8,128)(2,1)S(1)} %copy-done.13, bf16[128,2048]{1,0:T(8,128)(2,1)} %collective-permute-done.2.b_ref), custom_call_target="tpu_custom_call" | custom-call | tf_op jit(solution)/shard_map/pack_normed/pallas_call | solution.py:208
  30.1 1.6 %collective-permute-start.4 = (bf16[256,512]{1,0:T(8,128)(2,1)S(1)}, bf16[256,512]{1,0:T(8,128)(2,1)S(1)}, u32[]{:S(2)}, u32[]{:S(2)}) collective-permute-start(bf16[256,512]{1,0:T(8,128)(2,1)S(1)} %get-tuple-element.30), channel_id=1, source_target_pairs={{0,4},{2,6},{4,0},{6,2},{8,12},{10,14},{12,8},{14,10},{16,20},{18,... | collective-permute-start | bytes 786440 | tf_op jit(solution)/shard_map/ppermute | solution.py:135
  31.6 1.6 %collective-permute-start.6 = (bf16[256,512]{1,0:T(8,128)(2,1)S(1)}, bf16[256,512]{1,0:T(8,128)(2,1)S(1)}, u32[]{:S(2)}, u32[]{:S(2)}) collective-permute-start(bf16[256,512]{1,0:T(8,128)(2,1)S(1)} %get-tuple-element.31), channel_id=1, source_target_pairs={{0,8},{2,10},{4,12},{6,14},{8,0},{10,2},{12,4},{14,6},{16,24},{18,... | collective-permute-start | bytes 786440 | tf_op jit(solution)/shard_map/ppermute | solution.py:135
  33.2 1.0 broadcast_select_fusion.3
  34.3 0.5 collective-permute-start.16
  34.7 1.6 %collective-permute-start.14 = (bf16[256,512]{1,0:T(8,128)(2,1)S(1)}, bf16[256,512]{1,0:T(8,128)(2,1)S(1)}, u32[]{:S(2)}, u32[]{:S(2)}) collective-permute-start(bf16[256,512]{1,0:T(8,128)(2,1)S(1)} %pad_maximum_fusion.2.refs_8_), channel_id=1, source_target_pairs={{0,8},{2,10},{4,12},{6,14},{8,0},{10,2},{12,4},{14,6},{16,24},{18,... | collective-permute-start | bytes 786440 | tf_op jit(solution)/shard_map/ppermute | solution.py:135
  36.3 1.5 %collective-permute-start.12 = (bf16[256,512]{1,0:T(8,128)(2,1)S(1)}, bf16[256,512]{1,0:T(8,128)(2,1)S(1)}, u32[]{:S(2)}, u32[]{:S(2)}) collective-permute-start(bf16[256,512]{1,0:T(8,128)(2,1)S(1)} %pad_maximum_fusion.2.refs_8_), channel_id=1, source_target_pairs={{0,4},{2,6},{4,0},{6,2},{8,12},{10,14},{12,8},{14,10},{16,20},{18,... | collective-permute-start | bytes 786440 | tf_op jit(solution)/shard_map/ppermute | solution.py:135
  37.8 1.5 %collective-permute-done.4.refs_2_ = bf16[256,512]{1,0:T(8,128)(2,1)S(1)} collective-permute-done((bf16[256,512]{1,0:T(8,128)(2,1)S(1)}, bf16[256,512]{1,0:T(8,128)(2,1)S(1)}, u32[]{:S(2)}, u32[]{:S(2)}) %collective-permute-start.4) | collective-permute-done | bytes 262176 | tf_op jit(solution)/shard_map/ppermute | solution.py:135
  39.3 3.3 %collective-permute-start.8 = (bf16[256,512]{1,0:T(8,128)(2,1)S(1)}, bf16[256,512]{1,0:T(8,128)(2,1)S(1)}, u32[]{:S(2)}, u32[]{:S(2)}) collective-permute-start(bf16[256,512]{1,0:T(8,128)(2,1)S(1)} %get-tuple-element.32), channel_id=1, source_target_pairs={{0,12},{2,14},{4,8},{6,10},{8,4},{10,6},{12,0},{14,2},{16,28},{18,... | collective-permute-start | bytes 786440 | tf_op jit(solution)/shard_map/ppermute | solution.py:135
  42.7 0.2 collective-permute-start.3
  42.9 12.1 %collective-permute-done.8.refs_6_ = bf16[256,512]{1,0:T(8,128)(2,1)S(1)} collective-permute-done((bf16[256,512]{1,0:T(8,128)(2,1)S(1)}, bf16[256,512]{1,0:T(8,128)(2,1)S(1)}, u32[]{:S(2)}, u32[]{:S(2)}) %collective-permute-start.8) | collective-permute-done | bytes 262176 | tf_op jit(solution)/shard_map/ppermute | solution.py:135
  55.0 2.5 %collective-permute-start.25 = (bf16[256,512]{1,0:T(8,128)(2,1)S(1)}, bf16[256,512]{1,0:T(8,128)(2,1)S(1)}, u32[]{:S(2)}, u32[]{:S(2)}) collective-permute-start(bf16[256,512]{1,0:T(8,128)(2,1)S(1)} %pad_maximum_fusion.3.refs_8_), channel_id=1, source_target_pairs={{0,12},{2,14},{4,8},{6,10},{8,4},{10,6},{12,0},{14,2},{16,28},{18,... | collective-permute-start | bytes 786440 | tf_op jit(solution)/shard_map/ppermute | solution.py:135
  57.5 0.4 collective-permute-start.23
  57.9 0.5 collective-permute-start.21
  58.5 1.0 collective-permute-start.5
  59.5 1.1 collective-permute-start.7
  60.5 4.5 %collective-permute-done.25.refs_14_ = bf16[256,512]{1,0:T(8,128)(2,1)S(1)} collective-permute-done((bf16[256,512]{1,0:T(8,128)(2,1)S(1)}, bf16[256,512]{1,0:T(8,128)(2,1)S(1)}, u32[]{:S(2)}, u32[]{:S(2)}) %collective-permute-start.25) | collective-permute-done | bytes 262176 | tf_op jit(solution)/shard_map/ppermute | solution.py:135
  65.0 1.0 collective-permute-start.9
  66.0 4.3 %collective-permute-done.23.refs_12_ = bf16[256,512]{1,0:T(8,128)(2,1)S(1)} collective-permute-done((bf16[256,512]{1,0:T(8,128)(2,1)S(1)}, bf16[256,512]{1,0:T(8,128)(2,1)S(1)}, u32[]{:S(2)}, u32[]{:S(2)}) %collective-permute-start.23) | collective-permute-done | bytes 262176 | tf_op jit(solution)/shard_map/ppermute | solution.py:135
  70.3 0.5 collective-permute-start.15
  70.9 2.5 %collective-permute-done.7.refs_5_ = bf16[256,512]{1,0:T(8,128)(2,1)S(1)} collective-permute-done((bf16[256,512]{1,0:T(8,128)(2,1)S(1)}, bf16[256,512]{1,0:T(8,128)(2,1)S(1)}, u32[]{:S(2)}, u32[]{:S(2)}) %collective-permute-start.7) | collective-permute-done | bytes 262176 | tf_op jit(solution)/shard_map/ppermute | solution.py:139
  73.3 4.3 %collective-permute-done.9.refs_7_ = bf16[256,512]{1,0:T(8,128)(2,1)S(1)} collective-permute-done((bf16[256,512]{1,0:T(8,128)(2,1)S(1)}, bf16[256,512]{1,0:T(8,128)(2,1)S(1)}, u32[]{:S(2)}, u32[]{:S(2)}) %collective-permute-start.9) | collective-permute-done | bytes 262176 | tf_op jit(solution)/shard_map/ppermute | solution.py:139
  77.6 0.5 collective-permute-start.24
  78.2 1.3 %project.2 = (f32[256,512]{1,0:T(8,128)S(1)}, bf16[256,512]{1,0:T(8,128)(2,1)S(1)}) custom-call(bf16[256,512]{1,0:T(8,128)(2,1)S(1)} %get-tuple-element.29.refs_0_, bf16[256,512]{1,0:T(8,128)(2,1)S(1)} %collective-permute-done.3.refs_1_, bf16[256,512]{1,0:T(8,128)(2,1)S(1)} %collective-permute-done.4.refs_2_, ...), custom_call_target="tpu_custom_call" | custom-call | tf_op jit(solution)/shard_map/project/pallas_call | solution.py:380
  79.5 2.6 %collective-permute-start.18 = (bf16[256,512]{1,0:T(8,128)(2,1)S(1)}, bf16[256,512]{1,0:T(8,128)(2,1)S(1)}, u32[]{:S(2)}, u32[]{:S(2)}) collective-permute-start(bf16[256,512]{1,0:T(8,128)(2,1)S(1)} %get-tuple-element.37), channel_id=1, source_target_pairs={{0,16},{2,18},{4,20},{6,22},{8,24},{10,26},{12,28},{14,30},{16,0},... | collective-permute-start | bytes 786440 | tf_op jit(solution)/shard_map/ppermute | solution.py:135
  82.1 1.3 %project.3 = (f32[256,512]{1,0:T(8,128)S(1)}, bf16[256,512]{1,0:T(8,128)(2,1)S(1)}) custom-call(bf16[256,512]{1,0:T(8,128)(2,1)S(1)} %get-tuple-element.29.refs_0_, bf16[256,512]{1,0:T(8,128)(2,1)S(1)} %collective-permute-done.3.refs_1_, bf16[256,512]{1,0:T(8,128)(2,1)S(1)} %collective-permute-done.4.refs_2_, ...), custom_call_target="tpu_custom_call" | custom-call | tf_op jit(solution)/shard_map/project/pallas_call | solution.py:380
  83.4 0.4 collective-permute-start.27
  83.8 17.0 %collective-permute-done.18 = bf16[256,512]{1,0:T(8,128)(2,1)S(1)} collective-permute-done((bf16[256,512]{1,0:T(8,128)(2,1)S(1)}, bf16[256,512]{1,0:T(8,128)(2,1)S(1)}, u32[]{:S(2)}, u32[]{:S(2)}) %collective-permute-start.18) | collective-permute-done | bytes 262176 | tf_op jit(solution)/shard_map/ppermute | solution.py:135
  100.9 5.0 %collective-permute-done.27 = bf16[256,512]{1,0:T(8,128)(2,1)S(1)} collective-permute-done((bf16[256,512]{1,0:T(8,128)(2,1)S(1)}, bf16[256,512]{1,0:T(8,128)(2,1)S(1)}, u32[]{:S(2)}, u32[]{:S(2)}) %collective-permute-start.27) | collective-permute-done | bytes 262176 | tf_op jit(solution)/shard_map/ppermute | solution.py:135
  105.9 0.1 convert_add_fusion
  106.1 1.1 %pad_maximum_fusion = (f32[256,512]{1,0:T(8,128)}, f32[256,512]{1,0:T(8,128)}) fusion(f32[256,256]{1,0:T(8,128)S(1)} %get-tuple-element.50, f32[256,256]{1,0:T(8,128)S(1)} %get-tuple-element.48, f32[256,256]{1,0:T(8,128)S(1)} %get-tuple-element.49, f32[256,256]{1,0:T(8,128)S(1)} %get-tuple-element.47), kind=kLoop, calls=%fused_computation | loop fusion | flops 262144 | bytes 2097152 | tf_op jit(solution)/shard_map/concatenate | solution.py:425
  (56 shorter events, 0.5 us)
Async XLA Ops:
  0.6 1.0 copy-start.3
  1.6 0.9 copy-start.5
  2.5 11.2 %copy-start = (bf16[128,4096]{1,0:T(8,128)(2,1)S(1)}, bf16[128,4096]{1,0:T(8,128)(2,1)}, u32[]{:S(2)}) copy-start(bf16[128,4096]{1,0:T(8,128)(2,1)} %q_ref.3) | copy-start | bytes 3145732
  3.3 10.5 %collective-permute-start.1 = (bf16[128,1024]{1,0:T(8,128)(2,1)S(1)}, bf16[128,1024]{1,0:T(8,128)(2,1)S(1)}, u32[]{:S(2)}, u32[]{:S(2)}) collective-permute-start(bf16[128,1024]{1,0:T(8,128)(2,1)S(1)} %get-tuple-element.24), channel_id=1, source_target_pairs={{0,1},{2,3},{4,5},{6,7},{8,9},{10,11},{12,13},{14,15},{16,17},{18,... | collective-permute-start | bytes 786440 | tf_op jit(solution)/shard_map/ppermute | solution.py:398
  8.2 1.2 %copy-start.7 = (bf16[128,4096]{1,0:T(8,128)(2,1)S(1)}, bf16[128,4096]{1,0:T(8,128)(2,1)}, u32[]{:S(2)}) copy-start(bf16[128,4096]{1,0:T(8,128)(2,1)} %x_ref.1) | copy-start | bytes 3145732
  9.4 4.4 %copy-start.4 = (bf16[128,1024]{1,0:T(8,128)(2,1)S(1)}, bf16[128,1024]{1,0:T(8,128)(2,1)}, u32[]{:S(2)}) copy-start(bf16[128,1024]{1,0:T(8,128)(2,1)} %k_ref.5) | copy-start | bytes 786436
  9.4 4.4 %copy-start.6 = (bf16[128,1024]{1,0:T(8,128)(2,1)S(1)}, bf16[128,1024]{1,0:T(8,128)(2,1)}, u32[]{:S(2)}) copy-start(bf16[128,1024]{1,0:T(8,128)(2,1)} %v_ref.5) | copy-start | bytes 786436
  10.3 0.8 copy-start.12
  11.1 17.8 %collective-permute-start.2 = (bf16[128,2048]{1,0:T(8,128)(2,1)}, bf16[128,2048]{1,0:T(8,128)(2,1)}, u32[]{:S(2)}, u32[]{:S(2)}) collective-permute-start(bf16[128,2048]{1,0:T(8,128)(2,1)} %get-tuple-element.28), channel_id=1, source_target_pairs={{0,2},{2,0},{4,6},{6,4},{8,10},{10,8},{12,14},{14,12},{16,18},{18,... | collective-permute-start | bytes 1572872 | tf_op jit(solution)/shard_map/ppermute | solution.py:135
  11.1 13.3 %collective-permute-start = (bf16[128,1024]{1,0:T(8,128)(2,1)}, bf16[128,1024]{1,0:T(8,128)(2,1)S(1)}, u32[]{:S(2)}, u32[]{:S(2)}) collective-permute-start(bf16[128,1024]{1,0:T(8,128)(2,1)} %get-tuple-element.23), channel_id=1, source_target_pairs={{0,1},{2,3},{4,5},{6,7},{8,9},{10,11},{12,13},{14,15},{16,17},{18,... | collective-permute-start | bytes 786440 | tf_op jit(solution)/shard_map/ppermute | solution.py:398
  13.8 1.2 %copy-start.1 = (bf16[128,4096]{1,0:T(8,128)(2,1)S(1)}, bf16[128,4096]{1,0:T(8,128)(2,1)}, u32[]{:S(2)}) copy-start(bf16[128,4096]{1,0:T(8,128)(2,1)} %g_ref.3) | copy-start | bytes 3145732
  15.0 0.9 copy-start.8
  15.9 0.9 copy-start.10
  16.8 7.6 %copy-start.2 = (bf16[128,4096]{1,0:T(8,128)(2,1)S(1)}, bf16[128,4096]{1,0:T(8,128)(2,1)}, u32[]{:S(2)}) copy-start(bf16[128,4096]{1,0:T(8,128)(2,1)} %g_ref.3) | copy-start | bytes 3145732
  16.8 7.6 %copy-start.9 = (f32[256,128]{1,0:T(8,128)S(1)}, f32[256,128]{1,0:T(8,128)}, u32[]{:S(2)}) copy-start(f32[256,128]{1,0:T(8,128)} %constant.15.clone.sin_ref) | copy-start | bytes 393220
  16.8 7.7 %copy-start.11 = (f32[256,128]{1,0:T(8,128)S(1)}, f32[256,128]{1,0:T(8,128)}, u32[]{:S(2)}) copy-start(f32[256,128]{1,0:T(8,128)} %constant.14.clone.cos_ref) | copy-start | bytes 393220
  20.4 0.7 copy-start.14
  21.1 12.1 %collective-permute-start.10 = (bf16[256,512]{1,0:T(8,128)(2,1)}, bf16[256,512]{1,0:T(8,128)(2,1)}, u32[]{:S(2)}, u32[]{:S(2)}) collective-permute-start(bf16[256,512]{1,0:T(8,128)(2,1)} %get-tuple-element.34), channel_id=1, source_target_pairs={{0,1},{1,0},{2,3},{3,2},{4,5},{5,4},{6,7},{7,6},{8,9},{9,8},{10,11... | collective-permute-start | bytes 786440 | tf_op jit(solution)/shard_map/ppermute | solution.py:139
  24.5 4.4 %copy-start.13 = (bf16[128,2048]{1,0:T(8,128)(2,1)S(1)}, bf16[128,2048]{1,0:T(8,128)(2,1)}, u32[]{:S(2)}) copy-start(bf16[128,2048]{1,0:T(8,128)(2,1)} %copy-done.12) | copy-start | bytes 1572868
  28.0 8.3 %collective-permute-start.19 = (bf16[256,512]{1,0:T(8,128)(2,1)S(1)}, bf16[256,512]{1,0:T(8,128)(2,1)S(1)}, u32[]{:S(2)}, u32[]{:S(2)}) collective-permute-start(bf16[256,512]{1,0:T(8,128)(2,1)S(1)} %get-tuple-element.39), channel_id=1, source_target_pairs={{0,1},{1,0},{2,3},{3,2},{4,5},{5,4},{6,7},{7,6},{8,9},{9,8},{10,11... | collective-permute-start | bytes 786440 | tf_op jit(solution)/shard_map/ppermute | solution.py:139
  28.9 4.3 %copy-start.15 = (f32[128,512]{1,0:T(8,128)S(1)}, f32[128,512]{1,0:T(8,128)}, u32[]{:S(2)}) copy-start(f32[128,512]{1,0:T(8,128)} %copy-done.14) | copy-start | bytes 786436
  30.1 9.3 %collective-permute-start.4 = (bf16[256,512]{1,0:T(8,128)(2,1)S(1)}, bf16[256,512]{1,0:T(8,128)(2,1)S(1)}, u32[]{:S(2)}, u32[]{:S(2)}) collective-permute-start(bf16[256,512]{1,0:T(8,128)(2,1)S(1)} %get-tuple-element.30), channel_id=1, source_target_pairs={{0,4},{2,6},{4,0},{6,2},{8,12},{10,14},{12,8},{14,10},{16,20},{18,... | collective-permute-start | bytes 786440 | tf_op jit(solution)/shard_map/ppermute | solution.py:135
  31.6 11.0 %collective-permute-start.6 = (bf16[256,512]{1,0:T(8,128)(2,1)S(1)}, bf16[256,512]{1,0:T(8,128)(2,1)S(1)}, u32[]{:S(2)}, u32[]{:S(2)}) collective-permute-start(bf16[256,512]{1,0:T(8,128)(2,1)S(1)} %get-tuple-element.31), channel_id=1, source_target_pairs={{0,8},{2,10},{4,12},{6,14},{8,0},{10,2},{12,4},{14,6},{16,24},{18,... | collective-permute-start | bytes 786440 | tf_op jit(solution)/shard_map/ppermute | solution.py:135
  34.3 23.2 %collective-permute-start.16 = (bf16[256,512]{1,0:T(8,128)(2,1)S(1)}, bf16[256,512]{1,0:T(8,128)(2,1)S(1)}, u32[]{:S(2)}, u32[]{:S(2)}) collective-permute-start(bf16[256,512]{1,0:T(8,128)(2,1)S(1)} %pad_maximum_fusion.2.refs_8_), channel_id=1, source_target_pairs={{0,12},{2,14},{4,8},{6,10},{8,4},{10,6},{12,0},{14,2},{16,28},{18,... | collective-permute-start | bytes 786440 | tf_op jit(solution)/shard_map/ppermute | solution.py:135
  34.7 23.2 %collective-permute-start.14 = (bf16[256,512]{1,0:T(8,128)(2,1)S(1)}, bf16[256,512]{1,0:T(8,128)(2,1)S(1)}, u32[]{:S(2)}, u32[]{:S(2)}) collective-permute-start(bf16[256,512]{1,0:T(8,128)(2,1)S(1)} %pad_maximum_fusion.2.refs_8_), channel_id=1, source_target_pairs={{0,8},{2,10},{4,12},{6,14},{8,0},{10,2},{12,4},{14,6},{16,24},{18,... | collective-permute-start | bytes 786440 | tf_op jit(solution)/shard_map/ppermute | solution.py:135
  36.3 22.1 %collective-permute-start.12 = (bf16[256,512]{1,0:T(8,128)(2,1)S(1)}, bf16[256,512]{1,0:T(8,128)(2,1)S(1)}, u32[]{:S(2)}, u32[]{:S(2)}) collective-permute-start(bf16[256,512]{1,0:T(8,128)(2,1)S(1)} %pad_maximum_fusion.2.refs_8_), channel_id=1, source_target_pairs={{0,4},{2,6},{4,0},{6,2},{8,12},{10,14},{12,8},{14,10},{16,20},{18,... | collective-permute-start | bytes 786440 | tf_op jit(solution)/shard_map/ppermute | solution.py:135
  39.3 15.6 %collective-permute-start.8 = (bf16[256,512]{1,0:T(8,128)(2,1)S(1)}, bf16[256,512]{1,0:T(8,128)(2,1)S(1)}, u32[]{:S(2)}, u32[]{:S(2)}) collective-permute-start(bf16[256,512]{1,0:T(8,128)(2,1)S(1)} %get-tuple-element.32), channel_id=1, source_target_pairs={{0,12},{2,14},{4,8},{6,10},{8,4},{10,6},{12,0},{14,2},{16,28},{18,... | collective-permute-start | bytes 786440 | tf_op jit(solution)/shard_map/ppermute | solution.py:135
  42.7 12.3 %collective-permute-start.3 = (bf16[256,512]{1,0:T(8,128)(2,1)S(1)}, bf16[256,512]{1,0:T(8,128)(2,1)S(1)}, u32[]{:S(2)}, u32[]{:S(2)}) collective-permute-start(bf16[256,512]{1,0:T(8,128)(2,1)S(1)} %get-tuple-element.29.refs_0_), channel_id=1, source_target_pairs={{0,1},{1,0},{2,3},{3,2},{4,5},{5,4},{6,7},{7,6},{8,9},{9,8},{10,11... | collective-permute-start | bytes 786440 | tf_op jit(solution)/shard_map/ppermute | solution.py:139
  55.0 4.5 %collective-permute-start.11 = (bf16[256,512]{1,0:T(8,128)(2,1)S(1)}, bf16[256,512]{1,0:T(8,128)(2,1)S(1)}, u32[]{:S(2)}, u32[]{:S(2)}) collective-permute-start(bf16[256,512]{1,0:T(8,128)(2,1)S(1)} %pad_maximum_fusion.2.refs_8_), channel_id=1, source_target_pairs={{0,2},{2,0},{4,6},{6,4},{8,10},{10,8},{12,14},{14,12},{16,18},{18,... | collective-permute-start | bytes 786440 | tf_op jit(solution)/shard_map/ppermute | solution.py:135
  55.0 10.0 %collective-permute-start.25 = (bf16[256,512]{1,0:T(8,128)(2,1)S(1)}, bf16[256,512]{1,0:T(8,128)(2,1)S(1)}, u32[]{:S(2)}, u32[]{:S(2)}) collective-permute-start(bf16[256,512]{1,0:T(8,128)(2,1)S(1)} %pad_maximum_fusion.3.refs_8_), channel_id=1, source_target_pairs={{0,12},{2,14},{4,8},{6,10},{8,4},{10,6},{12,0},{14,2},{16,28},{18,... | collective-permute-start | bytes 786440 | tf_op jit(solution)/shard_map/ppermute | solution.py:135
  57.5 12.8 %collective-permute-start.23 = (bf16[256,512]{1,0:T(8,128)(2,1)S(1)}, bf16[256,512]{1,0:T(8,128)(2,1)S(1)}, u32[]{:S(2)}, u32[]{:S(2)}) collective-permute-start(bf16[256,512]{1,0:T(8,128)(2,1)S(1)} %pad_maximum_fusion.3.refs_8_), channel_id=1, source_target_pairs={{0,8},{2,10},{4,12},{6,14},{8,0},{10,2},{12,4},{14,6},{16,24},{18,... | collective-permute-start | bytes 786440 | tf_op jit(solution)/shard_map/ppermute | solution.py:135
  57.9 12.4 %collective-permute-start.21 = (bf16[256,512]{1,0:T(8,128)(2,1)S(1)}, bf16[256,512]{1,0:T(8,128)(2,1)S(1)}, u32[]{:S(2)}, u32[]{:S(2)}) collective-permute-start(bf16[256,512]{1,0:T(8,128)(2,1)S(1)} %pad_maximum_fusion.3.refs_8_), channel_id=1, source_target_pairs={{0,4},{2,6},{4,0},{6,2},{8,12},{10,14},{12,8},{14,10},{16,20},{18,... | collective-permute-start | bytes 786440 | tf_op jit(solution)/shard_map/ppermute | solution.py:135
  58.5 12.3 %collective-permute-start.5 = (bf16[256,512]{1,0:T(8,128)(2,1)S(1)}, bf16[256,512]{1,0:T(8,128)(2,1)S(1)}, u32[]{:S(2)}, u32[]{:S(2)}) collective-permute-start(bf16[256,512]{1,0:T(8,128)(2,1)S(1)} %collective-permute-done.4.refs_2_), channel_id=1, source_target_pairs={{0,1},{1,0},{2,3},{3,2},{4,5},{5,4},{6,7},{7,6},{8,9},{9,8},{10,11... | collective-permute-start | bytes 786440 | tf_op jit(solution)/shard_map/ppermute | solution.py:139
  59.5 13.9 %collective-permute-start.7 = (bf16[256,512]{1,0:T(8,128)(2,1)S(1)}, bf16[256,512]{1,0:T(8,128)(2,1)S(1)}, u32[]{:S(2)}, u32[]{:S(2)}) collective-permute-start(bf16[256,512]{1,0:T(8,128)(2,1)S(1)} %collective-permute-done.6.refs_4_), channel_id=1, source_target_pairs={{0,1},{1,0},{2,3},{3,2},{4,5},{5,4},{6,7},{7,6},{8,9},{9,8},{10,11... | collective-permute-start | bytes 786440 | tf_op jit(solution)/shard_map/ppermute | solution.py:139
  65.0 12.6 %collective-permute-start.9 = (bf16[256,512]{1,0:T(8,128)(2,1)S(1)}, bf16[256,512]{1,0:T(8,128)(2,1)S(1)}, u32[]{:S(2)}, u32[]{:S(2)}) collective-permute-start(bf16[256,512]{1,0:T(8,128)(2,1)S(1)} %collective-permute-done.8.refs_6_), channel_id=1, source_target_pairs={{0,1},{1,0},{2,3},{3,2},{4,5},{5,4},{6,7},{7,6},{8,9},{9,8},{10,11... | collective-permute-start | bytes 786440 | tf_op jit(solution)/shard_map/ppermute | solution.py:139
  70.3 7.3 %collective-permute-start.17 = (bf16[256,512]{1,0:T(8,128)(2,1)S(1)}, bf16[256,512]{1,0:T(8,128)(2,1)S(1)}, u32[]{:S(2)}, u32[]{:S(2)}) collective-permute-start(bf16[256,512]{1,0:T(8,128)(2,1)S(1)} %collective-permute-done.16.refs_14_), channel_id=1, source_target_pairs={{0,2},{2,0},{4,6},{6,4},{8,10},{10,8},{12,14},{14,12},{16,18},{18,... | collective-permute-start | bytes 786440 | tf_op jit(solution)/shard_map/ppermute | solution.py:135
  70.3 7.8 %collective-permute-start.15 = (bf16[256,512]{1,0:T(8,128)(2,1)S(1)}, bf16[256,512]{1,0:T(8,128)(2,1)S(1)}, u32[]{:S(2)}, u32[]{:S(2)}) collective-permute-start(bf16[256,512]{1,0:T(8,128)(2,1)S(1)} %collective-permute-done.14.refs_12_), channel_id=1, source_target_pairs={{0,2},{2,0},{4,6},{6,4},{8,10},{10,8},{12,14},{14,12},{16,18},{18,... | collective-permute-start | bytes 786440 | tf_op jit(solution)/shard_map/ppermute | solution.py:135
  70.8 7.4 %collective-permute-start.13 = (bf16[256,512]{1,0:T(8,128)(2,1)S(1)}, bf16[256,512]{1,0:T(8,128)(2,1)S(1)}, u32[]{:S(2)}, u32[]{:S(2)}) collective-permute-start(bf16[256,512]{1,0:T(8,128)(2,1)S(1)} %collective-permute-done.12.refs_10_), channel_id=1, source_target_pairs={{0,2},{2,0},{4,6},{6,4},{8,10},{10,8},{12,14},{14,12},{16,18},{18,... | collective-permute-start | bytes 786440 | tf_op jit(solution)/shard_map/ppermute | solution.py:135
  73.3 8.8 %collective-permute-start.20 = (bf16[256,512]{1,0:T(8,128)(2,1)S(1)}, bf16[256,512]{1,0:T(8,128)(2,1)S(1)}, u32[]{:S(2)}, u32[]{:S(2)}) collective-permute-start(bf16[256,512]{1,0:T(8,128)(2,1)S(1)} %pad_maximum_fusion.3.refs_8_), channel_id=1, source_target_pairs={{0,2},{2,0},{4,6},{6,4},{8,10},{10,8},{12,14},{14,12},{16,18},{18,... | collective-permute-start | bytes 786440 | tf_op jit(solution)/shard_map/ppermute | solution.py:135
  77.6 4.5 %collective-permute-start.26 = (bf16[256,512]{1,0:T(8,128)(2,1)S(1)}, bf16[256,512]{1,0:T(8,128)(2,1)S(1)}, u32[]{:S(2)}, u32[]{:S(2)}) collective-permute-start(bf16[256,512]{1,0:T(8,128)(2,1)S(1)} %collective-permute-done.25.refs_14_), channel_id=1, source_target_pairs={{0,2},{2,0},{4,6},{6,4},{8,10},{10,8},{12,14},{14,12},{16,18},{18,... | collective-permute-start | bytes 786440 | tf_op jit(solution)/shard_map/ppermute | solution.py:135
  77.6 4.5 %collective-permute-start.24 = (bf16[256,512]{1,0:T(8,128)(2,1)S(1)}, bf16[256,512]{1,0:T(8,128)(2,1)S(1)}, u32[]{:S(2)}, u32[]{:S(2)}) collective-permute-start(bf16[256,512]{1,0:T(8,128)(2,1)S(1)} %collective-permute-done.23.refs_12_), channel_id=1, source_target_pairs={{0,2},{2,0},{4,6},{6,4},{8,10},{10,8},{12,14},{14,12},{16,18},{18,... | collective-permute-start | bytes 786440 | tf_op jit(solution)/shard_map/ppermute | solution.py:135
  78.1 4.0 %collective-permute-start.22 = (bf16[256,512]{1,0:T(8,128)(2,1)S(1)}, bf16[256,512]{1,0:T(8,128)(2,1)S(1)}, u32[]{:S(2)}, u32[]{:S(2)}) collective-permute-start(bf16[256,512]{1,0:T(8,128)(2,1)S(1)} %collective-permute-done.21.refs_10_), channel_id=1, source_target_pairs={{0,2},{2,0},{4,6},{6,4},{8,10},{10,8},{12,14},{14,12},{16,18},{18,... | collective-permute-start | bytes 786440 | tf_op jit(solution)/shard_map/ppermute | solution.py:135
  79.5 21.3 %collective-permute-start.18 = (bf16[256,512]{1,0:T(8,128)(2,1)S(1)}, bf16[256,512]{1,0:T(8,128)(2,1)S(1)}, u32[]{:S(2)}, u32[]{:S(2)}) collective-permute-start(bf16[256,512]{1,0:T(8,128)(2,1)S(1)} %get-tuple-element.37), channel_id=1, source_target_pairs={{0,16},{2,18},{4,20},{6,22},{8,24},{10,26},{12,28},{14,30},{16,0},... | collective-permute-start | bytes 786440 | tf_op jit(solution)/shard_map/ppermute | solution.py:135
  83.4 22.5 %collective-permute-start.27 = (bf16[256,512]{1,0:T(8,128)(2,1)S(1)}, bf16[256,512]{1,0:T(8,128)(2,1)S(1)}, u32[]{:S(2)}, u32[]{:S(2)}) collective-permute-start(bf16[256,512]{1,0:T(8,128)(2,1)S(1)} %get-tuple-element.42), channel_id=1, source_target_pairs={{0,16},{2,18},{4,20},{6,22},{8,24},{10,26},{12,28},{14,30},{16,0},... | collective-permute-start | bytes 786440 | tf_op jit(solution)/shard_map/ppermute | solution.py:135

commit v2 on v0

--- a/solution.py
+++ b/solution.py
@@ -2,10 +2,18 @@
 
 import jax
 import jax.numpy as jnp
+import numpy as np
 from jax import lax
+from jax.experimental import pallas as pl
+from jax.experimental.pallas import tpu as pltpu
 from jax.sharding import PartitionSpec as P
 
 HD = 128
+NC = 2
+BF = jnp.bfloat16
+F32 = jnp.float32
+VMEM_LIMIT = 20 * 1024 * 1024
+VMEM_FULL = 60 * 1024 * 1024
 
 
 def unrotate(grad, position):
@@ -21,7 +29,7 @@
     )
 
 
-def local(queries, keys, values, out_grad, normed):
+def general_local(queries, keys, values, out_grad, normed):
     head_q, head_k, head_v, head_g = (
         lax.all_to_all(queries, "seq", split_axis=1, concat_axis=0, tiled=True),
         lax.all_to_all(keys, "seq", split_axis=1, concat_axis=0, tiled=True),
@@ -121,18 +129,459 @@
     return (query_grad, key_weight_grad, value_weight_grad)
 
 
+CORE, XBIT, ZLOW, ZHIGH = 1, 2, 4, 8
+
+
+def flip(array, mask):
+    return lax.ppermute(array, "dp", [(i, i ^ mask) for i in range(16)])
+
+
+def swap_seq(array):
+    return lax.ppermute(array, "seq", [(0, 1), (1, 0)])
+
+
+def params(limit=VMEM_LIMIT):
+    return pltpu.CompilerParams(vmem_limit_bytes=limit)
+
+
+def vmem():
+    return pl.BlockSpec(memory_space=pltpu.VMEM)
+
+
+def smem():
+    return pl.BlockSpec(memory_space=pltpu.SMEM)
+
+
+def rotary_tables(length):
+    half = HD // 2
+    freqs = np.exp(-math.log(500000.0) * (2.0 * np.arange(half, dtype=np.float64) / HD))
+    angle = np.arange(length, dtype=np.float64)[:, None] * freqs[None, :]
+    cosine = np.concatenate([np.cos(angle), np.cos(angle)], axis=1)
+    sine = np.concatenate([np.sin(angle), -np.sin(angle)], axis=1)
+    return cosine.astype(np.float32), sine.astype(np.float32)
+
+
+def hbm():
+    return pl.BlockSpec(memory_space=pltpu.HBM)
+
+
+def in_hbm(array):
+    return pltpu.with_memory_space_constraint(array, pltpu.HBM)
+
+
+def run_copies(copies):
+    for copy in copies:
+        copy.start()
+    for copy in copies:
+        copy.wait()
+
+
+def prepare(keys, values, normed, me):
+    rows, kv_width = keys.shape
+    width = normed.shape[1]
+    share = width // 16
+    wide = kv_width // (2 * NC)
+
+    def body(me_ref, k_hbm, v_hbm, x_hbm, k_ref, v_ref, *rest):
+        kv, parts, (x_ref, sem) = rest[:NC], rest[NC : NC + 4], rest[NC + 4 :]
+        mine = me_ref[0]
+        run_copies(
+            [
+                pltpu.make_async_copy(k_hbm, k_ref, sem.at[0]),
+                pltpu.make_async_copy(v_hbm, v_ref, sem.at[1]),
+                pltpu.make_async_copy(x_hbm, x_ref, sem.at[2]),
+            ]
+        )
+        for chunk, out in enumerate(kv):
+            for number, ref in enumerate((k_ref, v_ref)):
+                for half in range(2):
+                    low = (half * NC + chunk) * wide
+                    at = (number * 2 + half) * wide
+                    out[:, at : at + wide] = ref[:, low : low + wide]
+
+        for place, part in enumerate(parts):
+            for number, mask in enumerate((ZHIGH, ZHIGH | CORE, 0, CORE)):
+                low = pl.multiple_of((mine ^ (mask | (place * 2))) * share, share)
+                part[number] = x_ref[:, pl.ds(low, share)]
+
+    return pl.pallas_call(
+        body,
+        out_shape=[pltpu.VMEM((rows, kv_width), BF)] * 2
+        + [pltpu.VMEM((rows, 4 * wide), BF)] * NC
+        + [pltpu.VMEM((4, rows, share), BF)] * 4,
+        in_specs=[smem()] + [hbm()] * 3,
+        out_specs=[vmem()] * (6 + NC),
+        scratch_shapes=[pltpu.VMEM((rows, width), BF), pltpu.SemaphoreType.DMA((3,))],
+        compiler_params=params(),
+        name="prepare",
+    )(me, in_hbm(keys), in_hbm(values), in_hbm(normed))
+
+
+def stage(arrays):
+    count = len(arrays)
+
+    def body(*refs):
+        run_copies(
+            [
+                pltpu.make_async_copy(refs[n], refs[count + n], refs[-1].at[n])
+                for n in range(count)
+            ]
+        )
+
+    return pl.pallas_call(
+        body,
+        out_shape=[pltpu.VMEM(one.shape, one.dtype) for one in arrays],
+        in_specs=[hbm()] * count,
+        out_specs=[vmem()] * count,
+        scratch_shapes=[pltpu.SemaphoreType.DMA((count,))],
+        compiler_params=params(),
+        name="stage",
+    )(*[in_hbm(one) for one in arrays])
+
+
+def pack_normed(parts, numbers, after):
+    rows, share = parts[0].shape[1:]
+    shapes = [(4,) + (len(group),) * (len(group) > 1) + (rows, share) for group in numbers]
+
+    def body(*refs):
+        for group, out in zip(numbers, refs[-len(numbers) :]):
+            for place in range(4):
+                if len(group) > 1:
+                    for at, number in enumerate(group):
+                        out[place, at] = refs[place][number]
+                else:
+                    out[place] = refs[place][group[0]]
+
+    return pl.pallas_call(
+        body,
+        out_shape=[pltpu.VMEM(shape, BF) for shape in shapes],
+        in_specs=[vmem()] * 4 + [hbm()] * len(after),
+        out_specs=[vmem()] * len(shapes),
+        compiler_params=params(),
+        name="pack_normed",
+    )(*parts, *after)
+
+
+def combine(seq_at, keep_a, keep_b, recv, after):
+    rows, wide = keep_a.shape
+
+    def body(at_ref, a_ref, b_ref, recv_ref, *rest):
+        out = rest[-1]
+        early = (a_ref[...] + recv_ref[:rows].astype(F32)).astype(BF)
+
+        @pl.when(at_ref[0] == 0)
+        def _():
+            out[:rows] = early
+            out[rows:] = recv_ref[rows:]
+
+        @pl.when(at_ref[0] == 1)
+        def _():
+            out[:rows] = b_ref[...]
+            out[rows:] = early
+
+    return pl.pallas_call(
+        body,
+        out_shape=jax.ShapeDtypeStruct((2 * rows, wide), BF),
+        in_specs=[smem(), vmem(), vmem(), vmem()] + [hbm()] * len(after),
+        out_specs=vmem(),
+        compiler_params=params(),
+        name="combine",
+    )(seq_at, keep_a, keep_b, recv, *after)
+
+
+def attention(
+    chunk, seq_at, queries, out_grad, keys, values, kv_recv, cosine, sine, grad_so_far, after
+):
+    rows, width = queries.shape
+    wide = width // (2 * NC)
+    kv_wide = keys.shape[1] // (2 * NC)
+    kv_heads = kv_wide // HD
+    groups = wide // kv_wide
+    span = groups * rows
+    scale = 1.0 / math.sqrt(HD)
+
+    def rotate(grad, cos, sin):
+        return grad * cos + pltpu.roll(grad, HD // 2, 1) * sin
+
+    def nt(a, b):
+        return lax.dot_general(a, b, (((1,), (1,)), ((), ())), preferred_element_type=F32)
+
+    def tn(a, b):
+        return lax.dot_general(a, b, (((0,), (0,)), ((), ())), preferred_element_type=F32)
+
+    def body(at_ref, q_ref, g_ref, k_ref, v_ref, kv_ref, cos_ref, sin_ref, *rest):
+        qg_hbm, keep_a, keep_b, send, qg_buf, out_sem = rest[-6:]
+        late = at_ref[0]
+
+        def columns(j, size):
+            return pl.ds(pl.multiple_of(((late ^ j) * NC + chunk) * size, size), size)
+
+        outs = [
+            pltpu.make_async_copy(qg_buf.at[j], qg_hbm.at[:, columns(j, wide)], out_sem.at[j])
+            for j in range(2)
+        ]
+        for j in (1, 0):
+            one_side(
+                j, late,
+                q_ref.at[:, columns(j, wide)], g_ref.at[:, columns(j, wide)],
+                k_ref.at[:, columns(j, kv_wide)], v_ref.at[:, columns(j, kv_wide)],
+                kv_ref, cos_ref, sin_ref, qg_buf.at[j], keep_a, keep_b, send,
+            )
+            outs[j].start()
+        for copy in outs:
+            copy.wait()
+
+    def one_side(
+        other, late, q_ref, g_ref, k_ref, v_ref, kv_ref, cos_ref, sin_ref, qg_ref, keep_a, keep_b, send
+    ):
+        def earlier(number, head):
+            low = (number * 2 + (late ^ other)) * kv_wide + head * HD
+            return kv_ref[:, pl.ds(pl.multiple_of(low, HD), HD)]
+
+        def stack(ref, head):
+            return jnp.concatenate(
+                [
+                    ref[:, (head * groups + m) * HD : (head * groups + m + 1) * HD]
+                    for m in range(groups)
+                ],
+                axis=0,
+            )
+
+        def one_head(head, is_late):
+            cols = slice(head * HD, (head + 1) * HD)
+            qs = stack(q_ref, head)
+            gs = stack(g_ref, head)
+            ks = k_ref[:, cols]
+            vs = v_ref[:, cols]
+            if is_late:
+                ks = jnp.concatenate([earlier(0, head), ks], axis=0)
+                vs = jnp.concatenate([earlier(1, head), vs], axis=0)
+            count = ks.shape[0]
+            scores = nt(ks, qs)
+            key_pos = lax.broadcasted_iota(jnp.int32, (rows, span), 0)
+            query_pos = lax.broadcasted_iota(jnp.int32, (rows, span), 1) % rows
+            diagonal = jnp.where(key_pos <= query_pos, scores[count - rows :], -1e30)
+            scores = jnp.concatenate([scores[:rows], diagonal], axis=0) if is_late else diagonal
+            top = jnp.max(scores, axis=0, keepdims=True)
+            expo = jnp.exp2((scores - top) * (scale / math.log(2.0)))
+            probs = expo * (1.0 / jnp.sum(expo, axis=0, keepdims=True))
+            value_grad = jnp.dot(probs.astype(BF), gs, preferred_element_type=F32)
+            prob_grad = nt(vs, gs)
+            delta = jnp.sum(probs * prob_grad, axis=0, keepdims=True)
+            score_grad = (probs * (prob_grad - delta) * scale).astype(BF)
+            key_grad = jnp.dot(score_grad, qs, preferred_element_type=F32)
+            query_grad = tn(score_grad, ks).astype(BF)
+            for m in range(groups):
+                low = (head * groups + m) * HD
+                qg_ref[:, low : low + HD] = query_grad[m * rows : (m + 1) * rows]
+            first = (rotate(key_grad[:rows], cos_ref[:rows], sin_ref[:rows]), value_grad[:rows])
+            second = None
+            if is_late:
+                second = (
+                    rotate(key_grad[rows:], cos_ref[rows:], sin_ref[rows:]),
+                    value_grad[rows:],
+                )
+            return first, second
+
+        def all_heads(is_late):
+            parts = [one_head(head, is_late) for head in range(kv_heads)]
+
+            def write(first_ref, second_ref, second_at):
+                for head, (first, second) in enumerate(parts):
+                    for number in range(2):
+                        at = slice(number * kv_wide + head * HD, number * kv_wide + (head + 1) * HD)
+                        first_ref[:rows, at] = first[number].astype(first_ref.dtype)
+                        later = jnp.zeros((rows, HD), BF) if second is None else second[number].astype(BF)
+                        second_ref[second_at : second_at + rows, at] = later
+
+            if other == 0:
+                write(keep_a, keep_b, 0)
+            else:
+                write(send, send, rows)
+
+        @pl.when(late == 1)
+        def _():
+            all_heads(True)
+
+        @pl.when(late == 0)
+        def _():
+            all_heads(False)
+
+    operands = [seq_at, queries, out_grad, keys, values, kv_recv, cosine, sine]
+    specs = [smem()] + [vmem()] * 7
+    aliases = {}
+    if grad_so_far is not None:
+        specs.append(hbm())
+        operands.append(grad_so_far)
+        aliases = {8: 0}
+    specs += [hbm()] * len(after)
+    operands += after
+    return pl.pallas_call(
+        body,
+        out_shape=[
+            jax.ShapeDtypeStruct((rows, width), BF),
+            pltpu.VMEM((rows, 2 * kv_wide), F32),
+            pltpu.VMEM((rows, 2 * kv_wide), BF),
+            pltpu.VMEM((2 * rows, 2 * kv_wide), BF),
+        ],
+        in_specs=specs,
+        out_specs=[hbm(), vmem(), vmem(), vmem()],
+        scratch_shapes=[
+            pltpu.VMEM((2, rows, wide), BF),
+            pltpu.SemaphoreType.DMA((2,)),
+        ],
+        input_output_aliases=aliases,
+        compiler_params=params(),
+        name="attention",
+    )(*operands)
+
+
+def tn(a, b):
+    return lax.dot_general(a, b, (((0,), (0,)), ((), ())), preferred_element_type=F32)
+
+
+def project_away(normed_own, normed_other, grads, after):
+    share = normed_own.shape[3]
+    wide = grads[0].shape[1]
+
+    def body(xa_ref, xb_ref, *refs):
+        ys, outs = refs[:4], refs[-2:]
+        right = jnp.concatenate([ref[...] for ref in ys], axis=0)
+        for core, out in enumerate(outs):
+            left = [x_ref[place, core] for place in range(4) for x_ref in (xa_ref, xb_ref)]
+            out[...] = tn(jnp.concatenate(left, axis=0), right)
+
+    return pl.pallas_call(
+        body,
+        out_shape=[pltpu.VMEM((share, wide), F32)] * 2,
+        in_specs=[vmem()] * 6 + [hbm()] * len(after),
+        out_specs=[vmem()] * 2,
+        compiler_params=params(),
+        name="project_away",
+    )(normed_own, normed_other, *grads, *after)
+
+
+def add_round(own, recv):
+    def body(a_ref, b_ref, out):
+        out[...] = (a_ref[...] + b_ref[...]).astype(BF)
+
+    return pl.pallas_call(
+        body,
+        out_shape=pltpu.VMEM(own.shape, BF),
+        in_specs=[vmem()] * 2,
+        out_specs=vmem(),
+        compiler_params=params(),
+        name="add_round",
+    )(own, recv)
+
+
+def project_home(normed, grads, after):
+    rows, share = normed[0].shape[1:]
+    wide = grads[0][0].shape[1]
+    chunks = len(grads)
+
+    def body(*refs):
+        xs, ys, out = refs[:4], refs[4 : 4 + 8 * chunks], refs[-1]
+        left = [x_ref[place] for place in range(4) for x_ref in xs]
+        left = jnp.concatenate(left, axis=0)
+        for chunk in range(chunks):
+            right = [
+                ys[chunk * 8 + place * 2 + core][seq * rows : (seq + 1) * rows, :]
+                for place in range(4)
+                for seq in range(2)
+                for core in range(2)
+            ]
+            out[:, chunk * wide : (chunk + 1) * wide] = tn(left, jnp.concatenate(right, axis=0))
+
+    return pl.pallas_call(
+        body,
+        out_shape=pltpu.VMEM((share, chunks * wide), F32),
+        in_specs=[vmem()] * (4 + 8 * chunks) + [hbm()] * len(after),
+        out_specs=vmem(),
+        compiler_params=params(),
+        name="project_home",
+    )(*normed, *[part for parts in grads for part in parts], *after)
+
+
+def finish(keep, recv_half):
+    rows, width = keep.shape
+    wide = width // NC
+    part = wide // 2
+
+    def body(keep_ref, *refs):
+        halves, outs = refs[:NC], refs[NC:]
+        for chunk, half_ref in enumerate(halves):
+            for number, out in enumerate(outs):
+                low = number * part
+                at = slice(chunk * wide + low, chunk * wide + low + part)
+                out[:, chunk * part : (chunk + 1) * part] = (
+                    keep_ref[:, at] + half_ref[:, low : low + part].astype(F32)
+                )
+
+    return pl.pallas_call(
+        body,
+        out_shape=[jax.ShapeDtypeStruct((rows, width // 2), F32)] * 2,
+        in_specs=[vmem()] * (1 + NC),
+        out_specs=[vmem()] * 2,
+        compiler_params=params(),
+        name="finish",
+    )(keep, *recv_half)
+
+
+def cube_local(queries, keys, values, out_grad, normed):
+    seq_at = jnp.reshape(lax.axis_index("seq"), (1,)).astype(jnp.int32)
+    me = jnp.reshape(lax.axis_index("dp"), (1,)).astype(jnp.int32)
+    rows = queries.shape[0]
+    cosine, sine = (jnp.asarray(table) for table in rotary_tables(2 * rows))
+
+    keys, values, *rest = prepare(keys, values, normed, me)
+    kv, parts = rest[:NC], rest[NC:]
+    kv_recv = [lax.ppermute(part, "seq", [(0, 1)]) for part in kv]
+    masks = (0, XBIT, ZLOW, XBIT | ZLOW)
+    parts = [flip(part, mask) if mask else part for part, mask in zip(parts, masks)]
+    q_in, g_in, cosine, sine = stage([queries, out_grad, cosine, sine])
+
+    query_grad = None
+    made = []
+    for chunk in range(NC):
+        query_grad, *rest = attention(
+            chunk, seq_at, q_in, g_in, keys, values, kv_recv[chunk], cosine, sine, query_grad,
+            parts[1:] if chunk else [],
+        )
+        made.append(rest)
+    grads, mines = [], []
+    after = [made[-1][0]]
+    for keep_a, keep_b, send in made:
+        mine = combine(seq_at, keep_a, keep_b, swap_seq(send), after)
+        mines.append(mine)
+        below = flip(mine, ZLOW)
+        grads.append([mine, flip(mine, XBIT), below, flip(below, XBIT)])
+        after = [grads[-1][1]]
+    (away,) = pack_normed(parts, [(0, 1)], [made[-1][0]])
+    away_other = swap_seq(away)
+    same, cross = pack_normed(parts, [(2,), (3,)], [away_other])
+    same_other, cross_other = swap_seq(same), swap_seq(cross)
+    home = [same, flip(cross, CORE), same_other, flip(cross_other, CORE)]
+    recv_half = []
+    after = grads[1][1:3]
+    for part in grads:
+        own, send = project_away(away, away_other, part, after)
+        total = add_round(own, flip(send, CORE))
+        recv_half.append(flip(total, ZHIGH))
+        after = [recv_half[-1], same_other, cross_other]
+    both = [[one for one in part for one in (one, flip(one, CORE))] for part in grads]
+    keep = project_home(home, both, [total])
+    key_weight_grad, value_weight_grad = finish(keep, recv_half)
+    return (query_grad, key_weight_grad, value_weight_grad)
+
+
 def solution(mesh):
-    placed = (
-        P(("dp", "seq"), None),
-        P(("dp", "seq"), None),
-        P(("dp", "seq"), None),
-        P(("dp", "seq"), None),
-        P(("dp", "seq"), None),
-    )
+    spread = P(("dp", "seq"), None)
+    cube = dict(mesh.shape) == {"dp": 16, "seq": 2}
     return jax.shard_map(
-        local,
+        cube_local if cube else general_local,
         mesh=mesh,
-        in_specs=placed,
-        out_specs=(P(("dp", "seq"), None), P("dp", "seq"), P("dp", "seq")),
+        in_specs=(spread,) * 5,
+        out_specs=(spread, P("dp", "seq"), P("dp", "seq")),
         check_vma=False,
     )

time: 420 us -> 83.9 us (0.20)
  waiting for transfers between devices: 316 us -> 38.4 us
  matrix products: 45.3 us -> 0 us
  local copies, waits for them, and re-layouts: 17.6 us -> 0 us
  between operations: 14.9 us -> 0.8 us
  Pallas kernels: 0 us -> 13.6 us
  starting transfers between devices: 18.5 us -> 30.8 us
  other arithmetic: 6.5 us -> 0 us
    psum x1 -> x0, waiting for transfers between devices: 279 us -> none  [local(): key_full, value_full = lax.psum((key_part, value_part), 'dp')]
    dot_general x82 -> x0, matrix products: 45.3 us -> none  [the longest x16 11.7 us: local(): lax.dot_general(query_block, key_block, (((1,), (1,)), ((), ())), preferr...]
    ppermute x0 -> x30, waiting for transfers between devices: none -> 38.4 us  [the longest x23 21.4 us: flip(): return lax.ppermute(array, 'dp', [(i, i ^ mask) for i in range(16)])]
    all_to_all x5 -> x0, waiting for transfers between devices: 36.9 us -> none  [the longest x1 12.5 us: local(): lax.all_to_all(out_grad, 'seq', split_axis=1, concat_axis=0, tiled=True)]
    ppermute x0 -> x30, starting transfers between devices: none -> 30.8 us  [the longest x23 16.9 us: flip(): return lax.ppermute(array, 'dp', [(i, i ^ mask) for i in range(16)])]
    all_to_all x5 -> x0, starting transfers between devices: 18.4 us -> none  [the longest x1 4.23 us: local(): lax.all_to_all(keys, 'seq', split_axis=1, concat_axis=0, tiled=True)]
    pallas_call x0 -> x14, Pallas kernels: none -> 13.6 us  [the longest x2 6.19 us: attention(): pl.pallas_call(body, out_shape=[jax.ShapeDtypeStruct((rows, width), BF),...]
    unnamed x99 -> x0, local copies, waits for them, and re-layouts: 12.5 us -> none
  transfers between devices with their start and end apart: 7 -> 30, of which waited for: 6 -> 16; matrix products, arithmetic and copies ran while one was open for 13% -> 0% of each run, Pallas kernels for 0% -> 11%
where the time goes in v2:
time: 83.9 us; the launch traced here: 83.6 us
  waiting for transfers between devices  38.4 us (46%)
  starting transfers between devices  30.8 us (37%)
  Pallas kernels  13.6 us (16%)
    ppermute x23, waiting for transfers between devices, flip(): return lax.ppermute(array, 'dp', [(i, i ^ mask) for i in range(16)])  21.4 us
    ppermute x23, starting transfers between devices, flip(): return lax.ppermute(array, 'dp', [(i, i ^ mask) for i in range(16)])  16.9 us
    ppermute x5, waiting for transfers between devices, swap_seq(): return lax.ppermute(array, 'seq', [(0, 1), (1, 0)])  16.8 us
    ppermute x5, starting transfers between devices, swap_seq(): return lax.ppermute(array, 'seq', [(0, 1), (1, 0)])  7.71 us
    pallas_call x2, Pallas kernels, attention(): pl.pallas_call(body, out_shape=[jax.ShapeDtypeStruct((rows, width), BF),...  6.19 us
    ppermute x2, starting transfers between devices, cube_local(): kv_recv = [lax.ppermute(part, 'seq', [(0, 1)]) for part in kv]  6.18 us
  transfers between devices with their start and end apart: 30, of which 16 were waited for; matrix products, arithmetic and copies ran while one was open for 0% of the time, Pallas kernels for 11%

profile of v2, /device:TPU:0, one launch (start us, length us, event | category | flops | bytes accessed | tf_op | source)
XLA Modules:
  0.0 83.6 jit_solution(12151465663279785671)
XLA Ops:
  0.6 1.6 %prepare.1 = (bf16[128,1024]{1,0:T(8,128)(2,1)S(1)}, bf16[128,1024]{1,0:T(8,128)(2,1)S(1)}, bf16[128,1024]{1,0:T(8,128)(2,1)S(1)}, bf16[128,1024]{1,0:T(8,128)(2...) custom-call(s32[1]{0:T(128)} %bitcast.1.me_ref, ...), custom_call_target="tpu_custom_call" | custom-call | tf_op jit(solution)/shard_map/prepare/pallas_call | solution.py:207
  2.2 4.9 %collective-permute-start.1 = (bf16[128,1024]{1,0:T(8,128)(2,1)S(1)}, bf16[128,1024]{1,0:T(8,128)(2,1)S(1)}, u32[]{:S(2)}, u32[]{:S(2)}) collective-permute-start(bf16[128,1024]{1,0:T(8,128)(2,1)S(1)} %get-tuple-element.38), channel_id=1, source_target_pairs={{0,1},{2,3},{4,5},{6,7},{8,9},{10,11},{12,13},{14,15},{16,17},{18,... | collective-permute-start | bytes 786440 | tf_op jit(solution)/shard_map/ppermute | solution.py:539
  7.1 1.6 %collective-permute-start.2 = (bf16[4,128,256]{2,1,0:T(8,128)(2,1)S(1)}, bf16[4,128,256]{2,1,0:T(8,128)(2,1)S(1)}, u32[]{:S(2)}, u32[]{:S(2)}) collective-permute-start(bf16[4,128,256]{2,1,0:T(8,128)(2,1)S(1)} %get-tuple-element.40), channel_id=1, source_target_pairs={{0,4},{2,6},{4,0},{6,2},{8,12},{10,14},{12,8},{14,10},{16,20},{18,... | collective-permute-start | bytes 786440 | tf_op jit(solution)/shard_map/ppermute | solution.py:136
  8.7 1.6 %collective-permute-start.3 = (bf16[4,128,256]{2,1,0:T(8,128)(2,1)S(1)}, bf16[4,128,256]{2,1,0:T(8,128)(2,1)S(1)}, u32[]{:S(2)}, u32[]{:S(2)}) collective-permute-start(bf16[4,128,256]{2,1,0:T(8,128)(2,1)S(1)} %get-tuple-element.41), channel_id=1, source_target_pairs={{0,8},{2,10},{4,12},{6,14},{8,0},{10,2},{12,4},{14,6},{16,24},{18,... | collective-permute-start | bytes 786440 | tf_op jit(solution)/shard_map/ppermute | solution.py:136
  10.3 0.4 collective-permute-start.4
  10.7 1.3 %collective-permute-start = (bf16[128,1024]{1,0:T(8,128)(2,1)S(1)}, bf16[128,1024]{1,0:T(8,128)(2,1)S(1)}, u32[]{:S(2)}, u32[]{:S(2)}) collective-permute-start(bf16[128,1024]{1,0:T(8,128)(2,1)S(1)} %get-tuple-element.35), channel_id=1, source_target_pairs={{0,1},{2,3},{4,5},{6,7},{8,9},{10,11},{12,13},{14,15},{16,17},{18,... | collective-permute-start | bytes 786440 | tf_op jit(solution)/shard_map/ppermute | solution.py:539
  12.0 1.6 %stage.1 = (bf16[128,4096]{1,0:T(8,128)(2,1)S(1)}, bf16[128,4096]{1,0:T(8,128)(2,1)S(1)}, f32[256,128]{1,0:T(8,128)S(1)}, f32[256,128]{1,0:T(8,128)S(1)}) custom-call(bf16[128,4096]{1,0:T(8,128)(2,1)} %refs_0_.1, bf16[128,4096]{1,0:T(8,128)(2,1)} %refs_1_.1, f32[256,128]{1,0:T(8,128)} %constant.12.clone.refs_2_, f32[256,128]{1,0:T(8,128)} %constant.13.clone.refs_3_), custom_call_target="tpu_custom_call" | custom-call | tf_op jit(solution)/shard_map/stage/pallas_call | solution.py:231
  13.6 0.2 collective-permute-done.1.kv_ref
  13.8 3.1 %attention.2 = (bf16[128,4096]{1,0:T(8,128)(2,1)}, f32[128,512]{1,0:T(8,128)S(1)}, bf16[128,512]{1,0:T(8,128)(2,1)S(1)}, bf16[256,512]{1,0:T(8,128)(2,1)S(1)}) custom-call(s32[1]{0:T(128)} %bitcast.at_ref, bf16[128,4096]{1,0:T(8,128)(2,1)S(1)} %get-tuple-element.31.q_ref, bf16[128,4096]{1,0:T(8,128)(2,1)S(1)} %get-tuple-element.32.g_ref, ...), custom_call_target="tpu_custom_call" | custom-call | tf_op jit(solution)/shard_map/attention/pallas_call | solution.py:419
  16.9 3.5 %collective-permute-start.10 = (bf16[256,512]{1,0:T(8,128)(2,1)S(1)}, bf16[256,512]{1,0:T(8,128)(2,1)S(1)}, u32[]{:S(2)}, u32[]{:S(2)}) collective-permute-start(bf16[256,512]{1,0:T(8,128)(2,1)S(1)} %get-tuple-element.50), channel_id=1, source_target_pairs={{0,1},{1,0},{2,3},{3,2},{4,5},{5,4},{6,7},{7,6},{8,9},{9,8},{10,11... | collective-permute-start | bytes 786440 | tf_op jit(solution)/shard_map/ppermute | solution.py:140
  20.4 1.4 %collective-permute-done.4.rest_3_.refs_3_ = bf16[4,128,256]{2,1,0:T(8,128)(2,1)S(1)} collective-permute-done((bf16[4,128,256]{2,1,0:T(8,128)(2,1)S(1)}, bf16[4,128,256]{2,1,0:T(8,128)(2,1)S(1)}, u32[]{:S(2)}, u32[]{:S(2)}) %collective-permute-start.4) | collective-permute-done | bytes 262176 | tf_op jit(solution)/shard_map/ppermute | solution.py:136
  21.8 3.1 %attention.3 = (bf16[128,4096]{1,0:T(8,128)(2,1)}, f32[128,512]{1,0:T(8,128)S(1)}, bf16[128,512]{1,0:T(8,128)(2,1)S(1)}, bf16[256,512]{1,0:T(8,128)(2,1)S(1)}) custom-call(s32[1]{0:T(128)} %bitcast.at_ref, bf16[128,4096]{1,0:T(8,128)(2,1)S(1)} %get-tuple-element.31.q_ref, ...), custom_call_target="tpu_custom_call", output_to_operand_aliasing={{0}: (8, {})} | custom-call | tf_op jit(solution)/shard_map/attention/pallas_call | solution.py:419
  24.9 0.6 collective-permute-start.18
  25.6 1.6 %collective-permute-start.12 = (bf16[256,512]{1,0:T(8,128)(2,1)S(1)}, bf16[256,512]{1,0:T(8,128)(2,1)S(1)}, u32[]{:S(2)}, u32[]{:S(2)}) collective-permute-start(bf16[256,512]{1,0:T(8,128)(2,1)S(1)} %combine.2.refs_0_.refs_4_), channel_id=1, source_target_pairs={{0,4},{2,6},{4,0},{6,2},{8,12},{10,14},{12,8},{14,10},{16,20},{18,... | collective-permute-start | bytes 786440 | tf_op jit(solution)/shard_map/ppermute | solution.py:136
  27.2 1.5 %collective-permute-start.5 = (bf16[4,2,128,256]{3,2,1,0:T(8,128)(2,1)S(1)}, bf16[4,2,128,256]{3,2,1,0:T(8,128)(2,1)S(1)}, u32[]{:S(2)}, u32[]{:S(2)}) collective-permute-start(bf16[4,2,128,256]{3,2,1,0:T(8,128)(2,1)S(1)} %pack_normed.2.xa_ref), channel_id=1, source_target_pairs={{0,1},{1,0},{2,3},{3,2},{4,5},{5,4},{6,7},{7,6},{8,9},{9,8},{10,11... | collective-permute-start | bytes 1572872 | tf_op jit(solution)/shard_map/ppermute | solution.py:140
  28.7 1.6 %collective-permute-start.14 = (bf16[256,512]{1,0:T(8,128)(2,1)S(1)}, bf16[256,512]{1,0:T(8,128)(2,1)S(1)}, u32[]{:S(2)}, u32[]{:S(2)}) collective-permute-start(bf16[256,512]{1,0:T(8,128)(2,1)S(1)} %combine.2.refs_0_.refs_4_), channel_id=1, source_target_pairs={{0,8},{2,10},{4,12},{6,14},{8,0},{10,2},{12,4},{14,6},{16,24},{18,... | collective-permute-start | bytes 786440 | tf_op jit(solution)/shard_map/ppermute | solution.py:136
  30.3 3.9 %collective-permute-done.18.recv_ref = bf16[256,512]{1,0:T(8,128)(2,1)S(1)} collective-permute-done((bf16[256,512]{1,0:T(8,128)(2,1)S(1)}, bf16[256,512]{1,0:T(8,128)(2,1)S(1)}, u32[]{:S(2)}, u32[]{:S(2)}) %collective-permute-start.18) | collective-permute-done | bytes 262176 | tf_op jit(solution)/shard_map/ppermute | solution.py:140
  34.2 0.2 combine.3.refs_0_.refs_12_
  34.4 1.5 %collective-permute-start.20 = (bf16[256,512]{1,0:T(8,128)(2,1)S(1)}, bf16[256,512]{1,0:T(8,128)(2,1)S(1)}, u32[]{:S(2)}, u32[]{:S(2)}) collective-permute-start(bf16[256,512]{1,0:T(8,128)(2,1)S(1)} %combine.3.refs_0_.refs_12_), channel_id=1, source_target_pairs={{0,4},{2,6},{4,0},{6,2},{8,12},{10,14},{12,8},{14,10},{16,20},{18,... | collective-permute-start | bytes 786440 | tf_op jit(solution)/shard_map/ppermute | solution.py:136
  36.0 1.6 %collective-permute-start.22 = (bf16[256,512]{1,0:T(8,128)(2,1)S(1)}, bf16[256,512]{1,0:T(8,128)(2,1)S(1)}, u32[]{:S(2)}, u32[]{:S(2)}) collective-permute-start(bf16[256,512]{1,0:T(8,128)(2,1)S(1)} %combine.3.refs_0_.refs_12_), channel_id=1, source_target_pairs={{0,8},{2,10},{4,12},{6,14},{8,0},{10,2},{12,4},{14,6},{16,24},{18,... | collective-permute-start | bytes 786440 | tf_op jit(solution)/shard_map/ppermute | solution.py:136
  37.6 0.6 collective-permute-start.16
  38.1 4.6 %collective-permute-done.5.refs_4_.xb_ref = bf16[4,2,128,256]{3,2,1,0:T(8,128)(2,1)S(1)} collective-permute-done((bf16[4,2,128,256]{3,2,1,0:T(8,128)(2,1)S(1)}, bf16[4,2,128,256]{3,2,1,0:T(8,128)(2,1)S(1)}, u32[]{:S(2)}, u32[]{:S(2)}) %collective-permute-start.5) | collective-permute-done | bytes 524320 | tf_op jit(solution)/shard_map/ppermute | solution.py:140
  42.7 1.2 %collective-permute-done.16.refs_3_.refs_10_ = bf16[256,512]{1,0:T(8,128)(2,1)S(1)} collective-permute-done((bf16[256,512]{1,0:T(8,128)(2,1)S(1)}, bf16[256,512]{1,0:T(8,128)(2,1)S(1)}, u32[]{:S(2)}, u32[]{:S(2)}) %collective-permute-start.16) | collective-permute-done | bytes 262176 | tf_op jit(solution)/shard_map/ppermute | solution.py:136
  43.9 0.7 project_away.2
  44.8 0.9 %collective-permute-start.7 = (bf16[4,128,256]{2,1,0:T(8,128)(2,1)S(1)}, bf16[4,128,256]{2,1,0:T(8,128)(2,1)S(1)}, u32[]{:S(2)}, u32[]{:S(2)}) collective-permute-start(bf16[4,128,256]{2,1,0:T(8,128)(2,1)S(1)} %get-tuple-element.46.refs_0_), channel_id=1, source_target_pairs={{0,1},{1,0},{2,3},{3,2},{4,5},{5,4},{6,7},{7,6},{8,9},{9,8},{10,11... | collective-permute-start | bytes 786440 | tf_op jit(solution)/shard_map/ppermute | solution.py:140
  45.7 1.2 %collective-permute-start.8 = (bf16[4,128,256]{2,1,0:T(8,128)(2,1)S(1)}, bf16[4,128,256]{2,1,0:T(8,128)(2,1)S(1)}, u32[]{:S(2)}, u32[]{:S(2)}) collective-permute-start(bf16[4,128,256]{2,1,0:T(8,128)(2,1)S(1)} %get-tuple-element.47), channel_id=1, source_target_pairs={{0,1},{1,0},{2,3},{3,2},{4,5},{5,4},{6,7},{7,6},{8,9},{9,8},{10,11... | collective-permute-start | bytes 786440 | tf_op jit(solution)/shard_map/ppermute | solution.py:140
  46.9 1.3 %collective-permute-start.24 = (bf16[256,512]{1,0:T(8,128)(2,1)S(1)}, bf16[256,512]{1,0:T(8,128)(2,1)S(1)}, u32[]{:S(2)}, u32[]{:S(2)}) collective-permute-start(bf16[256,512]{1,0:T(8,128)(2,1)S(1)} %collective-permute-done.22.refs_5_.refs_2_.refs_16_), channel_id=1, source_target_pairs={{0,4},{2,6},{4,0},{6,2},{8,12},{10,14},{12,8},{14,10},{16,20},{18,... | collective-permute-start | bytes 786440 | tf_op jit(solution)/shard_map/ppermute | solution.py:136
  48.3 2.7 %collective-permute-start.27 = (bf16[256,512]{1,0:T(8,128)(2,1)S(1)}, bf16[256,512]{1,0:T(8,128)(2,1)S(1)}, u32[]{:S(2)}, u32[]{:S(2)}) collective-permute-start(bf16[256,512]{1,0:T(8,128)(2,1)S(1)} %add_round.2), channel_id=1, source_target_pairs={{0,16},{2,18},{4,20},{6,22},{8,24},{10,26},{12,28},{14,30},{16,0},... | collective-permute-start | bytes 786440 | tf_op jit(solution)/shard_map/ppermute | solution.py:136
  50.9 3.0 %collective-permute-done.7.refs_5_.refs_2_ = bf16[4,128,256]{2,1,0:T(8,128)(2,1)S(1)} collective-permute-done((bf16[4,128,256]{2,1,0:T(8,128)(2,1)S(1)}, bf16[4,128,256]{2,1,0:T(8,128)(2,1)S(1)}, u32[]{:S(2)}, u32[]{:S(2)}) %collective-permute-start.7) | collective-permute-done | bytes 262176 | tf_op jit(solution)/shard_map/ppermute | solution.py:140
  54.0 5.2 %collective-permute-done.8.refs_6_ = bf16[4,128,256]{2,1,0:T(8,128)(2,1)S(1)} collective-permute-done((bf16[4,128,256]{2,1,0:T(8,128)(2,1)S(1)}, bf16[4,128,256]{2,1,0:T(8,128)(2,1)S(1)}, u32[]{:S(2)}, u32[]{:S(2)}) %collective-permute-start.8) | collective-permute-done | bytes 262176 | tf_op jit(solution)/shard_map/ppermute | solution.py:140
  59.2 3.5 %collective-permute-done.27.refs_4_.refs_0_ = bf16[256,512]{1,0:T(8,128)(2,1)S(1)} collective-permute-done((bf16[256,512]{1,0:T(8,128)(2,1)S(1)}, bf16[256,512]{1,0:T(8,128)(2,1)S(1)}, u32[]{:S(2)}, u32[]{:S(2)}) %collective-permute-start.27) | collective-permute-done | bytes 262176 | tf_op jit(solution)/shard_map/ppermute | solution.py:136
  62.7 0.7 project_away.3
  63.5 0.5 collective-permute-start.11
  64.1 0.4 collective-permute-start.13
  64.6 1.2 %collective-permute-done.11.refs_5_ = bf16[256,512]{1,0:T(8,128)(2,1)S(1)} collective-permute-done((bf16[256,512]{1,0:T(8,128)(2,1)S(1)}, bf16[256,512]{1,0:T(8,128)(2,1)S(1)}, u32[]{:S(2)}, u32[]{:S(2)}) %collective-permute-start.11) | collective-permute-done | bytes 262176 | tf_op jit(solution)/shard_map/ppermute | solution.py:136
  65.9 0.4 collective-permute-start.21
  66.4 0.2 collective-permute-start.23
  66.6 0.4 collective-permute-start.17
  67.1 0.2 collective-permute-done.6.refs_1_
  67.3 0.1 collective-permute-start.25
  67.5 0.2 collective-permute-done.21.refs_15_
  67.7 0.4 collective-permute-done.23.refs_17_
  68.1 0.4 collective-permute-done.17.refs_11_
  68.5 0.4 collective-permute-done.9.refs_3_
  68.8 0.4 collective-permute-done.25.refs_19_
  69.2 1.3 %project_home.1.keep_ref = f32[256,1024]{1,0:T(8,128)S(1)} custom-call(bf16[4,128,256]{2,1,0:T(8,128)(2,1)S(1)} %get-tuple-element.46.refs_0_, bf16[4,128,256]{2,1,0:T(8,128)(2,1)S(1)} %collective-permute-done.6.refs_1_, bf16[4,128,256]{2,1,0:T(8,128)(2,1)S(1)} %collective-permute-done.7.refs_5_.refs_2_, ...), custom_call_target="tpu_custom_call" | custom-call | tf_op jit(solution)/shard_map/project_home/pallas_call | solution.py:496
  70.5 12.1 %collective-permute-done.29.refs_1_ = bf16[256,512]{1,0:T(8,128)(2,1)S(1)} collective-permute-done((bf16[256,512]{1,0:T(8,128)(2,1)S(1)}, bf16[256,512]{1,0:T(8,128)(2,1)S(1)}, u32[]{:S(2)}, u32[]{:S(2)}) %collective-permute-start.29) | collective-permute-done | bytes 262176 | tf_op jit(solution)/shard_map/ppermute | solution.py:136
  82.6 1.1 %finish.1 = (f32[256,512]{1,0:T(8,128)}, f32[256,512]{1,0:T(8,128)}) custom-call(f32[256,1024]{1,0:T(8,128)S(1)} %project_home.1.keep_ref, bf16[256,512]{1,0:T(8,128)(2,1)S(1)} %collective-permute-done.27.refs_4_.refs_0_, bf16[256,512]{1,0:T(8,128)(2,1)S(1)} %collective-permute-done.29.refs_1_), custom_call_target="tpu_custom_call" | custom-call | tf_op jit(solution)/shard_map/finish/pallas_call | solution.py:521
  (26 shorter events, 0.8 us)
Async XLA Ops:
  2.2 11.6 %collective-permute-start.1 = (bf16[128,1024]{1,0:T(8,128)(2,1)S(1)}, bf16[128,1024]{1,0:T(8,128)(2,1)S(1)}, u32[]{:S(2)}, u32[]{:S(2)}) collective-permute-start(bf16[128,1024]{1,0:T(8,128)(2,1)S(1)} %get-tuple-element.38), channel_id=1, source_target_pairs={{0,1},{2,3},{4,5},{6,7},{8,9},{10,11},{12,13},{14,15},{16,17},{18,... | collective-permute-start | bytes 786440 | tf_op jit(solution)/shard_map/ppermute | solution.py:539
  7.1 13.3 %collective-permute-start.2 = (bf16[4,128,256]{2,1,0:T(8,128)(2,1)S(1)}, bf16[4,128,256]{2,1,0:T(8,128)(2,1)S(1)}, u32[]{:S(2)}, u32[]{:S(2)}) collective-permute-start(bf16[4,128,256]{2,1,0:T(8,128)(2,1)S(1)} %get-tuple-element.40), channel_id=1, source_target_pairs={{0,4},{2,6},{4,0},{6,2},{8,12},{10,14},{12,8},{14,10},{16,20},{18,... | collective-permute-start | bytes 786440 | tf_op jit(solution)/shard_map/ppermute | solution.py:136
  8.7 11.7 %collective-permute-start.3 = (bf16[4,128,256]{2,1,0:T(8,128)(2,1)S(1)}, bf16[4,128,256]{2,1,0:T(8,128)(2,1)S(1)}, u32[]{:S(2)}, u32[]{:S(2)}) collective-permute-start(bf16[4,128,256]{2,1,0:T(8,128)(2,1)S(1)} %get-tuple-element.41), channel_id=1, source_target_pairs={{0,8},{2,10},{4,12},{6,14},{8,0},{10,2},{12,4},{14,6},{16,24},{18,... | collective-permute-start | bytes 786440 | tf_op jit(solution)/shard_map/ppermute | solution.py:136
  10.3 11.5 %collective-permute-start.4 = (bf16[4,128,256]{2,1,0:T(8,128)(2,1)S(1)}, bf16[4,128,256]{2,1,0:T(8,128)(2,1)S(1)}, u32[]{:S(2)}, u32[]{:S(2)}) collective-permute-start(bf16[4,128,256]{2,1,0:T(8,128)(2,1)S(1)} %get-tuple-element.42), channel_id=1, source_target_pairs={{0,12},{2,14},{4,8},{6,10},{8,4},{10,6},{12,0},{14,2},{16,28},{18,... | collective-permute-start | bytes 786440 | tf_op jit(solution)/shard_map/ppermute | solution.py:136
  10.7 11.1 %collective-permute-start = (bf16[128,1024]{1,0:T(8,128)(2,1)S(1)}, bf16[128,1024]{1,0:T(8,128)(2,1)S(1)}, u32[]{:S(2)}, u32[]{:S(2)}) collective-permute-start(bf16[128,1024]{1,0:T(8,128)(2,1)S(1)} %get-tuple-element.35), channel_id=1, source_target_pairs={{0,1},{2,3},{4,5},{6,7},{8,9},{10,11},{12,13},{14,15},{16,17},{18,... | collective-permute-start | bytes 786440 | tf_op jit(solution)/shard_map/ppermute | solution.py:539
  16.9 8.6 %collective-permute-start.10 = (bf16[256,512]{1,0:T(8,128)(2,1)S(1)}, bf16[256,512]{1,0:T(8,128)(2,1)S(1)}, u32[]{:S(2)}, u32[]{:S(2)}) collective-permute-start(bf16[256,512]{1,0:T(8,128)(2,1)S(1)} %get-tuple-element.50), channel_id=1, source_target_pairs={{0,1},{1,0},{2,3},{3,2},{4,5},{5,4},{6,7},{7,6},{8,9},{9,8},{10,11... | collective-permute-start | bytes 786440 | tf_op jit(solution)/shard_map/ppermute | solution.py:140
  24.9 9.3 %collective-permute-start.18 = (bf16[256,512]{1,0:T(8,128)(2,1)S(1)}, bf16[256,512]{1,0:T(8,128)(2,1)S(1)}, u32[]{:S(2)}, u32[]{:S(2)}) collective-permute-start(bf16[256,512]{1,0:T(8,128)(2,1)S(1)} %get-tuple-element.52), channel_id=1, source_target_pairs={{0,1},{1,0},{2,3},{3,2},{4,5},{5,4},{6,7},{7,6},{8,9},{9,8},{10,11... | collective-permute-start | bytes 786440 | tf_op jit(solution)/shard_map/ppermute | solution.py:140
  25.6 8.6 %collective-permute-start.12 = (bf16[256,512]{1,0:T(8,128)(2,1)S(1)}, bf16[256,512]{1,0:T(8,128)(2,1)S(1)}, u32[]{:S(2)}, u32[]{:S(2)}) collective-permute-start(bf16[256,512]{1,0:T(8,128)(2,1)S(1)} %combine.2.refs_0_.refs_4_), channel_id=1, source_target_pairs={{0,4},{2,6},{4,0},{6,2},{8,12},{10,14},{12,8},{14,10},{16,20},{18,... | collective-permute-start | bytes 786440 | tf_op jit(solution)/shard_map/ppermute | solution.py:136
  27.2 15.6 %collective-permute-start.5 = (bf16[4,2,128,256]{3,2,1,0:T(8,128)(2,1)S(1)}, bf16[4,2,128,256]{3,2,1,0:T(8,128)(2,1)S(1)}, u32[]{:S(2)}, u32[]{:S(2)}) collective-permute-start(bf16[4,2,128,256]{3,2,1,0:T(8,128)(2,1)S(1)} %pack_normed.2.xa_ref), channel_id=1, source_target_pairs={{0,1},{1,0},{2,3},{3,2},{4,5},{5,4},{6,7},{7,6},{8,9},{9,8},{10,11... | collective-permute-start | bytes 1572872 | tf_op jit(solution)/shard_map/ppermute | solution.py:140
  28.7 8.9 %collective-permute-start.14 = (bf16[256,512]{1,0:T(8,128)(2,1)S(1)}, bf16[256,512]{1,0:T(8,128)(2,1)S(1)}, u32[]{:S(2)}, u32[]{:S(2)}) collective-permute-start(bf16[256,512]{1,0:T(8,128)(2,1)S(1)} %combine.2.refs_0_.refs_4_), channel_id=1, source_target_pairs={{0,8},{2,10},{4,12},{6,14},{8,0},{10,2},{12,4},{14,6},{16,24},{18,... | collective-permute-start | bytes 786440 | tf_op jit(solution)/shard_map/ppermute | solution.py:136
  34.4 8.3 %collective-permute-start.20 = (bf16[256,512]{1,0:T(8,128)(2,1)S(1)}, bf16[256,512]{1,0:T(8,128)(2,1)S(1)}, u32[]{:S(2)}, u32[]{:S(2)}) collective-permute-start(bf16[256,512]{1,0:T(8,128)(2,1)S(1)} %combine.3.refs_0_.refs_12_), channel_id=1, source_target_pairs={{0,4},{2,6},{4,0},{6,2},{8,12},{10,14},{12,8},{14,10},{16,20},{18,... | collective-permute-start | bytes 786440 | tf_op jit(solution)/shard_map/ppermute | solution.py:136
  36.0 6.8 %collective-permute-start.22 = (bf16[256,512]{1,0:T(8,128)(2,1)S(1)}, bf16[256,512]{1,0:T(8,128)(2,1)S(1)}, u32[]{:S(2)}, u32[]{:S(2)}) collective-permute-start(bf16[256,512]{1,0:T(8,128)(2,1)S(1)} %combine.3.refs_0_.refs_12_), channel_id=1, source_target_pairs={{0,8},{2,10},{4,12},{6,14},{8,0},{10,2},{12,4},{14,6},{16,24},{18,... | collective-permute-start | bytes 786440 | tf_op jit(solution)/shard_map/ppermute | solution.py:136
  37.6 6.4 %collective-permute-start.16 = (bf16[256,512]{1,0:T(8,128)(2,1)S(1)}, bf16[256,512]{1,0:T(8,128)(2,1)S(1)}, u32[]{:S(2)}, u32[]{:S(2)}) collective-permute-start(bf16[256,512]{1,0:T(8,128)(2,1)S(1)} %collective-permute-done.14.refs_2_.refs_8_), channel_id=1, source_target_pairs={{0,4},{2,6},{4,0},{6,2},{8,12},{10,14},{12,8},{14,10},{16,20},{18,... | collective-permute-start | bytes 786440 | tf_op jit(solution)/shard_map/ppermute | solution.py:136
  44.7 3.6 %collective-permute-start.26 = (f32[256,512]{1,0:T(8,128)S(1)}, f32[256,512]{1,0:T(8,128)S(1)}, u32[]{:S(2)}, u32[]{:S(2)}) collective-permute-start(f32[256,512]{1,0:T(8,128)S(1)} %get-tuple-element.54), channel_id=1, source_target_pairs={{0,2},{2,0},{4,6},{6,4},{8,10},{10,8},{12,14},{14,12},{16,18},{18,... | collective-permute-start | bytes 1572872 | tf_op jit(solution)/shard_map/ppermute | solution.py:136
  44.8 9.2 %collective-permute-start.7 = (bf16[4,128,256]{2,1,0:T(8,128)(2,1)S(1)}, bf16[4,128,256]{2,1,0:T(8,128)(2,1)S(1)}, u32[]{:S(2)}, u32[]{:S(2)}) collective-permute-start(bf16[4,128,256]{2,1,0:T(8,128)(2,1)S(1)} %get-tuple-element.46.refs_0_), channel_id=1, source_target_pairs={{0,1},{1,0},{2,3},{3,2},{4,5},{5,4},{6,7},{7,6},{8,9},{9,8},{10,11... | collective-permute-start | bytes 786440 | tf_op jit(solution)/shard_map/ppermute | solution.py:140
  45.7 13.5 %collective-permute-start.8 = (bf16[4,128,256]{2,1,0:T(8,128)(2,1)S(1)}, bf16[4,128,256]{2,1,0:T(8,128)(2,1)S(1)}, u32[]{:S(2)}, u32[]{:S(2)}) collective-permute-start(bf16[4,128,256]{2,1,0:T(8,128)(2,1)S(1)} %get-tuple-element.47), channel_id=1, source_target_pairs={{0,1},{1,0},{2,3},{3,2},{4,5},{5,4},{6,7},{7,6},{8,9},{9,8},{10,11... | collective-permute-start | bytes 786440 | tf_op jit(solution)/shard_map/ppermute | solution.py:140
  46.9 12.3 %collective-permute-start.24 = (bf16[256,512]{1,0:T(8,128)(2,1)S(1)}, bf16[256,512]{1,0:T(8,128)(2,1)S(1)}, u32[]{:S(2)}, u32[]{:S(2)}) collective-permute-start(bf16[256,512]{1,0:T(8,128)(2,1)S(1)} %collective-permute-done.22.refs_5_.refs_2_.refs_16_), channel_id=1, source_target_pairs={{0,4},{2,6},{4,0},{6,2},{8,12},{10,14},{12,8},{14,10},{16,20},{18,... | collective-permute-start | bytes 786440 | tf_op jit(solution)/shard_map/ppermute | solution.py:136
  48.3 14.4 %collective-permute-start.27 = (bf16[256,512]{1,0:T(8,128)(2,1)S(1)}, bf16[256,512]{1,0:T(8,128)(2,1)S(1)}, u32[]{:S(2)}, u32[]{:S(2)}) collective-permute-start(bf16[256,512]{1,0:T(8,128)(2,1)S(1)} %add_round.2), channel_id=1, source_target_pairs={{0,16},{2,18},{4,20},{6,22},{8,24},{10,26},{12,28},{14,30},{16,0},... | collective-permute-start | bytes 786440 | tf_op jit(solution)/shard_map/ppermute | solution.py:136
  63.5 2.5 %collective-permute-start.28 = (f32[256,512]{1,0:T(8,128)S(1)}, f32[256,512]{1,0:T(8,128)S(1)}, u32[]{:S(2)}, u32[]{:S(2)}) collective-permute-start(f32[256,512]{1,0:T(8,128)S(1)} %get-tuple-element.56), channel_id=1, source_target_pairs={{0,2},{2,0},{4,6},{6,4},{8,10},{10,8},{12,14},{14,12},{16,18},{18,... | collective-permute-start | bytes 1572872 | tf_op jit(solution)/shard_map/ppermute | solution.py:136
  63.5 2.3 %collective-permute-start.11 = (bf16[256,512]{1,0:T(8,128)(2,1)S(1)}, bf16[256,512]{1,0:T(8,128)(2,1)S(1)}, u32[]{:S(2)}, u32[]{:S(2)}) collective-permute-start(bf16[256,512]{1,0:T(8,128)(2,1)S(1)} %combine.2.refs_0_.refs_4_), channel_id=1, source_target_pairs={{0,2},{2,0},{4,6},{6,4},{8,10},{10,8},{12,14},{14,12},{16,18},{18,... | collective-permute-start | bytes 786440 | tf_op jit(solution)/shard_map/ppermute | solution.py:136
  64.0 2.3 %collective-permute-start.19 = (bf16[256,512]{1,0:T(8,128)(2,1)S(1)}, bf16[256,512]{1,0:T(8,128)(2,1)S(1)}, u32[]{:S(2)}, u32[]{:S(2)}) collective-permute-start(bf16[256,512]{1,0:T(8,128)(2,1)S(1)} %combine.3.refs_0_.refs_12_), channel_id=1, source_target_pairs={{0,2},{2,0},{4,6},{6,4},{8,10},{10,8},{12,14},{14,12},{16,18},{18,... | collective-permute-start | bytes 786440 | tf_op jit(solution)/shard_map/ppermute | solution.py:136
  64.1 2.5 %collective-permute-start.13 = (bf16[256,512]{1,0:T(8,128)(2,1)S(1)}, bf16[256,512]{1,0:T(8,128)(2,1)S(1)}, u32[]{:S(2)}, u32[]{:S(2)}) collective-permute-start(bf16[256,512]{1,0:T(8,128)(2,1)S(1)} %collective-permute-done.12.rest_0_.refs_1_.refs_6_), channel_id=1, source_target_pairs={{0,2},{2,0},{4,6},{6,4},{8,10},{10,8},{12,14},{14,12},{16,18},{18,... | collective-permute-start | bytes 786440 | tf_op jit(solution)/shard_map/ppermute | solution.py:136
  64.5 2.4 %collective-permute-start.15 = (bf16[256,512]{1,0:T(8,128)(2,1)S(1)}, bf16[256,512]{1,0:T(8,128)(2,1)S(1)}, u32[]{:S(2)}, u32[]{:S(2)}) collective-permute-start(bf16[256,512]{1,0:T(8,128)(2,1)S(1)} %collective-permute-done.14.refs_2_.refs_8_), channel_id=1, source_target_pairs={{0,2},{2,0},{4,6},{6,4},{8,10},{10,8},{12,14},{14,12},{16,18},{18,... | collective-permute-start | bytes 786440 | tf_op jit(solution)/shard_map/ppermute | solution.py:136
  65.8 1.5 %collective-permute-start.6 = (bf16[4,128,256]{2,1,0:T(8,128)(2,1)S(1)}, bf16[4,128,256]{2,1,0:T(8,128)(2,1)S(1)}, u32[]{:S(2)}, u32[]{:S(2)}) collective-permute-start(bf16[4,128,256]{2,1,0:T(8,128)(2,1)S(1)} %get-tuple-element.47), channel_id=1, source_target_pairs={{0,2},{2,0},{4,6},{6,4},{8,10},{10,8},{12,14},{14,12},{16,18},{18,... | collective-permute-start | bytes 786440 | tf_op jit(solution)/shard_map/ppermute | solution.py:136
  65.9 1.8 %collective-permute-start.21 = (bf16[256,512]{1,0:T(8,128)(2,1)S(1)}, bf16[256,512]{1,0:T(8,128)(2,1)S(1)}, u32[]{:S(2)}, u32[]{:S(2)}) collective-permute-start(bf16[256,512]{1,0:T(8,128)(2,1)S(1)} %collective-permute-done.20.refs_4_.refs_1_.refs_14_), channel_id=1, source_target_pairs={{0,2},{2,0},{4,6},{6,4},{8,10},{10,8},{12,14},{14,12},{16,18},{18,... | collective-permute-start | bytes 786440 | tf_op jit(solution)/shard_map/ppermute | solution.py:136
  66.4 1.7 %collective-permute-start.23 = (bf16[256,512]{1,0:T(8,128)(2,1)S(1)}, bf16[256,512]{1,0:T(8,128)(2,1)S(1)}, u32[]{:S(2)}, u32[]{:S(2)}) collective-permute-start(bf16[256,512]{1,0:T(8,128)(2,1)S(1)} %collective-permute-done.22.refs_5_.refs_2_.refs_16_), channel_id=1, source_target_pairs={{0,2},{2,0},{4,6},{6,4},{8,10},{10,8},{12,14},{14,12},{16,18},{18,... | collective-permute-start | bytes 786440 | tf_op jit(solution)/shard_map/ppermute | solution.py:136
  66.6 1.9 %collective-permute-start.17 = (bf16[256,512]{1,0:T(8,128)(2,1)S(1)}, bf16[256,512]{1,0:T(8,128)(2,1)S(1)}, u32[]{:S(2)}, u32[]{:S(2)}) collective-permute-start(bf16[256,512]{1,0:T(8,128)(2,1)S(1)} %collective-permute-done.16.refs_3_.refs_10_), channel_id=1, source_target_pairs={{0,2},{2,0},{4,6},{6,4},{8,10},{10,8},{12,14},{14,12},{16,18},{18,... | collective-permute-start | bytes 786440 | tf_op jit(solution)/shard_map/ppermute | solution.py:136
  67.0 1.9 %collective-permute-start.9 = (bf16[4,128,256]{2,1,0:T(8,128)(2,1)S(1)}, bf16[4,128,256]{2,1,0:T(8,128)(2,1)S(1)}, u32[]{:S(2)}, u32[]{:S(2)}) collective-permute-start(bf16[4,128,256]{2,1,0:T(8,128)(2,1)S(1)} %collective-permute-done.8.refs_6_), channel_id=1, source_target_pairs={{0,2},{2,0},{4,6},{6,4},{8,10},{10,8},{12,14},{14,12},{16,18},{18,... | collective-permute-start | bytes 786440 | tf_op jit(solution)/shard_map/ppermute | solution.py:136
  67.3 1.9 %collective-permute-start.25 = (bf16[256,512]{1,0:T(8,128)(2,1)S(1)}, bf16[256,512]{1,0:T(8,128)(2,1)S(1)}, u32[]{:S(2)}, u32[]{:S(2)}) collective-permute-start(bf16[256,512]{1,0:T(8,128)(2,1)S(1)} %collective-permute-done.24.refs_3_.refs_18_), channel_id=1, source_target_pairs={{0,2},{2,0},{4,6},{6,4},{8,10},{10,8},{12,14},{14,12},{16,18},{18,... | collective-permute-start | bytes 786440 | tf_op jit(solution)/shard_map/ppermute | solution.py:136
  67.7 14.9 %collective-permute-start.29 = (bf16[256,512]{1,0:T(8,128)(2,1)S(1)}, bf16[256,512]{1,0:T(8,128)(2,1)S(1)}, u32[]{:S(2)}, u32[]{:S(2)}) collective-permute-start(bf16[256,512]{1,0:T(8,128)(2,1)S(1)} %add_round.3.refs_20_), channel_id=1, source_target_pairs={{0,16},{2,18},{4,20},{6,22},{8,24},{10,26},{12,28},{14,30},{16,0},... | collective-permute-start | bytes 786440 | tf_op jit(solution)/shard_map/ppermute | solution.py:136

commit v3 on v2

--- a/solution.py
+++ b/solution.py
@@ -13,7 +13,7 @@
 BF = jnp.bfloat16
 F32 = jnp.float32
 VMEM_LIMIT = 20 * 1024 * 1024
-VMEM_FULL = 60 * 1024 * 1024
+CUT = 4
 
 
 def unrotate(grad, position):
@@ -182,6 +182,7 @@
     share = width // 16
     wide = kv_width // (2 * NC)
 
+
     def body(me_ref, k_hbm, v_hbm, x_hbm, k_ref, v_ref, *rest):
         kv, parts, (x_ref, sem) = rest[:NC], rest[NC : NC + 4], rest[NC + 4 :]
         mine = me_ref[0]
@@ -239,6 +240,23 @@
     )(*[in_hbm(one) for one in arrays])
 
 
+def join_cores(same, recv, after):
+    def body(a_ref, b_ref, *refs):
+        out = refs[-1]
+        for place in range(4):
+            out[place, 0] = a_ref[place]
+            out[place, 1] = b_ref[place]
+
+    return pl.pallas_call(
+        body,
+        out_shape=pltpu.VMEM((4, 2) + same.shape[1:], BF),
+        in_specs=[vmem()] * 2 + [hbm()] * len(after),
+        out_specs=vmem(),
+        compiler_params=params(),
+        name="join_cores",
+    )(same, recv, *after)
+
+
 def pack_normed(parts, numbers, after):
     rows, share = parts[0].shape[1:]
     shapes = [(4,) + (len(group),) * (len(group) > 1) + (rows, share) for group in numbers]
@@ -290,7 +308,7 @@
 
 
 def attention(
-    chunk, seq_at, queries, out_grad, keys, values, kv_recv, cosine, sine, grad_so_far, after
+    chunk, seq_at, queries, out_grad, keys, values, kv_recv, cosine, sine, after
 ):
     rows, width = queries.shape
     wide = width // (2 * NC)
@@ -310,26 +328,19 @@
         return lax.dot_general(a, b, (((0,), (0,)), ((), ())), preferred_element_type=F32)
 
     def body(at_ref, q_ref, g_ref, k_ref, v_ref, kv_ref, cos_ref, sin_ref, *rest):
-        qg_hbm, keep_a, keep_b, send, qg_buf, out_sem = rest[-6:]
+        qg_ref, keep_a, keep_b, send = rest[-4:]
         late = at_ref[0]
 
         def columns(j, size):
             return pl.ds(pl.multiple_of(((late ^ j) * NC + chunk) * size, size), size)
 
-        outs = [
-            pltpu.make_async_copy(qg_buf.at[j], qg_hbm.at[:, columns(j, wide)], out_sem.at[j])
-            for j in range(2)
-        ]
         for j in (1, 0):
             one_side(
                 j, late,
                 q_ref.at[:, columns(j, wide)], g_ref.at[:, columns(j, wide)],
                 k_ref.at[:, columns(j, kv_wide)], v_ref.at[:, columns(j, kv_wide)],
-                kv_ref, cos_ref, sin_ref, qg_buf.at[j], keep_a, keep_b, send,
+                kv_ref, cos_ref, sin_ref, qg_ref.at[j], keep_a, keep_b, send,
             )
-            outs[j].start()
-        for copy in outs:
-            copy.wait()
 
     def one_side(
         other, late, q_ref, g_ref, k_ref, v_ref, kv_ref, cos_ref, sin_ref, qg_ref, keep_a, keep_b, send
@@ -408,32 +419,19 @@
             all_heads(False)
 
     operands = [seq_at, queries, out_grad, keys, values, kv_recv, cosine, sine]
-    specs = [smem()] + [vmem()] * 7
-    aliases = {}
-    if grad_so_far is not None:
-        specs.append(hbm())
-        operands.append(grad_so_far)
-        aliases = {8: 0}
-    specs += [hbm()] * len(after)
-    operands += after
     return pl.pallas_call(
         body,
         out_shape=[
-            jax.ShapeDtypeStruct((rows, width), BF),
+            pltpu.VMEM((2, rows, wide), BF),
             pltpu.VMEM((rows, 2 * kv_wide), F32),
             pltpu.VMEM((rows, 2 * kv_wide), BF),
             pltpu.VMEM((2 * rows, 2 * kv_wide), BF),
         ],
-        in_specs=specs,
-        out_specs=[hbm(), vmem(), vmem(), vmem()],
-        scratch_shapes=[
-            pltpu.VMEM((2, rows, wide), BF),
-            pltpu.SemaphoreType.DMA((2,)),
-        ],
-        input_output_aliases=aliases,
+        in_specs=[smem()] + [vmem()] * 7 + [hbm()] * len(after),
+        out_specs=[vmem()] * 4,
         compiler_params=params(),
         name="attention",
-    )(*operands)
+    )(*operands, *after)
 
 
 def tn(a, b):
@@ -445,62 +443,111 @@
     wide = grads[0].shape[1]
 
     def body(xa_ref, xb_ref, *refs):
-        ys, outs = refs[:4], refs[-2:]
+        ys, keep, sends = refs[:4], refs[-1 - CUT], refs[-CUT:]
         right = jnp.concatenate([ref[...] for ref in ys], axis=0)
-        for core, out in enumerate(outs):
+
+        def total(core):
             left = [x_ref[place, core] for place in range(4) for x_ref in (xa_ref, xb_ref)]
-            out[...] = tn(jnp.concatenate(left, axis=0), right)
-
-    return pl.pallas_call(
-        body,
-        out_shape=[pltpu.VMEM((share, wide), F32)] * 2,
+            return tn(jnp.concatenate(left, axis=0), right)
+
+        keep[...] = total(0)
+        sent = total(1)
+        for n, out in enumerate(sends):
+            out[...] = sent[n * share // CUT : (n + 1) * share // CUT]
+
+    return pl.pallas_call(
+        body,
+        out_shape=[pltpu.VMEM((share, wide), F32)] + [pltpu.VMEM((share // CUT, wide), F32)] * CUT,
         in_specs=[vmem()] * 6 + [hbm()] * len(after),
-        out_specs=[vmem()] * 2,
+        out_specs=[vmem()] * (1 + CUT),
         compiler_params=params(),
         name="project_away",
     )(normed_own, normed_other, *grads, *after)
 
 
-def add_round(own, recv):
-    def body(a_ref, b_ref, out):
-        out[...] = (a_ref[...] + b_ref[...]).astype(BF)
+def add_round(own, recv, after):
+    rows = own.shape[0] // CUT
+
+    def body(a_ref, *refs):
+        out = refs[-1]
+        for n, b_ref in enumerate(refs[:CUT]):
+            at = slice(n * rows, (n + 1) * rows)
+            out[at] = (a_ref[at] + b_ref[...]).astype(BF)
 
     return pl.pallas_call(
         body,
         out_shape=pltpu.VMEM(own.shape, BF),
-        in_specs=[vmem()] * 2,
+        in_specs=[vmem()] * (1 + CUT) + [hbm()] * len(after),
         out_specs=vmem(),
         compiler_params=params(),
         name="add_round",
-    )(own, recv)
-
-
-def project_home(normed, grads, after):
-    rows, share = normed[0].shape[1:]
+    )(own, *recv, *after)
+
+
+def join_places(grads, after):
+    length, wide = grads[0].shape
+
+    def body(*refs):
+        out = refs[-1]
+        for place, ref in enumerate(refs[:4]):
+            out[place * length : (place + 1) * length] = ref[...]
+
+    return pl.pallas_call(
+        body,
+        out_shape=pltpu.VMEM((4 * length, wide), BF),
+        in_specs=[vmem()] * 4 + [hbm()] * len(after),
+        out_specs=vmem(),
+        compiler_params=params(),
+        name="join_places",
+    )(*grads, *after)
+
+
+def project_home(seq_at, normed, grads, recv, query_grads, after):
+    rows, share = normed[0].shape[2:]
     wide = grads[0][0].shape[1]
     chunks = len(grads)
-
-    def body(*refs):
-        xs, ys, out = refs[:4], refs[4 : 4 + 8 * chunks], refs[-1]
-        left = [x_ref[place] for place in range(4) for x_ref in xs]
+    part = query_grads[0].shape[2]
+
+    def body(at_ref, xa_ref, xb_ref, *refs):
+        ys, refs = refs[: 4 * chunks], refs[4 * chunks :]
+        others, qs = refs[:chunks], refs[chunks : 2 * chunks]
+        out, query_out, sem = refs[-3:]
+        copies = []
+        for chunk, ref in enumerate(qs):
+            for j in range(2):
+                low = pl.multiple_of(((at_ref[0] ^ j) * chunks + chunk) * part, part)
+                copies.append(
+                    pltpu.make_async_copy(ref.at[j], query_out.at[:, pl.ds(low, part)], sem.at[chunk, j])
+                )
+        for copy in copies:
+            copy.start()
+        left = [
+            x_ref[place, core] for place in range(4) for x_ref in (xa_ref, xb_ref) for core in range(2)
+        ]
         left = jnp.concatenate(left, axis=0)
         for chunk in range(chunks):
-            right = [
-                ys[chunk * 8 + place * 2 + core][seq * rows : (seq + 1) * rows, :]
-                for place in range(4)
-                for seq in range(2)
-                for core in range(2)
-            ]
+            right = []
+            for place in range(4):
+                for seq in range(2):
+                    right.append(ys[chunk * 4 + place][seq * rows : (seq + 1) * rows, :])
+                    low = (place * 2 + seq) * rows
+                    right.append(others[chunk][low : low + rows, :])
             out[:, chunk * wide : (chunk + 1) * wide] = tn(left, jnp.concatenate(right, axis=0))
-
-    return pl.pallas_call(
-        body,
-        out_shape=pltpu.VMEM((share, chunks * wide), F32),
-        in_specs=[vmem()] * (4 + 8 * chunks) + [hbm()] * len(after),
-        out_specs=vmem(),
+        for copy in copies:
+            copy.wait()
+
+    return pl.pallas_call(
+        body,
+        out_shape=[
+            pltpu.VMEM((share, chunks * wide), F32),
+            jax.ShapeDtypeStruct((rows, 2 * chunks * part), BF),
+        ],
+        in_specs=[smem()] + [vmem()] * (2 + 6 * chunks) + [hbm()] * len(after),
+        out_specs=[vmem(), hbm()],
+        scratch_shapes=[pltpu.SemaphoreType.DMA((chunks, 2))],
         compiler_params=params(),
         name="project_home",
-    )(*normed, *[part for parts in grads for part in parts], *after)
+    )(seq_at, *normed, *[part for parts in grads for part in parts], *recv, *query_grads, *after)
 
 
 def finish(keep, recv_half):
@@ -541,36 +588,41 @@
     parts = [flip(part, mask) if mask else part for part, mask in zip(parts, masks)]
     q_in, g_in, cosine, sine = stage([queries, out_grad, cosine, sine])
 
-    query_grad = None
-    made = []
+    query_grads, made = [], []
     for chunk in range(NC):
         query_grad, *rest = attention(
-            chunk, seq_at, q_in, g_in, keys, values, kv_recv[chunk], cosine, sine, query_grad,
-            parts[1:] if chunk else [],
+            chunk, seq_at, q_in, g_in, keys, values, kv_recv[chunk], cosine, sine,
+            parts[1:] + query_grads if chunk else [],
         )
+        query_grads.append(query_grad)
         made.append(rest)
-    grads, mines = [], []
+
+    grads = []
     after = [made[-1][0]]
     for keep_a, keep_b, send in made:
         mine = combine(seq_at, keep_a, keep_b, swap_seq(send), after)
-        mines.append(mine)
         below = flip(mine, ZLOW)
         grads.append([mine, flip(mine, XBIT), below, flip(below, XBIT)])
         after = [grads[-1][1]]
+
     (away,) = pack_normed(parts, [(0, 1)], [made[-1][0]])
     away_other = swap_seq(away)
-    same, cross = pack_normed(parts, [(2,), (3,)], [away_other])
-    same_other, cross_other = swap_seq(same), swap_seq(cross)
-    home = [same, flip(cross, CORE), same_other, flip(cross_other, CORE)]
-    recv_half = []
-    after = grads[1][1:3]
+    same, cross = pack_normed(parts, [(2,), (3,)], [made[-1][0]])
+    cross = flip(cross, CORE)
+
+    recv_half, recv_core = [], []
+    after, fence = [grads[1][2], cross], [grads[1][1]]
     for part in grads:
-        own, send = project_away(away, away_other, part, after)
-        total = add_round(own, flip(send, CORE))
+        own, *sends = project_away(away, away_other, part, after)
+        total = add_round(own, [flip(send, CORE) for send in sends], fence)
+        gathered = join_places(part, [total] + recv_half)
+        recv_core.append(flip(gathered, CORE))
         recv_half.append(flip(total, ZHIGH))
-        after = [recv_half[-1], same_other, cross_other]
-    both = [[one for one in part for one in (one, flip(one, CORE))] for part in grads]
-    keep = project_home(home, both, [total])
+        if part is grads[0]:
+            home = join_cores(same, cross, [away_other])
+            home_other = swap_seq(home)
+            after, fence = recv_core[:], [home_other]
+    keep, query_grad = project_home(seq_at, (home, home_other), grads, recv_core, query_grads, [total])
     key_weight_grad, value_weight_grad = finish(keep, recv_half)
     return (query_grad, key_weight_grad, value_weight_grad)
 

time: 83.9 us -> 79.2 us (0.944)
  waiting for transfers between devices: 38.4 us -> 33.8 us
    ppermute x5 -> x4, waiting for transfers between devices: 16.8 us -> 11 us  [swap_seq(): return lax.ppermute(array, 'seq', [(0, 1), (1, 0)])]
    ppermute x23 -> x22, starting transfers between devices: 16.9 us -> 18.5 us  [flip(): return lax.ppermute(array, 'dp', [(i, i ^ mask) for i in range(16)])]
    ppermute x23 -> x22, waiting for transfers between devices: 21.4 us -> 22.6 us  [flip(): return lax.ppermute(array, 'dp', [(i, i ^ mask) for i in range(16)])]
    ppermute x5 -> x4, starting transfers between devices: 7.71 us -> 6.65 us  [swap_seq(): return lax.ppermute(array, 'seq', [(0, 1), (1, 0)])]
    pallas_call x5 -> x8, Pallas kernels: 8.92 us -> 8.28 us  [the longest x2 4.74 us: attention(): pl.pallas_call(body, out_shape=[pltpu.VMEM((2, rows, wide), BF), pltpu.VM...]
  transfers between devices with their start and end apart: 30 -> 28, of which waited for: 16 -> 13; matrix products, arithmetic and copies ran while one was open for 0% -> 0% of each run, Pallas kernels for 11% -> 13%
where the time goes in v3:
time: 79.2 us; the launch traced here: 79 us
  waiting for transfers between devices  33.8 us (43%)
  starting transfers between devices  31.4 us (40%)
  Pallas kernels  13 us (16%)
  between operations  0.82 us (1%)
    ppermute x22, waiting for transfers between devices, flip(): return lax.ppermute(array, 'dp', [(i, i ^ mask) for i in range(16)])  22.6 us
    ppermute x22, starting transfers between devices, flip(): return lax.ppermute(array, 'dp', [(i, i ^ mask) for i in range(16)])  18.5 us
    ppermute x4, waiting for transfers between devices, swap_seq(): return lax.ppermute(array, 'seq', [(0, 1), (1, 0)])  11 us
    ppermute x4, starting transfers between devices, swap_seq(): return lax.ppermute(array, 'seq', [(0, 1), (1, 0)])  6.65 us
    ppermute x2, starting transfers between devices, cube_local(): kv_recv = [lax.ppermute(part, 'seq', [(0, 1)]) for part in kv]  6.18 us
    pallas_call x2, Pallas kernels, attention(): pl.pallas_call(body, out_shape=[pltpu.VMEM((2, rows, wide), BF), pltpu.VM...  4.74 us
    pallas_call x1, Pallas kernels, project_home(): pl.pallas_call(body, out_shape=[pltpu.VMEM((share, chunks * wide), F32),...  1.91 us
    pallas_call x1, Pallas kernels, stage(): pl.pallas_call(body, out_shape=[pltpu.VMEM(one.shape, one.dtype) for one...  1.61 us
  transfers between devices with their start and end apart: 28, of which 13 were waited for; matrix products, arithmetic and copies ran while one was open for 0% of the time, Pallas kernels for 13%

profile of v3, /device:TPU:0, one launch (start us, length us, event | category | flops | bytes accessed | tf_op | source)
XLA Modules:
  0.0 79.0 jit_solution(7219093876577113189)
XLA Ops:
  0.6 1.6 %prepare.1 = (bf16[128,1024]{1,0:T(8,128)(2,1)S(1)}, bf16[128,1024]{1,0:T(8,128)(2,1)S(1)}, bf16[128,1024]{1,0:T(8,128)(2,1)S(1)}, bf16[128,1024]{1,0:T(8,128)(2...) custom-call(s32[1]{0:T(128)} %bitcast.1.me_ref, ...), custom_call_target="tpu_custom_call" | custom-call | tf_op jit(solution)/shard_map/prepare/pallas_call | solution.py:208
  2.2 4.9 %collective-permute-start.4 = (bf16[128,1024]{1,0:T(8,128)(2,1)S(1)}, bf16[128,1024]{1,0:T(8,128)(2,1)S(1)}, u32[]{:S(2)}, u32[]{:S(2)}) collective-permute-start(bf16[128,1024]{1,0:T(8,128)(2,1)S(1)} %get-tuple-element.50), channel_id=1, source_target_pairs={{0,1},{2,3},{4,5},{6,7},{8,9},{10,11},{12,13},{14,15},{16,17},{18,... | collective-permute-start | bytes 786440 | tf_op jit(solution)/shard_map/ppermute | solution.py:586
  7.1 1.6 %collective-permute-start = (bf16[4,128,256]{2,1,0:T(8,128)(2,1)S(1)}, bf16[4,128,256]{2,1,0:T(8,128)(2,1)S(1)}, u32[]{:S(2)}, u32[]{:S(2)}) collective-permute-start(bf16[4,128,256]{2,1,0:T(8,128)(2,1)S(1)} %get-tuple-element.40), channel_id=1, source_target_pairs={{0,4},{2,6},{4,0},{6,2},{8,12},{10,14},{12,8},{14,10},{16,20},{18,... | collective-permute-start | bytes 786440 | tf_op jit(solution)/shard_map/ppermute | solution.py:136
  8.7 1.6 %collective-permute-start.1 = (bf16[4,128,256]{2,1,0:T(8,128)(2,1)S(1)}, bf16[4,128,256]{2,1,0:T(8,128)(2,1)S(1)}, u32[]{:S(2)}, u32[]{:S(2)}) collective-permute-start(bf16[4,128,256]{2,1,0:T(8,128)(2,1)S(1)} %get-tuple-element.41), channel_id=1, source_target_pairs={{0,8},{2,10},{4,12},{6,14},{8,0},{10,2},{12,4},{14,6},{16,24},{18,... | collective-permute-start | bytes 786440 | tf_op jit(solution)/shard_map/ppermute | solution.py:136
  10.3 0.4 collective-permute-start.2
  10.7 1.3 %collective-permute-start.3 = (bf16[128,1024]{1,0:T(8,128)(2,1)S(1)}, bf16[128,1024]{1,0:T(8,128)(2,1)S(1)}, u32[]{:S(2)}, u32[]{:S(2)}) collective-permute-start(bf16[128,1024]{1,0:T(8,128)(2,1)S(1)} %get-tuple-element.47), channel_id=1, source_target_pairs={{0,1},{2,3},{4,5},{6,7},{8,9},{10,11},{12,13},{14,15},{16,17},{18,... | collective-permute-start | bytes 786440 | tf_op jit(solution)/shard_map/ppermute | solution.py:586
  12.0 1.6 %stage.1 = (bf16[128,4096]{1,0:T(8,128)(2,1)S(1)}, bf16[128,4096]{1,0:T(8,128)(2,1)S(1)}, f32[256,128]{1,0:T(8,128)S(1)}, f32[256,128]{1,0:T(8,128)S(1)}) custom-call(bf16[128,4096]{1,0:T(8,128)(2,1)} %refs_0_.1, bf16[128,4096]{1,0:T(8,128)(2,1)} %refs_1_.1, f32[256,128]{1,0:T(8,128)} %constant.12.clone.refs_2_, f32[256,128]{1,0:T(8,128)} %constant.13.clone.refs_3_), custom_call_target="tpu_custom_call" | custom-call | tf_op jit(solution)/shard_map/stage/pallas_call | solution.py:232
  13.6 0.2 collective-permute-done.4.kv_ref
  13.8 2.4 %attention.2 = (bf16[2,128,1024]{2,1,0:T(8,128)(2,1)S(1)}, f32[128,512]{1,0:T(8,128)S(1)}, bf16[128,512]{1,0:T(8,128)(2,1)S(1)}, bf16[256,512]{1,0:T(8,128)(2,1)S(1)}) custom-call(s32[1]{0:T(128)} %bitcast.at_ref, bf16[128,4096]{1,0:T(8,128)(2,1)S(1)} %get-tuple-element.43.q_ref, bf16[128,4096]{1,0:T(8,128)(2,1)S(1)} %get-tuple-element.44.g_ref, ...), custom_call_target="tpu_custom_call" | custom-call | tf_op jit(solution)/shard_map/attention/pallas_call | solution.py:422
  16.2 3.5 %collective-permute-start.8 = (bf16[256,512]{1,0:T(8,128)(2,1)S(1)}, bf16[256,512]{1,0:T(8,128)(2,1)S(1)}, u32[]{:S(2)}, u32[]{:S(2)}) collective-permute-start(bf16[256,512]{1,0:T(8,128)(2,1)S(1)} %get-tuple-element.57), channel_id=1, source_target_pairs={{0,1},{1,0},{2,3},{3,2},{4,5},{5,4},{6,7},{7,6},{8,9},{9,8},{10,11... | collective-permute-start | bytes 786440 | tf_op jit(solution)/shard_map/ppermute | solution.py:140
  19.7 2.1 %collective-permute-done.2.rest_2_.refs_3_ = bf16[4,128,256]{2,1,0:T(8,128)(2,1)S(1)} collective-permute-done((bf16[4,128,256]{2,1,0:T(8,128)(2,1)S(1)}, bf16[4,128,256]{2,1,0:T(8,128)(2,1)S(1)}, u32[]{:S(2)}, u32[]{:S(2)}) %collective-permute-start.2) | collective-permute-done | bytes 262176 | tf_op jit(solution)/shard_map/ppermute | solution.py:136
  21.8 2.4 %attention.3 = (bf16[2,128,1024]{2,1,0:T(8,128)(2,1)S(1)}, f32[128,512]{1,0:T(8,128)S(1)}, bf16[128,512]{1,0:T(8,128)(2,1)S(1)}, bf16[256,512]{1,0:T(8,128)(2,1)S(1)}) custom-call(s32[1]{0:T(128)} %bitcast.at_ref, bf16[128,4096]{1,0:T(8,128)(2,1)S(1)} %get-tuple-element.43.q_ref, bf16[128,4096]{1,0:T(8,128)(2,1)S(1)} %get-tuple-element.44.g_ref, ...), custom_call_target="tpu_custom_call" | custom-call | tf_op jit(solution)/shard_map/attention/pallas_call | solution.py:422
  24.1 0.7 collective-permute-start.12
  24.9 1.6 %collective-permute-start.9 = (bf16[256,512]{1,0:T(8,128)(2,1)S(1)}, bf16[256,512]{1,0:T(8,128)(2,1)S(1)}, u32[]{:S(2)}, u32[]{:S(2)}) collective-permute-start(bf16[256,512]{1,0:T(8,128)(2,1)S(1)} %combine.2.refs_0_), channel_id=1, source_target_pairs={{0,4},{2,6},{4,0},{6,2},{8,12},{10,14},{12,8},{14,10},{16,20},{18,... | collective-permute-start | bytes 786440 | tf_op jit(solution)/shard_map/ppermute | solution.py:136
  26.4 1.9 %collective-permute-start.6 = (bf16[4,2,128,256]{3,2,1,0:T(8,128)(2,1)S(1)}, bf16[4,2,128,256]{3,2,1,0:T(8,128)(2,1)S(1)}, u32[]{:S(2)}, u32[]{:S(2)}) collective-permute-start(bf16[4,2,128,256]{3,2,1,0:T(8,128)(2,1)S(1)} %pack_normed.3.xa_ref), channel_id=1, source_target_pairs={{0,1},{1,0},{2,3},{3,2},{4,5},{5,4},{6,7},{7,6},{8,9},{9,8},{10,11... | collective-permute-start | bytes 1572872 | tf_op jit(solution)/shard_map/ppermute | solution.py:140
  28.4 1.6 %collective-permute-start.10 = (bf16[256,512]{1,0:T(8,128)(2,1)S(1)}, bf16[256,512]{1,0:T(8,128)(2,1)S(1)}, u32[]{:S(2)}, u32[]{:S(2)}) collective-permute-start(bf16[256,512]{1,0:T(8,128)(2,1)S(1)} %combine.2.refs_0_), channel_id=1, source_target_pairs={{0,8},{2,10},{4,12},{6,14},{8,0},{10,2},{12,4},{14,6},{16,24},{18,... | collective-permute-start | bytes 786440 | tf_op jit(solution)/shard_map/ppermute | solution.py:136
  30.0 0.1 collective-permute-start.5
  30.1 3.4 %collective-permute-done.12.recv_ref = bf16[256,512]{1,0:T(8,128)(2,1)S(1)} collective-permute-done((bf16[256,512]{1,0:T(8,128)(2,1)S(1)}, bf16[256,512]{1,0:T(8,128)(2,1)S(1)}, u32[]{:S(2)}, u32[]{:S(2)}) %collective-permute-start.12) | collective-permute-done | bytes 262176 | tf_op jit(solution)/shard_map/ppermute | solution.py:140
  33.4 0.2 combine.3.refs_0_.refs_4_
  33.7 1.7 %collective-permute-start.14 = (bf16[256,512]{1,0:T(8,128)(2,1)S(1)}, bf16[256,512]{1,0:T(8,128)(2,1)S(1)}, u32[]{:S(2)}, u32[]{:S(2)}) collective-permute-start(bf16[256,512]{1,0:T(8,128)(2,1)S(1)} %combine.3.refs_0_.refs_4_), channel_id=1, source_target_pairs={{0,8},{2,10},{4,12},{6,14},{8,0},{10,2},{12,4},{14,6},{16,24},{18,... | collective-permute-start | bytes 786440 | tf_op jit(solution)/shard_map/ppermute | solution.py:136
  35.4 1.0 %collective-permute-done.10.refs_2_ = bf16[256,512]{1,0:T(8,128)(2,1)S(1)} collective-permute-done((bf16[256,512]{1,0:T(8,128)(2,1)S(1)}, bf16[256,512]{1,0:T(8,128)(2,1)S(1)}, u32[]{:S(2)}, u32[]{:S(2)}) %collective-permute-start.10) | collective-permute-done | bytes 262176 | tf_op jit(solution)/shard_map/ppermute | solution.py:136
  36.3 0.5 collective-permute-start.11
  36.8 1.5 %collective-permute-start.13 = (bf16[256,512]{1,0:T(8,128)(2,1)S(1)}, bf16[256,512]{1,0:T(8,128)(2,1)S(1)}, u32[]{:S(2)}, u32[]{:S(2)}) collective-permute-start(bf16[256,512]{1,0:T(8,128)(2,1)S(1)} %combine.3.refs_0_.refs_4_), channel_id=1, source_target_pairs={{0,4},{2,6},{4,0},{6,2},{8,12},{10,14},{12,8},{14,10},{16,20},{18,... | collective-permute-start | bytes 786440 | tf_op jit(solution)/shard_map/ppermute | solution.py:136
  38.4 3.6 %collective-permute-done.6.refs_0_.xb_ref = bf16[4,2,128,256]{3,2,1,0:T(8,128)(2,1)S(1)} collective-permute-done((bf16[4,2,128,256]{3,2,1,0:T(8,128)(2,1)S(1)}, bf16[4,2,128,256]{3,2,1,0:T(8,128)(2,1)S(1)}, u32[]{:S(2)}, u32[]{:S(2)}) %collective-permute-start.6) | collective-permute-done | bytes 524320 | tf_op jit(solution)/shard_map/ppermute | solution.py:140
  42.0 0.7 collective-permute-done.11.refs_3_
  42.7 0.7 project_away.2
  43.5 0.5 collective-permute-start.17
  44.0 0.1 collective-permute-start.18
  44.1 0.4 collective-permute-start.19
  44.5 1.0 %collective-permute-done.13.refs_4_.refs_1_.refs_5_ = bf16[256,512]{1,0:T(8,128)(2,1)S(1)} collective-permute-done((bf16[256,512]{1,0:T(8,128)(2,1)S(1)}, bf16[256,512]{1,0:T(8,128)(2,1)S(1)}, u32[]{:S(2)}, u32[]{:S(2)}) %collective-permute-start.13) | collective-permute-done | bytes 262176 | tf_op jit(solution)/shard_map/ppermute | solution.py:136
  45.7 0.4 collective-permute-start.20
  46.1 0.6 collective-permute-start.7
  46.7 1.5 %collective-permute-start.15 = (bf16[256,512]{1,0:T(8,128)(2,1)S(1)}, bf16[256,512]{1,0:T(8,128)(2,1)S(1)}, u32[]{:S(2)}, u32[]{:S(2)}) collective-permute-start(bf16[256,512]{1,0:T(8,128)(2,1)S(1)} %collective-permute-done.14.refs_4_.refs_2_.refs_6_), channel_id=1, source_target_pairs={{0,4},{2,6},{4,0},{6,2},{8,12},{10,14},{12,8},{14,10},{16,20},{18,... | collective-permute-start | bytes 786440 | tf_op jit(solution)/shard_map/ppermute | solution.py:136
  48.2 2.6 %collective-permute-start.25 = (bf16[256,512]{1,0:T(8,128)(2,1)S(1)}, bf16[256,512]{1,0:T(8,128)(2,1)S(1)}, u32[]{:S(2)}, u32[]{:S(2)}) collective-permute-start(bf16[256,512]{1,0:T(8,128)(2,1)S(1)} %add_round.2.refs_4_), channel_id=1, source_target_pairs={{0,16},{2,18},{4,20},{6,22},{8,24},{10,26},{12,28},{14,30},{16,0},... | collective-permute-start | bytes 786440 | tf_op jit(solution)/shard_map/ppermute | solution.py:136
  50.8 4.0 %collective-permute-done.15.refs_3_.refs_7_ = bf16[256,512]{1,0:T(8,128)(2,1)S(1)} collective-permute-done((bf16[256,512]{1,0:T(8,128)(2,1)S(1)}, bf16[256,512]{1,0:T(8,128)(2,1)S(1)}, u32[]{:S(2)}, u32[]{:S(2)}) %collective-permute-start.15) | collective-permute-done | bytes 262176 | tf_op jit(solution)/shard_map/ppermute | solution.py:136
  54.8 0.7 project_away.3
  55.6 0.1 collective-permute-start.21
  55.6 0.5 collective-permute-start.22
  56.1 0.1 collective-permute-start.23
  56.2 4.0 %collective-permute-done.7.refs_4_.xb_ref = bf16[4,2,128,256]{3,2,1,0:T(8,128)(2,1)S(1)} collective-permute-done((bf16[4,2,128,256]{3,2,1,0:T(8,128)(2,1)S(1)}, bf16[4,2,128,256]{3,2,1,0:T(8,128)(2,1)S(1)}, u32[]{:S(2)}, u32[]{:S(2)}) %collective-permute-start.7) | collective-permute-done | bytes 524320 | tf_op jit(solution)/shard_map/ppermute | solution.py:140
  60.2 1.3 %collective-permute-done.24.refs_3_ = f32[64,512]{1,0:T(8,128)S(1)} collective-permute-done((f32[64,512]{1,0:T(8,128)S(1)}, f32[64,512]{1,0:T(8,128)S(1)}, u32[]{:S(2)}, u32[]{:S(2)}) %collective-permute-start.24) | collective-permute-done | bytes 131104 | tf_op jit(solution)/shard_map/ppermute | solution.py:136
  61.6 1.0 %collective-permute-done.25.refs_5_.refs_0_ = bf16[256,512]{1,0:T(8,128)(2,1)S(1)} collective-permute-done((bf16[256,512]{1,0:T(8,128)(2,1)S(1)}, bf16[256,512]{1,0:T(8,128)(2,1)S(1)}, u32[]{:S(2)}, u32[]{:S(2)}) %collective-permute-start.25) | collective-permute-done | bytes 262176 | tf_op jit(solution)/shard_map/ppermute | solution.py:136
  62.6 0.1 collective-permute-start.26
  62.7 1.8 %collective-permute-start.27 = (bf16[256,512]{1,0:T(8,128)(2,1)S(1)}, bf16[256,512]{1,0:T(8,128)(2,1)S(1)}, u32[]{:S(2)}, u32[]{:S(2)}) collective-permute-start(bf16[256,512]{1,0:T(8,128)(2,1)S(1)} %add_round.3.refs_4_.refs_12_), channel_id=1, source_target_pairs={{0,16},{2,18},{4,20},{6,22},{8,24},{10,26},{12,28},{14,30},{16,0},... | collective-permute-start | bytes 786440 | tf_op jit(solution)/shard_map/ppermute | solution.py:136
  64.5 0.9 %collective-permute-done.26.refs_9_ = bf16[1024,512]{1,0:T(8,128)(2,1)S(1)} collective-permute-done((bf16[1024,512]{1,0:T(8,128)(2,1)S(1)}, bf16[1024,512]{1,0:T(8,128)(2,1)S(1)}, u32[]{:S(2)}, u32[]{:S(2)}) %collective-permute-start.26) | collective-permute-done | bytes 1048608 | tf_op jit(solution)/shard_map/ppermute | solution.py:136
  65.4 1.9 %project_home.1 = (f32[256,1024]{1,0:T(8,128)S(1)}, bf16[128,4096]{1,0:T(8,128)(2,1)}) custom-call(s32[1]{0:T(128)} %bitcast.at_ref, bf16[4,2,128,256]{3,2,1,0:T(8,128)(2,1)S(1)} %join_cores.1.xa_ref, bf16[4,2,128,256]{3,2,1,0:T(8,128)(2,1)S(1)} %collective-permute-done.7.refs_4_.xb_ref, bf16[256,512]{1,0:T(8,128)(2,1)S(1)} %combine.2.refs_0_, ...), custom_call_target="tpu_custom_call" | custom-call | tf_op jit(solution)/shard_map/project_home/pallas_call | solution.py:539
  67.3 10.7 %collective-permute-done.27.refs_1_ = bf16[256,512]{1,0:T(8,128)(2,1)S(1)} collective-permute-done((bf16[256,512]{1,0:T(8,128)(2,1)S(1)}, bf16[256,512]{1,0:T(8,128)(2,1)S(1)}, u32[]{:S(2)}, u32[]{:S(2)}) %collective-permute-start.27) | collective-permute-done | bytes 262176 | tf_op jit(solution)/shard_map/ppermute | solution.py:136
  77.9 1.1 %finish.1 = (f32[256,512]{1,0:T(8,128)}, f32[256,512]{1,0:T(8,128)}) custom-call(f32[256,1024]{1,0:T(8,128)S(1)} %get-tuple-element.72.keep_ref, bf16[256,512]{1,0:T(8,128)(2,1)S(1)} %collective-permute-done.25.refs_5_.refs_0_, bf16[256,512]{1,0:T(8,128)(2,1)S(1)} %collective-permute-done.27.refs_1_), custom_call_target="tpu_custom_call" | custom-call | tf_op jit(solution)/shard_map/finish/pallas_call | solution.py:568
  (25 shorter events, 0.5 us)
Async XLA Ops:
  2.2 11.6 %collective-permute-start.4 = (bf16[128,1024]{1,0:T(8,128)(2,1)S(1)}, bf16[128,1024]{1,0:T(8,128)(2,1)S(1)}, u32[]{:S(2)}, u32[]{:S(2)}) collective-permute-start(bf16[128,1024]{1,0:T(8,128)(2,1)S(1)} %get-tuple-element.50), channel_id=1, source_target_pairs={{0,1},{2,3},{4,5},{6,7},{8,9},{10,11},{12,13},{14,15},{16,17},{18,... | collective-permute-start | bytes 786440 | tf_op jit(solution)/shard_map/ppermute | solution.py:586
  7.1 12.5 %collective-permute-start = (bf16[4,128,256]{2,1,0:T(8,128)(2,1)S(1)}, bf16[4,128,256]{2,1,0:T(8,128)(2,1)S(1)}, u32[]{:S(2)}, u32[]{:S(2)}) collective-permute-start(bf16[4,128,256]{2,1,0:T(8,128)(2,1)S(1)} %get-tuple-element.40), channel_id=1, source_target_pairs={{0,4},{2,6},{4,0},{6,2},{8,12},{10,14},{12,8},{14,10},{16,20},{18,... | collective-permute-start | bytes 786440 | tf_op jit(solution)/shard_map/ppermute | solution.py:136
  8.7 11.0 %collective-permute-start.1 = (bf16[4,128,256]{2,1,0:T(8,128)(2,1)S(1)}, bf16[4,128,256]{2,1,0:T(8,128)(2,1)S(1)}, u32[]{:S(2)}, u32[]{:S(2)}) collective-permute-start(bf16[4,128,256]{2,1,0:T(8,128)(2,1)S(1)} %get-tuple-element.41), channel_id=1, source_target_pairs={{0,8},{2,10},{4,12},{6,14},{8,0},{10,2},{12,4},{14,6},{16,24},{18,... | collective-permute-start | bytes 786440 | tf_op jit(solution)/shard_map/ppermute | solution.py:136
  10.3 11.5 %collective-permute-start.2 = (bf16[4,128,256]{2,1,0:T(8,128)(2,1)S(1)}, bf16[4,128,256]{2,1,0:T(8,128)(2,1)S(1)}, u32[]{:S(2)}, u32[]{:S(2)}) collective-permute-start(bf16[4,128,256]{2,1,0:T(8,128)(2,1)S(1)} %get-tuple-element.42), channel_id=1, source_target_pairs={{0,12},{2,14},{4,8},{6,10},{8,4},{10,6},{12,0},{14,2},{16,28},{18,... | collective-permute-start | bytes 786440 | tf_op jit(solution)/shard_map/ppermute | solution.py:136
  10.7 11.1 %collective-permute-start.3 = (bf16[128,1024]{1,0:T(8,128)(2,1)S(1)}, bf16[128,1024]{1,0:T(8,128)(2,1)S(1)}, u32[]{:S(2)}, u32[]{:S(2)}) collective-permute-start(bf16[128,1024]{1,0:T(8,128)(2,1)S(1)} %get-tuple-element.47), channel_id=1, source_target_pairs={{0,1},{2,3},{4,5},{6,7},{8,9},{10,11},{12,13},{14,15},{16,17},{18,... | collective-permute-start | bytes 786440 | tf_op jit(solution)/shard_map/ppermute | solution.py:586
  16.2 8.6 %collective-permute-start.8 = (bf16[256,512]{1,0:T(8,128)(2,1)S(1)}, bf16[256,512]{1,0:T(8,128)(2,1)S(1)}, u32[]{:S(2)}, u32[]{:S(2)}) collective-permute-start(bf16[256,512]{1,0:T(8,128)(2,1)S(1)} %get-tuple-element.57), channel_id=1, source_target_pairs={{0,1},{1,0},{2,3},{3,2},{4,5},{5,4},{6,7},{7,6},{8,9},{9,8},{10,11... | collective-permute-start | bytes 786440 | tf_op jit(solution)/shard_map/ppermute | solution.py:140
  24.1 9.3 %collective-permute-start.12 = (bf16[256,512]{1,0:T(8,128)(2,1)S(1)}, bf16[256,512]{1,0:T(8,128)(2,1)S(1)}, u32[]{:S(2)}, u32[]{:S(2)}) collective-permute-start(bf16[256,512]{1,0:T(8,128)(2,1)S(1)} %get-tuple-element.59), channel_id=1, source_target_pairs={{0,1},{1,0},{2,3},{3,2},{4,5},{5,4},{6,7},{7,6},{8,9},{9,8},{10,11... | collective-permute-start | bytes 786440 | tf_op jit(solution)/shard_map/ppermute | solution.py:140
  24.9 8.6 %collective-permute-start.9 = (bf16[256,512]{1,0:T(8,128)(2,1)S(1)}, bf16[256,512]{1,0:T(8,128)(2,1)S(1)}, u32[]{:S(2)}, u32[]{:S(2)}) collective-permute-start(bf16[256,512]{1,0:T(8,128)(2,1)S(1)} %combine.2.refs_0_), channel_id=1, source_target_pairs={{0,4},{2,6},{4,0},{6,2},{8,12},{10,14},{12,8},{14,10},{16,20},{18,... | collective-permute-start | bytes 786440 | tf_op jit(solution)/shard_map/ppermute | solution.py:136
  26.4 15.6 %collective-permute-start.6 = (bf16[4,2,128,256]{3,2,1,0:T(8,128)(2,1)S(1)}, bf16[4,2,128,256]{3,2,1,0:T(8,128)(2,1)S(1)}, u32[]{:S(2)}, u32[]{:S(2)}) collective-permute-start(bf16[4,2,128,256]{3,2,1,0:T(8,128)(2,1)S(1)} %pack_normed.3.xa_ref), channel_id=1, source_target_pairs={{0,1},{1,0},{2,3},{3,2},{4,5},{5,4},{6,7},{7,6},{8,9},{9,8},{10,11... | collective-permute-start | bytes 1572872 | tf_op jit(solution)/shard_map/ppermute | solution.py:140
  28.4 8.0 %collective-permute-start.10 = (bf16[256,512]{1,0:T(8,128)(2,1)S(1)}, bf16[256,512]{1,0:T(8,128)(2,1)S(1)}, u32[]{:S(2)}, u32[]{:S(2)}) collective-permute-start(bf16[256,512]{1,0:T(8,128)(2,1)S(1)} %combine.2.refs_0_), channel_id=1, source_target_pairs={{0,8},{2,10},{4,12},{6,14},{8,0},{10,2},{12,4},{14,6},{16,24},{18,... | collective-permute-start | bytes 786440 | tf_op jit(solution)/shard_map/ppermute | solution.py:136
  30.0 8.4 %collective-permute-start.5 = (bf16[4,128,256]{2,1,0:T(8,128)(2,1)S(1)}, bf16[4,128,256]{2,1,0:T(8,128)(2,1)S(1)}, u32[]{:S(2)}, u32[]{:S(2)}) collective-permute-start(bf16[4,128,256]{2,1,0:T(8,128)(2,1)S(1)} %get-tuple-element.54), channel_id=1, source_target_pairs={{0,2},{2,0},{4,6},{6,4},{8,10},{10,8},{12,14},{14,12},{16,18},{18,... | collective-permute-start | bytes 786440 | tf_op jit(solution)/shard_map/ppermute | solution.py:136
  33.7 8.3 %collective-permute-start.14 = (bf16[256,512]{1,0:T(8,128)(2,1)S(1)}, bf16[256,512]{1,0:T(8,128)(2,1)S(1)}, u32[]{:S(2)}, u32[]{:S(2)}) collective-permute-start(bf16[256,512]{1,0:T(8,128)(2,1)S(1)} %combine.3.refs_0_.refs_4_), channel_id=1, source_target_pairs={{0,8},{2,10},{4,12},{6,14},{8,0},{10,2},{12,4},{14,6},{16,24},{18,... | collective-permute-start | bytes 786440 | tf_op jit(solution)/shard_map/ppermute | solution.py:136
  36.3 6.4 %collective-permute-start.11 = (bf16[256,512]{1,0:T(8,128)(2,1)S(1)}, bf16[256,512]{1,0:T(8,128)(2,1)S(1)}, u32[]{:S(2)}, u32[]{:S(2)}) collective-permute-start(bf16[256,512]{1,0:T(8,128)(2,1)S(1)} %collective-permute-done.10.refs_2_), channel_id=1, source_target_pairs={{0,4},{2,6},{4,0},{6,2},{8,12},{10,14},{12,8},{14,10},{16,20},{18,... | collective-permute-start | bytes 786440 | tf_op jit(solution)/shard_map/ppermute | solution.py:136
  36.8 8.7 %collective-permute-start.13 = (bf16[256,512]{1,0:T(8,128)(2,1)S(1)}, bf16[256,512]{1,0:T(8,128)(2,1)S(1)}, u32[]{:S(2)}, u32[]{:S(2)}) collective-permute-start(bf16[256,512]{1,0:T(8,128)(2,1)S(1)} %combine.3.refs_0_.refs_4_), channel_id=1, source_target_pairs={{0,4},{2,6},{4,0},{6,2},{8,12},{10,14},{12,8},{14,10},{16,20},{18,... | collective-permute-start | bytes 786440 | tf_op jit(solution)/shard_map/ppermute | solution.py:136
  43.4 2.1 %collective-permute-start.16 = (f32[64,512]{1,0:T(8,128)S(1)}, f32[64,512]{1,0:T(8,128)S(1)}, u32[]{:S(2)}, u32[]{:S(2)}) collective-permute-start(f32[64,512]{1,0:T(8,128)S(1)} %get-tuple-element.61), channel_id=1, source_target_pairs={{0,2},{2,0},{4,6},{6,4},{8,10},{10,8},{12,14},{14,12},{16,18},{18,... | collective-permute-start | bytes 393224 | tf_op jit(solution)/shard_map/ppermute | solution.py:136
  43.5 2.0 %collective-permute-start.17 = (f32[64,512]{1,0:T(8,128)S(1)}, f32[64,512]{1,0:T(8,128)S(1)}, u32[]{:S(2)}, u32[]{:S(2)}) collective-permute-start(f32[64,512]{1,0:T(8,128)S(1)} %get-tuple-element.62), channel_id=1, source_target_pairs={{0,2},{2,0},{4,6},{6,4},{8,10},{10,8},{12,14},{14,12},{16,18},{18,... | collective-permute-start | bytes 393224 | tf_op jit(solution)/shard_map/ppermute | solution.py:136
  44.0 1.5 %collective-permute-start.18 = (f32[64,512]{1,0:T(8,128)S(1)}, f32[64,512]{1,0:T(8,128)S(1)}, u32[]{:S(2)}, u32[]{:S(2)}) collective-permute-start(f32[64,512]{1,0:T(8,128)S(1)} %get-tuple-element.63), channel_id=1, source_target_pairs={{0,2},{2,0},{4,6},{6,4},{8,10},{10,8},{12,14},{14,12},{16,18},{18,... | collective-permute-start | bytes 393224 | tf_op jit(solution)/shard_map/ppermute | solution.py:136
  44.1 1.5 %collective-permute-start.19 = (f32[64,512]{1,0:T(8,128)S(1)}, f32[64,512]{1,0:T(8,128)S(1)}, u32[]{:S(2)}, u32[]{:S(2)}) collective-permute-start(f32[64,512]{1,0:T(8,128)S(1)} %get-tuple-element.64), channel_id=1, source_target_pairs={{0,2},{2,0},{4,6},{6,4},{8,10},{10,8},{12,14},{14,12},{16,18},{18,... | collective-permute-start | bytes 393224 | tf_op jit(solution)/shard_map/ppermute | solution.py:136
  45.7 9.1 %collective-permute-start.20 = (bf16[1024,512]{1,0:T(8,128)(2,1)S(1)}, bf16[1024,512]{1,0:T(8,128)(2,1)S(1)}, u32[]{:S(2)}, u32[]{:S(2)}) collective-permute-start(bf16[1024,512]{1,0:T(8,128)(2,1)S(1)} %join_places.2), channel_id=1, source_target_pairs={{0,2},{2,0},{4,6},{6,4},{8,10},{10,8},{12,14},{14,12},{16,18},{18,... | collective-permute-start | bytes 3145736 | tf_op jit(solution)/shard_map/ppermute | solution.py:136
  46.1 14.1 %collective-permute-start.7 = (bf16[4,2,128,256]{3,2,1,0:T(8,128)(2,1)S(1)}, bf16[4,2,128,256]{3,2,1,0:T(8,128)(2,1)S(1)}, u32[]{:S(2)}, u32[]{:S(2)}) collective-permute-start(bf16[4,2,128,256]{3,2,1,0:T(8,128)(2,1)S(1)} %join_cores.1.xa_ref), channel_id=1, source_target_pairs={{0,1},{1,0},{2,3},{3,2},{4,5},{5,4},{6,7},{7,6},{8,9},{9,8},{10,11... | collective-permute-start | bytes 1572872 | tf_op jit(solution)/shard_map/ppermute | solution.py:140
  46.7 8.1 %collective-permute-start.15 = (bf16[256,512]{1,0:T(8,128)(2,1)S(1)}, bf16[256,512]{1,0:T(8,128)(2,1)S(1)}, u32[]{:S(2)}, u32[]{:S(2)}) collective-permute-start(bf16[256,512]{1,0:T(8,128)(2,1)S(1)} %collective-permute-done.14.refs_4_.refs_2_.refs_6_), channel_id=1, source_target_pairs={{0,4},{2,6},{4,0},{6,2},{8,12},{10,14},{12,8},{14,10},{16,20},{18,... | collective-permute-start | bytes 786440 | tf_op jit(solution)/shard_map/ppermute | solution.py:136
  48.2 14.4 %collective-permute-start.25 = (bf16[256,512]{1,0:T(8,128)(2,1)S(1)}, bf16[256,512]{1,0:T(8,128)(2,1)S(1)}, u32[]{:S(2)}, u32[]{:S(2)}) collective-permute-start(bf16[256,512]{1,0:T(8,128)(2,1)S(1)} %add_round.2.refs_4_), channel_id=1, source_target_pairs={{0,16},{2,18},{4,20},{6,22},{8,24},{10,26},{12,28},{14,30},{16,0},... | collective-permute-start | bytes 786440 | tf_op jit(solution)/shard_map/ppermute | solution.py:136
  55.6 4.6 %collective-permute-start.21 = (f32[64,512]{1,0:T(8,128)S(1)}, f32[64,512]{1,0:T(8,128)S(1)}, u32[]{:S(2)}, u32[]{:S(2)}) collective-permute-start(f32[64,512]{1,0:T(8,128)S(1)} %get-tuple-element.66), channel_id=1, source_target_pairs={{0,2},{2,0},{4,6},{6,4},{8,10},{10,8},{12,14},{14,12},{16,18},{18,... | collective-permute-start | bytes 393224 | tf_op jit(solution)/shard_map/ppermute | solution.py:136
  55.6 4.6 %collective-permute-start.22 = (f32[64,512]{1,0:T(8,128)S(1)}, f32[64,512]{1,0:T(8,128)S(1)}, u32[]{:S(2)}, u32[]{:S(2)}) collective-permute-start(f32[64,512]{1,0:T(8,128)S(1)} %get-tuple-element.67), channel_id=1, source_target_pairs={{0,2},{2,0},{4,6},{6,4},{8,10},{10,8},{12,14},{14,12},{16,18},{18,... | collective-permute-start | bytes 393224 | tf_op jit(solution)/shard_map/ppermute | solution.py:136
  56.1 4.1 %collective-permute-start.23 = (f32[64,512]{1,0:T(8,128)S(1)}, f32[64,512]{1,0:T(8,128)S(1)}, u32[]{:S(2)}, u32[]{:S(2)}) collective-permute-start(f32[64,512]{1,0:T(8,128)S(1)} %get-tuple-element.68), channel_id=1, source_target_pairs={{0,2},{2,0},{4,6},{6,4},{8,10},{10,8},{12,14},{14,12},{16,18},{18,... | collective-permute-start | bytes 393224 | tf_op jit(solution)/shard_map/ppermute | solution.py:136
  60.2 1.3 %collective-permute-start.24 = (f32[64,512]{1,0:T(8,128)S(1)}, f32[64,512]{1,0:T(8,128)S(1)}, u32[]{:S(2)}, u32[]{:S(2)}) collective-permute-start(f32[64,512]{1,0:T(8,128)S(1)} %get-tuple-element.69), channel_id=1, source_target_pairs={{0,2},{2,0},{4,6},{6,4},{8,10},{10,8},{12,14},{14,12},{16,18},{18,... | collective-permute-start | bytes 393224 | tf_op jit(solution)/shard_map/ppermute | solution.py:136
  62.6 2.7 %collective-permute-start.26 = (bf16[1024,512]{1,0:T(8,128)(2,1)S(1)}, bf16[1024,512]{1,0:T(8,128)(2,1)S(1)}, u32[]{:S(2)}, u32[]{:S(2)}) collective-permute-start(bf16[1024,512]{1,0:T(8,128)(2,1)S(1)} %join_places.3), channel_id=1, source_target_pairs={{0,2},{2,0},{4,6},{6,4},{8,10},{10,8},{12,14},{14,12},{16,18},{18,... | collective-permute-start | bytes 3145736 | tf_op jit(solution)/shard_map/ppermute | solution.py:136
  62.7 15.2 %collective-permute-start.27 = (bf16[256,512]{1,0:T(8,128)(2,1)S(1)}, bf16[256,512]{1,0:T(8,128)(2,1)S(1)}, u32[]{:S(2)}, u32[]{:S(2)}) collective-permute-start(bf16[256,512]{1,0:T(8,128)(2,1)S(1)} %add_round.3.refs_4_.refs_12_), channel_id=1, source_target_pairs={{0,16},{2,18},{4,20},{6,22},{8,24},{10,26},{12,28},{14,30},{16,0},... | collective-permute-start | bytes 786440 | tf_op jit(solution)/shard_map/ppermute | solution.py:136

commit v4 on v3

--- a/solution.py
+++ b/solution.py
@@ -176,21 +176,16 @@
         copy.wait()
 
 
-def prepare(keys, values, normed, me):
+def prepare_kv(keys, values):
     rows, kv_width = keys.shape
-    width = normed.shape[1]
-    share = width // 16
     wide = kv_width // (2 * NC)
 
-
-    def body(me_ref, k_hbm, v_hbm, x_hbm, k_ref, v_ref, *rest):
-        kv, parts, (x_ref, sem) = rest[:NC], rest[NC : NC + 4], rest[NC + 4 :]
-        mine = me_ref[0]
+    def body(k_hbm, v_hbm, k_ref, v_ref, *rest):
+        kv, sem = rest[:NC], rest[NC]
         run_copies(
             [
                 pltpu.make_async_copy(k_hbm, k_ref, sem.at[0]),
                 pltpu.make_async_copy(v_hbm, v_ref, sem.at[1]),
-                pltpu.make_async_copy(x_hbm, x_ref, sem.at[2]),
             ]
         )
         for chunk, out in enumerate(kv):
@@ -200,6 +195,25 @@
                     at = (number * 2 + half) * wide
                     out[:, at : at + wide] = ref[:, low : low + wide]
 
+    return pl.pallas_call(
+        body,
+        out_shape=[pltpu.VMEM((rows, kv_width), BF)] * 2 + [pltpu.VMEM((rows, 4 * wide), BF)] * NC,
+        in_specs=[hbm()] * 2,
+        out_specs=[vmem()] * (2 + NC),
+        scratch_shapes=[pltpu.SemaphoreType.DMA((2,))],
+        compiler_params=params(),
+        name="prepare_kv",
+    )(in_hbm(keys), in_hbm(values))
+
+
+def prepare_normed(normed, me, after):
+    rows, width = normed.shape
+    share = width // 16
+
+    def body(me_ref, x_hbm, after_ref, *rest):
+        parts, (x_ref, sem) = rest[:4], rest[4:]
+        mine = me_ref[0]
+        run_copies([pltpu.make_async_copy(x_hbm, x_ref, sem)])
         for place, part in enumerate(parts):
             for number, mask in enumerate((ZHIGH, ZHIGH | CORE, 0, CORE)):
                 low = pl.multiple_of((mine ^ (mask | (place * 2))) * share, share)
@@ -207,15 +221,13 @@
 
     return pl.pallas_call(
         body,
-        out_shape=[pltpu.VMEM((rows, kv_width), BF)] * 2
-        + [pltpu.VMEM((rows, 4 * wide), BF)] * NC
-        + [pltpu.VMEM((4, rows, share), BF)] * 4,
-        in_specs=[smem()] + [hbm()] * 3,
-        out_specs=[vmem()] * (6 + NC),
-        scratch_shapes=[pltpu.VMEM((rows, width), BF), pltpu.SemaphoreType.DMA((3,))],
-        compiler_params=params(),
-        name="prepare",
-    )(me, in_hbm(keys), in_hbm(values), in_hbm(normed))
+        out_shape=[pltpu.VMEM((4, rows, share), BF)] * 4,
+        in_specs=[smem(), hbm(), hbm()],
+        out_specs=[vmem()] * 4,
+        scratch_shapes=[pltpu.VMEM((rows, width), BF), pltpu.SemaphoreType.DMA],
+        compiler_params=params(),
+        name="prepare_normed",
+    )(me, in_hbm(normed), after)
 
 
 def stage(arrays):
@@ -581,8 +593,8 @@
     rows = queries.shape[0]
     cosine, sine = (jnp.asarray(table) for table in rotary_tables(2 * rows))
 
-    keys, values, *rest = prepare(keys, values, normed, me)
-    kv, parts = rest[:NC], rest[NC:]
+    keys, values, *kv = prepare_kv(keys, values)
+    parts = prepare_normed(normed, me, kv[0])
     kv_recv = [lax.ppermute(part, "seq", [(0, 1)]) for part in kv]
     masks = (0, XBIT, ZLOW, XBIT | ZLOW)
     parts = [flip(part, mask) if mask else part for part, mask in zip(parts, masks)]
@@ -592,7 +604,7 @@
     for chunk in range(NC):
         query_grad, *rest = attention(
             chunk, seq_at, q_in, g_in, keys, values, kv_recv[chunk], cosine, sine,
-            parts[1:] + query_grads if chunk else [],
+            [parts[1], parts[3]] + query_grads if chunk else [],
         )
         query_grads.append(query_grad)
         made.append(rest)
@@ -603,7 +615,7 @@
         mine = combine(seq_at, keep_a, keep_b, swap_seq(send), after)
         below = flip(mine, ZLOW)
         grads.append([mine, flip(mine, XBIT), below, flip(below, XBIT)])
-        after = [grads[-1][1]]
+        after = grads[-1][1:3]
 
     (away,) = pack_normed(parts, [(0, 1)], [made[-1][0]])
     away_other = swap_seq(away)

time: 79.2 us -> 79 us (level)
  waiting for transfers between devices: 33.8 us -> 32.7 us
  Pallas kernels: 13 us -> 13.9 us
    ppermute x22, waiting for transfers between devices: 22.6 us -> 20.5 us  [flip(): return lax.ppermute(array, 'dp', [(i, i ^ mask) for i in range(16)])]
    ppermute x22, starting transfers between devices: 18.5 us -> 20.2 us  [flip(): return lax.ppermute(array, 'dp', [(i, i ^ mask) for i in range(16)])]
    ppermute x4, starting transfers between devices: 6.65 us -> 5.01 us  [swap_seq(): return lax.ppermute(array, 'seq', [(0, 1), (1, 0)])]
    ppermute x4, waiting for transfers between devices: 11 us -> 12.2 us  [swap_seq(): return lax.ppermute(array, 'seq', [(0, 1), (1, 0)])]
    pallas_call x1 -> x2, Pallas kernels: 1.59 us -> 2.45 us  [the longest x1 1.37 us: prepare_normed(): pl.pallas_call(body, out_shape=[pltpu.VMEM((4, rows, share), BF)] * 4, in...]
  transfers between devices with their start and end apart: 28 -> 28, of which waited for: 13 -> 11; matrix products, arithmetic and copies ran while one was open for 0% -> 0% of each run, Pallas kernels for 13% -> 15%
where the time goes in v4:
time: 79 us; the launch traced here: 78.8 us
  waiting for transfers between devices  32.7 us (41%)
  starting transfers between devices  31.4 us (40%)
  Pallas kernels  13.9 us (18%)
  between operations  0.84 us (1%)
    ppermute x22, waiting for transfers between devices, flip(): return lax.ppermute(array, 'dp', [(i, i ^ mask) for i in range(16)])  20.5 us
    ppermute x22, starting transfers between devices, flip(): return lax.ppermute(array, 'dp', [(i, i ^ mask) for i in range(16)])  20.2 us
    ppermute x4, waiting for transfers between devices, swap_seq(): return lax.ppermute(array, 'seq', [(0, 1), (1, 0)])  12.2 us
    ppermute x2, starting transfers between devices, cube_local(): kv_recv = [lax.ppermute(part, 'seq', [(0, 1)]) for part in kv]  6.18 us
    ppermute x4, starting transfers between devices, swap_seq(): return lax.ppermute(array, 'seq', [(0, 1), (1, 0)])  5.01 us
    pallas_call x2, Pallas kernels, attention(): pl.pallas_call(body, out_shape=[pltpu.VMEM((2, rows, wide), BF), pltpu.VM...  4.76 us
    pallas_call x1, Pallas kernels, project_home(): pl.pallas_call(body, out_shape=[pltpu.VMEM((share, chunks * wide), F32),...  1.91 us
    pallas_call x1, Pallas kernels, stage(): pl.pallas_call(body, out_shape=[pltpu.VMEM(one.shape, one.dtype) for one...  1.61 us
  transfers between devices with their start and end apart: 28, of which 11 were waited for; matrix products, arithmetic and copies ran while one was open for 0% of the time, Pallas kernels for 15%

profile of v4, /device:TPU:0, one launch (start us, length us, event | category | flops | bytes accessed | tf_op | source)
XLA Modules:
  0.0 78.8 jit_solution(17568630191162148301)
XLA Ops:
  0.6 1.1 %prepare_kv.1 = (bf16[128,1024]{1,0:T(8,128)(2,1)S(1)}, bf16[128,1024]{1,0:T(8,128)(2,1)S(1)}, bf16[128,1024]{1,0:T(8,128)(2,1)S(1)}, bf16[128,1024]{1,0:T(8,128)(2,1)S(1)}) custom-call(bf16[128,1024]{1,0:T(8,128)(2,1)} %k_hbm.1, bf16[128,1024]{1,0:T(8,128)(2,1)} %v_hbm.1), custom_call_target="tpu_custom_call" | custom-call | tf_op jit(solution)/shard_map/prepare_kv/pallas_call | solution.py:198
  1.7 4.9 %collective-permute-start.4 = (bf16[128,1024]{1,0:T(8,128)(2,1)S(1)}, bf16[128,1024]{1,0:T(8,128)(2,1)S(1)}, u32[]{:S(2)}, u32[]{:S(2)}) collective-permute-start(bf16[128,1024]{1,0:T(8,128)(2,1)S(1)} %get-tuple-element.39.after_ref), channel_id=1, source_target_pairs={{0,1},{2,3},{4,5},{6,7},{8,9},{10,11},{12,13},{14,15},{16,17},{18,... | collective-permute-start | bytes 786440 | tf_op jit(solution)/shard_map/ppermute | solution.py:598
  6.6 1.4 %prepare_normed.1 = (bf16[4,128,256]{2,1,0:T(8,128)(2,1)S(1)}, bf16[4,128,256]{2,1,0:T(8,128)(2,1)S(1)}, bf16[4,128,256]{2,1,0:T(8,128)(2,1)S(1)}, bf16[4,128,256]{2,1,0:T(8,128)(2,1)S(1)}) custom-call(s32[1]{0:T(128)} %bitcast.1.me_ref, bf16[128,4096]{1,0:T(8,128)(2,1)} %x_hbm.1, bf16[128,1024]{1,0:T(8,128)(2,1)S(1)} %get-tuple-element.39.after_ref), custom_call_target="tpu_custom_call" | custom-call | tf_op jit(solution)/shard_map/prepare_normed/pallas_call | solution.py:222
  8.0 1.6 %collective-permute-start = (bf16[4,128,256]{2,1,0:T(8,128)(2,1)S(1)}, bf16[4,128,256]{2,1,0:T(8,128)(2,1)S(1)}, u32[]{:S(2)}, u32[]{:S(2)}) collective-permute-start(bf16[4,128,256]{2,1,0:T(8,128)(2,1)S(1)} %get-tuple-element.41), channel_id=1, source_target_pairs={{0,4},{2,6},{4,0},{6,2},{8,12},{10,14},{12,8},{14,10},{16,20},{18,... | collective-permute-start | bytes 786440 | tf_op jit(solution)/shard_map/ppermute | solution.py:136
  9.6 1.5 %collective-permute-start.2 = (bf16[4,128,256]{2,1,0:T(8,128)(2,1)S(1)}, bf16[4,128,256]{2,1,0:T(8,128)(2,1)S(1)}, u32[]{:S(2)}, u32[]{:S(2)}) collective-permute-start(bf16[4,128,256]{2,1,0:T(8,128)(2,1)S(1)} %get-tuple-element.43), channel_id=1, source_target_pairs={{0,12},{2,14},{4,8},{6,10},{8,4},{10,6},{12,0},{14,2},{16,28},{18,... | collective-permute-start | bytes 786440 | tf_op jit(solution)/shard_map/ppermute | solution.py:136
  11.1 1.3 %collective-permute-start.3 = (bf16[128,1024]{1,0:T(8,128)(2,1)S(1)}, bf16[128,1024]{1,0:T(8,128)(2,1)S(1)}, u32[]{:S(2)}, u32[]{:S(2)}) collective-permute-start(bf16[128,1024]{1,0:T(8,128)(2,1)S(1)} %get-tuple-element.48), channel_id=1, source_target_pairs={{0,1},{2,3},{4,5},{6,7},{8,9},{10,11},{12,13},{14,15},{16,17},{18,... | collective-permute-start | bytes 786440 | tf_op jit(solution)/shard_map/ppermute | solution.py:598
  12.4 1.6 %stage.1 = (bf16[128,4096]{1,0:T(8,128)(2,1)S(1)}, bf16[128,4096]{1,0:T(8,128)(2,1)S(1)}, f32[256,128]{1,0:T(8,128)S(1)}, f32[256,128]{1,0:T(8,128)S(1)}) custom-call(bf16[128,4096]{1,0:T(8,128)(2,1)} %refs_0_.1, bf16[128,4096]{1,0:T(8,128)(2,1)} %refs_1_.1, f32[256,128]{1,0:T(8,128)} %constant.12.clone.refs_2_, f32[256,128]{1,0:T(8,128)} %constant.13.clone.refs_3_), custom_call_target="tpu_custom_call" | custom-call | tf_op jit(solution)/shard_map/stage/pallas_call | solution.py:244
  14.0 2.4 %attention.2 = (bf16[2,128,1024]{2,1,0:T(8,128)(2,1)S(1)}, f32[128,512]{1,0:T(8,128)S(1)}, bf16[128,512]{1,0:T(8,128)(2,1)S(1)}, bf16[256,512]{1,0:T(8,128)(2,1)S(1)}) custom-call(s32[1]{0:T(128)} %bitcast.at_ref, bf16[128,4096]{1,0:T(8,128)(2,1)S(1)} %get-tuple-element.44.q_ref, bf16[128,4096]{1,0:T(8,128)(2,1)S(1)} %get-tuple-element.45.g_ref, ...), custom_call_target="tpu_custom_call" | custom-call | tf_op jit(solution)/shard_map/attention/pallas_call | solution.py:434
  16.4 1.9 %collective-permute-start.8 = (bf16[256,512]{1,0:T(8,128)(2,1)S(1)}, bf16[256,512]{1,0:T(8,128)(2,1)S(1)}, u32[]{:S(2)}, u32[]{:S(2)}) collective-permute-start(bf16[256,512]{1,0:T(8,128)(2,1)S(1)} %get-tuple-element.57), channel_id=1, source_target_pairs={{0,1},{1,0},{2,3},{3,2},{4,5},{5,4},{6,7},{7,6},{8,9},{9,8},{10,11... | collective-permute-start | bytes 786440 | tf_op jit(solution)/shard_map/ppermute | solution.py:140
  18.3 2.4 %collective-permute-start.1 = (bf16[4,128,256]{2,1,0:T(8,128)(2,1)S(1)}, bf16[4,128,256]{2,1,0:T(8,128)(2,1)S(1)}, u32[]{:S(2)}, u32[]{:S(2)}) collective-permute-start(bf16[4,128,256]{2,1,0:T(8,128)(2,1)S(1)} %get-tuple-element.42), channel_id=1, source_target_pairs={{0,8},{2,10},{4,12},{6,14},{8,0},{10,2},{12,4},{14,6},{16,24},{18,... | collective-permute-start | bytes 786440 | tf_op jit(solution)/shard_map/ppermute | solution.py:136
  20.7 0.7 collective-permute-done.rest_0_.refs_1_
  21.5 2.4 %attention.3 = (bf16[2,128,1024]{2,1,0:T(8,128)(2,1)S(1)}, f32[128,512]{1,0:T(8,128)S(1)}, bf16[128,512]{1,0:T(8,128)(2,1)S(1)}, bf16[256,512]{1,0:T(8,128)(2,1)S(1)}) custom-call(s32[1]{0:T(128)} %bitcast.at_ref, bf16[128,4096]{1,0:T(8,128)(2,1)S(1)} %get-tuple-element.44.q_ref, bf16[128,4096]{1,0:T(8,128)(2,1)S(1)} %get-tuple-element.45.g_ref, ...), custom_call_target="tpu_custom_call" | custom-call | tf_op jit(solution)/shard_map/attention/pallas_call | solution.py:434
  23.8 0.7 collective-permute-start.12
  24.5 1.6 %collective-permute-start.10 = (bf16[256,512]{1,0:T(8,128)(2,1)S(1)}, bf16[256,512]{1,0:T(8,128)(2,1)S(1)}, u32[]{:S(2)}, u32[]{:S(2)}) collective-permute-start(bf16[256,512]{1,0:T(8,128)(2,1)S(1)} %combine.2.refs_0_), channel_id=1, source_target_pairs={{0,8},{2,10},{4,12},{6,14},{8,0},{10,2},{12,4},{14,6},{16,24},{18,... | collective-permute-start | bytes 786440 | tf_op jit(solution)/shard_map/ppermute | solution.py:136
  26.2 1.5 %collective-permute-start.9 = (bf16[256,512]{1,0:T(8,128)(2,1)S(1)}, bf16[256,512]{1,0:T(8,128)(2,1)S(1)}, u32[]{:S(2)}, u32[]{:S(2)}) collective-permute-start(bf16[256,512]{1,0:T(8,128)(2,1)S(1)} %combine.2.refs_0_), channel_id=1, source_target_pairs={{0,4},{2,6},{4,0},{6,2},{8,12},{10,14},{12,8},{14,10},{16,20},{18,... | collective-permute-start | bytes 786440 | tf_op jit(solution)/shard_map/ppermute | solution.py:136
  27.7 1.5 %collective-permute-start.6 = (bf16[4,2,128,256]{3,2,1,0:T(8,128)(2,1)S(1)}, bf16[4,2,128,256]{3,2,1,0:T(8,128)(2,1)S(1)}, u32[]{:S(2)}, u32[]{:S(2)}) collective-permute-start(bf16[4,2,128,256]{3,2,1,0:T(8,128)(2,1)S(1)} %pack_normed.3.xa_ref), channel_id=1, source_target_pairs={{0,1},{1,0},{2,3},{3,2},{4,5},{5,4},{6,7},{7,6},{8,9},{9,8},{10,11... | collective-permute-start | bytes 1572872 | tf_op jit(solution)/shard_map/ppermute | solution.py:140
  29.3 0.1 collective-permute-start.5
  29.3 3.7 %collective-permute-done.12.recv_ref = bf16[256,512]{1,0:T(8,128)(2,1)S(1)} collective-permute-done((bf16[256,512]{1,0:T(8,128)(2,1)S(1)}, bf16[256,512]{1,0:T(8,128)(2,1)S(1)}, u32[]{:S(2)}, u32[]{:S(2)}) %collective-permute-start.12) | collective-permute-done | bytes 262176 | tf_op jit(solution)/shard_map/ppermute | solution.py:140
  33.0 0.2 combine.3.refs_0_.refs_4_
  33.2 1.8 %collective-permute-start.14 = (bf16[256,512]{1,0:T(8,128)(2,1)S(1)}, bf16[256,512]{1,0:T(8,128)(2,1)S(1)}, u32[]{:S(2)}, u32[]{:S(2)}) collective-permute-start(bf16[256,512]{1,0:T(8,128)(2,1)S(1)} %combine.3.refs_0_.refs_4_), channel_id=1, source_target_pairs={{0,8},{2,10},{4,12},{6,14},{8,0},{10,2},{12,4},{14,6},{16,24},{18,... | collective-permute-start | bytes 786440 | tf_op jit(solution)/shard_map/ppermute | solution.py:136
  35.0 1.5 %collective-permute-start.11 = (bf16[256,512]{1,0:T(8,128)(2,1)S(1)}, bf16[256,512]{1,0:T(8,128)(2,1)S(1)}, u32[]{:S(2)}, u32[]{:S(2)}) collective-permute-start(bf16[256,512]{1,0:T(8,128)(2,1)S(1)} %collective-permute-done.10.rest_1_.refs_2_), channel_id=1, source_target_pairs={{0,4},{2,6},{4,0},{6,2},{8,12},{10,14},{12,8},{14,10},{16,20},{18,... | collective-permute-start | bytes 786440 | tf_op jit(solution)/shard_map/ppermute | solution.py:136
  36.5 0.5 collective-permute-start.13
  37.1 4.9 %collective-permute-done.6.refs_0_.xb_ref = bf16[4,2,128,256]{3,2,1,0:T(8,128)(2,1)S(1)} collective-permute-done((bf16[4,2,128,256]{3,2,1,0:T(8,128)(2,1)S(1)}, bf16[4,2,128,256]{3,2,1,0:T(8,128)(2,1)S(1)}, u32[]{:S(2)}, u32[]{:S(2)}) %collective-permute-start.6) | collective-permute-done | bytes 524320 | tf_op jit(solution)/shard_map/ppermute | solution.py:140
  42.0 0.7 project_away.2
  42.7 0.1 collective-permute-start.16
  42.8 0.5 collective-permute-start.17
  43.3 0.1 collective-permute-start.18
  43.4 0.4 collective-permute-start.19
  43.8 0.9 %collective-permute-done.13.refs_4_.refs_1_.refs_5_ = bf16[256,512]{1,0:T(8,128)(2,1)S(1)} collective-permute-done((bf16[256,512]{1,0:T(8,128)(2,1)S(1)}, bf16[256,512]{1,0:T(8,128)(2,1)S(1)}, u32[]{:S(2)}, u32[]{:S(2)}) %collective-permute-start.13) | collective-permute-done | bytes 262176 | tf_op jit(solution)/shard_map/ppermute | solution.py:136
  44.7 0.1 collective-permute-done.19.refs_3_
  45.0 0.4 collective-permute-start.20
  45.4 1.0 %collective-permute-start.7 = (bf16[4,2,128,256]{3,2,1,0:T(8,128)(2,1)S(1)}, bf16[4,2,128,256]{3,2,1,0:T(8,128)(2,1)S(1)}, u32[]{:S(2)}, u32[]{:S(2)}) collective-permute-start(bf16[4,2,128,256]{3,2,1,0:T(8,128)(2,1)S(1)} %join_cores.1.xa_ref), channel_id=1, source_target_pairs={{0,1},{1,0},{2,3},{3,2},{4,5},{5,4},{6,7},{7,6},{8,9},{9,8},{10,11... | collective-permute-start | bytes 1572872 | tf_op jit(solution)/shard_map/ppermute | solution.py:140
  46.4 1.6 %collective-permute-start.15 = (bf16[256,512]{1,0:T(8,128)(2,1)S(1)}, bf16[256,512]{1,0:T(8,128)(2,1)S(1)}, u32[]{:S(2)}, u32[]{:S(2)}) collective-permute-start(bf16[256,512]{1,0:T(8,128)(2,1)S(1)} %collective-permute-done.14.refs_4_.refs_2_.refs_6_), channel_id=1, source_target_pairs={{0,4},{2,6},{4,0},{6,2},{8,12},{10,14},{12,8},{14,10},{16,20},{18,... | collective-permute-start | bytes 786440 | tf_op jit(solution)/shard_map/ppermute | solution.py:136
  48.0 2.6 %collective-permute-start.25 = (bf16[256,512]{1,0:T(8,128)(2,1)S(1)}, bf16[256,512]{1,0:T(8,128)(2,1)S(1)}, u32[]{:S(2)}, u32[]{:S(2)}) collective-permute-start(bf16[256,512]{1,0:T(8,128)(2,1)S(1)} %add_round.2.refs_4_), channel_id=1, source_target_pairs={{0,16},{2,18},{4,20},{6,22},{8,24},{10,26},{12,28},{14,30},{16,0},... | collective-permute-start | bytes 786440 | tf_op jit(solution)/shard_map/ppermute | solution.py:136
  50.6 3.9 %collective-permute-done.15.refs_3_.refs_7_ = bf16[256,512]{1,0:T(8,128)(2,1)S(1)} collective-permute-done((bf16[256,512]{1,0:T(8,128)(2,1)S(1)}, bf16[256,512]{1,0:T(8,128)(2,1)S(1)}, u32[]{:S(2)}, u32[]{:S(2)}) %collective-permute-start.15) | collective-permute-done | bytes 262176 | tf_op jit(solution)/shard_map/ppermute | solution.py:136
  54.5 0.7 project_away.3
  55.2 0.1 collective-permute-start.21
  55.3 0.5 collective-permute-start.22
  55.8 0.1 collective-permute-start.23
  55.9 3.6 %collective-permute-done.7.refs_4_.xb_ref = bf16[4,2,128,256]{3,2,1,0:T(8,128)(2,1)S(1)} collective-permute-done((bf16[4,2,128,256]{3,2,1,0:T(8,128)(2,1)S(1)}, bf16[4,2,128,256]{3,2,1,0:T(8,128)(2,1)S(1)}, u32[]{:S(2)}, u32[]{:S(2)}) %collective-permute-start.7) | collective-permute-done | bytes 524320 | tf_op jit(solution)/shard_map/ppermute | solution.py:140
  59.5 1.3 %collective-permute-done.24.refs_3_ = f32[64,512]{1,0:T(8,128)S(1)} collective-permute-done((f32[64,512]{1,0:T(8,128)S(1)}, f32[64,512]{1,0:T(8,128)S(1)}, u32[]{:S(2)}, u32[]{:S(2)}) %collective-permute-start.24) | collective-permute-done | bytes 131104 | tf_op jit(solution)/shard_map/ppermute | solution.py:136
  60.9 1.4 %collective-permute-done.25.refs_5_.refs_0_ = bf16[256,512]{1,0:T(8,128)(2,1)S(1)} collective-permute-done((bf16[256,512]{1,0:T(8,128)(2,1)S(1)}, bf16[256,512]{1,0:T(8,128)(2,1)S(1)}, u32[]{:S(2)}, u32[]{:S(2)}) %collective-permute-start.25) | collective-permute-done | bytes 262176 | tf_op jit(solution)/shard_map/ppermute | solution.py:136
  62.4 0.1 collective-permute-start.26
  62.5 1.3 %collective-permute-start.27 = (bf16[256,512]{1,0:T(8,128)(2,1)S(1)}, bf16[256,512]{1,0:T(8,128)(2,1)S(1)}, u32[]{:S(2)}, u32[]{:S(2)}) collective-permute-start(bf16[256,512]{1,0:T(8,128)(2,1)S(1)} %add_round.3.refs_4_.refs_12_), channel_id=1, source_target_pairs={{0,16},{2,18},{4,20},{6,22},{8,24},{10,26},{12,28},{14,30},{16,0},... | collective-permute-start | bytes 786440 | tf_op jit(solution)/shard_map/ppermute | solution.py:136
  63.8 1.3 %collective-permute-done.26.refs_9_ = bf16[1024,512]{1,0:T(8,128)(2,1)S(1)} collective-permute-done((bf16[1024,512]{1,0:T(8,128)(2,1)S(1)}, bf16[1024,512]{1,0:T(8,128)(2,1)S(1)}, u32[]{:S(2)}, u32[]{:S(2)}) %collective-permute-start.26) | collective-permute-done | bytes 1048608 | tf_op jit(solution)/shard_map/ppermute | solution.py:136
  65.1 1.9 %project_home.1 = (f32[256,1024]{1,0:T(8,128)S(1)}, bf16[128,4096]{1,0:T(8,128)(2,1)}) custom-call(s32[1]{0:T(128)} %bitcast.at_ref, bf16[4,2,128,256]{3,2,1,0:T(8,128)(2,1)S(1)} %join_cores.1.xa_ref, bf16[4,2,128,256]{3,2,1,0:T(8,128)(2,1)S(1)} %collective-permute-done.7.refs_4_.xb_ref, bf16[256,512]{1,0:T(8,128)(2,1)S(1)} %combine.2.refs_0_, ...), custom_call_target="tpu_custom_call" | custom-call | tf_op jit(solution)/shard_map/project_home/pallas_call | solution.py:551
  67.0 10.7 %collective-permute-done.27.refs_1_ = bf16[256,512]{1,0:T(8,128)(2,1)S(1)} collective-permute-done((bf16[256,512]{1,0:T(8,128)(2,1)S(1)}, bf16[256,512]{1,0:T(8,128)(2,1)S(1)}, u32[]{:S(2)}, u32[]{:S(2)}) %collective-permute-start.27) | collective-permute-done | bytes 262176 | tf_op jit(solution)/shard_map/ppermute | solution.py:136
  77.7 1.1 %finish.1 = (f32[256,512]{1,0:T(8,128)}, f32[256,512]{1,0:T(8,128)}) custom-call(f32[256,1024]{1,0:T(8,128)S(1)} %get-tuple-element.72.keep_ref, bf16[256,512]{1,0:T(8,128)(2,1)S(1)} %collective-permute-done.25.refs_5_.refs_0_, bf16[256,512]{1,0:T(8,128)(2,1)S(1)} %collective-permute-done.27.refs_1_), custom_call_target="tpu_custom_call" | custom-call | tf_op jit(solution)/shard_map/finish/pallas_call | solution.py:580
  (26 shorter events, 0.4 us)
Async XLA Ops:
  1.7 12.3 %collective-permute-start.4 = (bf16[128,1024]{1,0:T(8,128)(2,1)S(1)}, bf16[128,1024]{1,0:T(8,128)(2,1)S(1)}, u32[]{:S(2)}, u32[]{:S(2)}) collective-permute-start(bf16[128,1024]{1,0:T(8,128)(2,1)S(1)} %get-tuple-element.39.after_ref), channel_id=1, source_target_pairs={{0,1},{2,3},{4,5},{6,7},{8,9},{10,11},{12,13},{14,15},{16,17},{18,... | collective-permute-start | bytes 786440 | tf_op jit(solution)/shard_map/ppermute | solution.py:598
  8.0 13.4 %collective-permute-start = (bf16[4,128,256]{2,1,0:T(8,128)(2,1)S(1)}, bf16[4,128,256]{2,1,0:T(8,128)(2,1)S(1)}, u32[]{:S(2)}, u32[]{:S(2)}) collective-permute-start(bf16[4,128,256]{2,1,0:T(8,128)(2,1)S(1)} %get-tuple-element.41), channel_id=1, source_target_pairs={{0,4},{2,6},{4,0},{6,2},{8,12},{10,14},{12,8},{14,10},{16,20},{18,... | collective-permute-start | bytes 786440 | tf_op jit(solution)/shard_map/ppermute | solution.py:136
  9.6 11.9 %collective-permute-start.2 = (bf16[4,128,256]{2,1,0:T(8,128)(2,1)S(1)}, bf16[4,128,256]{2,1,0:T(8,128)(2,1)S(1)}, u32[]{:S(2)}, u32[]{:S(2)}) collective-permute-start(bf16[4,128,256]{2,1,0:T(8,128)(2,1)S(1)} %get-tuple-element.43), channel_id=1, source_target_pairs={{0,12},{2,14},{4,8},{6,10},{8,4},{10,6},{12,0},{14,2},{16,28},{18,... | collective-permute-start | bytes 786440 | tf_op jit(solution)/shard_map/ppermute | solution.py:136
  11.1 10.4 %collective-permute-start.3 = (bf16[128,1024]{1,0:T(8,128)(2,1)S(1)}, bf16[128,1024]{1,0:T(8,128)(2,1)S(1)}, u32[]{:S(2)}, u32[]{:S(2)}) collective-permute-start(bf16[128,1024]{1,0:T(8,128)(2,1)S(1)} %get-tuple-element.48), channel_id=1, source_target_pairs={{0,1},{2,3},{4,5},{6,7},{8,9},{10,11},{12,13},{14,15},{16,17},{18,... | collective-permute-start | bytes 786440 | tf_op jit(solution)/shard_map/ppermute | solution.py:598
  16.4 8.1 %collective-permute-start.8 = (bf16[256,512]{1,0:T(8,128)(2,1)S(1)}, bf16[256,512]{1,0:T(8,128)(2,1)S(1)}, u32[]{:S(2)}, u32[]{:S(2)}) collective-permute-start(bf16[256,512]{1,0:T(8,128)(2,1)S(1)} %get-tuple-element.57), channel_id=1, source_target_pairs={{0,1},{1,0},{2,3},{3,2},{4,5},{5,4},{6,7},{7,6},{8,9},{9,8},{10,11... | collective-permute-start | bytes 786440 | tf_op jit(solution)/shard_map/ppermute | solution.py:140
  18.3 9.4 %collective-permute-start.1 = (bf16[4,128,256]{2,1,0:T(8,128)(2,1)S(1)}, bf16[4,128,256]{2,1,0:T(8,128)(2,1)S(1)}, u32[]{:S(2)}, u32[]{:S(2)}) collective-permute-start(bf16[4,128,256]{2,1,0:T(8,128)(2,1)S(1)} %get-tuple-element.42), channel_id=1, source_target_pairs={{0,8},{2,10},{4,12},{6,14},{8,0},{10,2},{12,4},{14,6},{16,24},{18,... | collective-permute-start | bytes 786440 | tf_op jit(solution)/shard_map/ppermute | solution.py:136
  23.8 9.2 %collective-permute-start.12 = (bf16[256,512]{1,0:T(8,128)(2,1)S(1)}, bf16[256,512]{1,0:T(8,128)(2,1)S(1)}, u32[]{:S(2)}, u32[]{:S(2)}) collective-permute-start(bf16[256,512]{1,0:T(8,128)(2,1)S(1)} %get-tuple-element.59), channel_id=1, source_target_pairs={{0,1},{1,0},{2,3},{3,2},{4,5},{5,4},{6,7},{7,6},{8,9},{9,8},{10,11... | collective-permute-start | bytes 786440 | tf_op jit(solution)/shard_map/ppermute | solution.py:140
  24.5 8.5 %collective-permute-start.10 = (bf16[256,512]{1,0:T(8,128)(2,1)S(1)}, bf16[256,512]{1,0:T(8,128)(2,1)S(1)}, u32[]{:S(2)}, u32[]{:S(2)}) collective-permute-start(bf16[256,512]{1,0:T(8,128)(2,1)S(1)} %combine.2.refs_0_), channel_id=1, source_target_pairs={{0,8},{2,10},{4,12},{6,14},{8,0},{10,2},{12,4},{14,6},{16,24},{18,... | collective-permute-start | bytes 786440 | tf_op jit(solution)/shard_map/ppermute | solution.py:136
  26.2 6.8 %collective-permute-start.9 = (bf16[256,512]{1,0:T(8,128)(2,1)S(1)}, bf16[256,512]{1,0:T(8,128)(2,1)S(1)}, u32[]{:S(2)}, u32[]{:S(2)}) collective-permute-start(bf16[256,512]{1,0:T(8,128)(2,1)S(1)} %combine.2.refs_0_), channel_id=1, source_target_pairs={{0,4},{2,6},{4,0},{6,2},{8,12},{10,14},{12,8},{14,10},{16,20},{18,... | collective-permute-start | bytes 786440 | tf_op jit(solution)/shard_map/ppermute | solution.py:136
  27.7 14.3 %collective-permute-start.6 = (bf16[4,2,128,256]{3,2,1,0:T(8,128)(2,1)S(1)}, bf16[4,2,128,256]{3,2,1,0:T(8,128)(2,1)S(1)}, u32[]{:S(2)}, u32[]{:S(2)}) collective-permute-start(bf16[4,2,128,256]{3,2,1,0:T(8,128)(2,1)S(1)} %pack_normed.3.xa_ref), channel_id=1, source_target_pairs={{0,1},{1,0},{2,3},{3,2},{4,5},{5,4},{6,7},{7,6},{8,9},{9,8},{10,11... | collective-permute-start | bytes 1572872 | tf_op jit(solution)/shard_map/ppermute | solution.py:140
  29.3 7.8 %collective-permute-start.5 = (bf16[4,128,256]{2,1,0:T(8,128)(2,1)S(1)}, bf16[4,128,256]{2,1,0:T(8,128)(2,1)S(1)}, u32[]{:S(2)}, u32[]{:S(2)}) collective-permute-start(bf16[4,128,256]{2,1,0:T(8,128)(2,1)S(1)} %get-tuple-element.54), channel_id=1, source_target_pairs={{0,2},{2,0},{4,6},{6,4},{8,10},{10,8},{12,14},{14,12},{16,18},{18,... | collective-permute-start | bytes 786440 | tf_op jit(solution)/shard_map/ppermute | solution.py:136
  33.2 8.8 %collective-permute-start.14 = (bf16[256,512]{1,0:T(8,128)(2,1)S(1)}, bf16[256,512]{1,0:T(8,128)(2,1)S(1)}, u32[]{:S(2)}, u32[]{:S(2)}) collective-permute-start(bf16[256,512]{1,0:T(8,128)(2,1)S(1)} %combine.3.refs_0_.refs_4_), channel_id=1, source_target_pairs={{0,8},{2,10},{4,12},{6,14},{8,0},{10,2},{12,4},{14,6},{16,24},{18,... | collective-permute-start | bytes 786440 | tf_op jit(solution)/shard_map/ppermute | solution.py:136
  35.0 7.0 %collective-permute-start.11 = (bf16[256,512]{1,0:T(8,128)(2,1)S(1)}, bf16[256,512]{1,0:T(8,128)(2,1)S(1)}, u32[]{:S(2)}, u32[]{:S(2)}) collective-permute-start(bf16[256,512]{1,0:T(8,128)(2,1)S(1)} %collective-permute-done.10.rest_1_.refs_2_), channel_id=1, source_target_pairs={{0,4},{2,6},{4,0},{6,2},{8,12},{10,14},{12,8},{14,10},{16,20},{18,... | collective-permute-start | bytes 786440 | tf_op jit(solution)/shard_map/ppermute | solution.py:136
  36.5 8.2 %collective-permute-start.13 = (bf16[256,512]{1,0:T(8,128)(2,1)S(1)}, bf16[256,512]{1,0:T(8,128)(2,1)S(1)}, u32[]{:S(2)}, u32[]{:S(2)}) collective-permute-start(bf16[256,512]{1,0:T(8,128)(2,1)S(1)} %combine.3.refs_0_.refs_4_), channel_id=1, source_target_pairs={{0,4},{2,6},{4,0},{6,2},{8,12},{10,14},{12,8},{14,10},{16,20},{18,... | collective-permute-start | bytes 786440 | tf_op jit(solution)/shard_map/ppermute | solution.py:136
  42.7 2.0 %collective-permute-start.16 = (f32[64,512]{1,0:T(8,128)S(1)}, f32[64,512]{1,0:T(8,128)S(1)}, u32[]{:S(2)}, u32[]{:S(2)}) collective-permute-start(f32[64,512]{1,0:T(8,128)S(1)} %get-tuple-element.61), channel_id=1, source_target_pairs={{0,2},{2,0},{4,6},{6,4},{8,10},{10,8},{12,14},{14,12},{16,18},{18,... | collective-permute-start | bytes 393224 | tf_op jit(solution)/shard_map/ppermute | solution.py:136
  42.8 1.9 %collective-permute-start.17 = (f32[64,512]{1,0:T(8,128)S(1)}, f32[64,512]{1,0:T(8,128)S(1)}, u32[]{:S(2)}, u32[]{:S(2)}) collective-permute-start(f32[64,512]{1,0:T(8,128)S(1)} %get-tuple-element.62), channel_id=1, source_target_pairs={{0,2},{2,0},{4,6},{6,4},{8,10},{10,8},{12,14},{14,12},{16,18},{18,... | collective-permute-start | bytes 393224 | tf_op jit(solution)/shard_map/ppermute | solution.py:136
  43.3 1.4 %collective-permute-start.18 = (f32[64,512]{1,0:T(8,128)S(1)}, f32[64,512]{1,0:T(8,128)S(1)}, u32[]{:S(2)}, u32[]{:S(2)}) collective-permute-start(f32[64,512]{1,0:T(8,128)S(1)} %get-tuple-element.63), channel_id=1, source_target_pairs={{0,2},{2,0},{4,6},{6,4},{8,10},{10,8},{12,14},{14,12},{16,18},{18,... | collective-permute-start | bytes 393224 | tf_op jit(solution)/shard_map/ppermute | solution.py:136
  43.4 1.5 %collective-permute-start.19 = (f32[64,512]{1,0:T(8,128)S(1)}, f32[64,512]{1,0:T(8,128)S(1)}, u32[]{:S(2)}, u32[]{:S(2)}) collective-permute-start(f32[64,512]{1,0:T(8,128)S(1)} %get-tuple-element.64), channel_id=1, source_target_pairs={{0,2},{2,0},{4,6},{6,4},{8,10},{10,8},{12,14},{14,12},{16,18},{18,... | collective-permute-start | bytes 393224 | tf_op jit(solution)/shard_map/ppermute | solution.py:136
  45.0 9.5 %collective-permute-start.20 = (bf16[1024,512]{1,0:T(8,128)(2,1)S(1)}, bf16[1024,512]{1,0:T(8,128)(2,1)S(1)}, u32[]{:S(2)}, u32[]{:S(2)}) collective-permute-start(bf16[1024,512]{1,0:T(8,128)(2,1)S(1)} %join_places.2), channel_id=1, source_target_pairs={{0,2},{2,0},{4,6},{6,4},{8,10},{10,8},{12,14},{14,12},{16,18},{18,... | collective-permute-start | bytes 3145736 | tf_op jit(solution)/shard_map/ppermute | solution.py:136
  45.4 14.1 %collective-permute-start.7 = (bf16[4,2,128,256]{3,2,1,0:T(8,128)(2,1)S(1)}, bf16[4,2,128,256]{3,2,1,0:T(8,128)(2,1)S(1)}, u32[]{:S(2)}, u32[]{:S(2)}) collective-permute-start(bf16[4,2,128,256]{3,2,1,0:T(8,128)(2,1)S(1)} %join_cores.1.xa_ref), channel_id=1, source_target_pairs={{0,1},{1,0},{2,3},{3,2},{4,5},{5,4},{6,7},{7,6},{8,9},{9,8},{10,11... | collective-permute-start | bytes 1572872 | tf_op jit(solution)/shard_map/ppermute | solution.py:140
  46.4 8.1 %collective-permute-start.15 = (bf16[256,512]{1,0:T(8,128)(2,1)S(1)}, bf16[256,512]{1,0:T(8,128)(2,1)S(1)}, u32[]{:S(2)}, u32[]{:S(2)}) collective-permute-start(bf16[256,512]{1,0:T(8,128)(2,1)S(1)} %collective-permute-done.14.refs_4_.refs_2_.refs_6_), channel_id=1, source_target_pairs={{0,4},{2,6},{4,0},{6,2},{8,12},{10,14},{12,8},{14,10},{16,20},{18,... | collective-permute-start | bytes 786440 | tf_op jit(solution)/shard_map/ppermute | solution.py:136
  48.0 14.4 %collective-permute-start.25 = (bf16[256,512]{1,0:T(8,128)(2,1)S(1)}, bf16[256,512]{1,0:T(8,128)(2,1)S(1)}, u32[]{:S(2)}, u32[]{:S(2)}) collective-permute-start(bf16[256,512]{1,0:T(8,128)(2,1)S(1)} %add_round.2.refs_4_), channel_id=1, source_target_pairs={{0,16},{2,18},{4,20},{6,22},{8,24},{10,26},{12,28},{14,30},{16,0},... | collective-permute-start | bytes 786440 | tf_op jit(solution)/shard_map/ppermute | solution.py:136
  55.2 4.3 %collective-permute-start.21 = (f32[64,512]{1,0:T(8,128)S(1)}, f32[64,512]{1,0:T(8,128)S(1)}, u32[]{:S(2)}, u32[]{:S(2)}) collective-permute-start(f32[64,512]{1,0:T(8,128)S(1)} %get-tuple-element.66), channel_id=1, source_target_pairs={{0,2},{2,0},{4,6},{6,4},{8,10},{10,8},{12,14},{14,12},{16,18},{18,... | collective-permute-start | bytes 393224 | tf_op jit(solution)/shard_map/ppermute | solution.py:136
  55.3 4.2 %collective-permute-start.22 = (f32[64,512]{1,0:T(8,128)S(1)}, f32[64,512]{1,0:T(8,128)S(1)}, u32[]{:S(2)}, u32[]{:S(2)}) collective-permute-start(f32[64,512]{1,0:T(8,128)S(1)} %get-tuple-element.67), channel_id=1, source_target_pairs={{0,2},{2,0},{4,6},{6,4},{8,10},{10,8},{12,14},{14,12},{16,18},{18,... | collective-permute-start | bytes 393224 | tf_op jit(solution)/shard_map/ppermute | solution.py:136
  55.8 3.7 %collective-permute-start.23 = (f32[64,512]{1,0:T(8,128)S(1)}, f32[64,512]{1,0:T(8,128)S(1)}, u32[]{:S(2)}, u32[]{:S(2)}) collective-permute-start(f32[64,512]{1,0:T(8,128)S(1)} %get-tuple-element.68), channel_id=1, source_target_pairs={{0,2},{2,0},{4,6},{6,4},{8,10},{10,8},{12,14},{14,12},{16,18},{18,... | collective-permute-start | bytes 393224 | tf_op jit(solution)/shard_map/ppermute | solution.py:136
  59.5 1.3 %collective-permute-start.24 = (f32[64,512]{1,0:T(8,128)S(1)}, f32[64,512]{1,0:T(8,128)S(1)}, u32[]{:S(2)}, u32[]{:S(2)}) collective-permute-start(f32[64,512]{1,0:T(8,128)S(1)} %get-tuple-element.69), channel_id=1, source_target_pairs={{0,2},{2,0},{4,6},{6,4},{8,10},{10,8},{12,14},{14,12},{16,18},{18,... | collective-permute-start | bytes 393224 | tf_op jit(solution)/shard_map/ppermute | solution.py:136
  62.4 2.7 %collective-permute-start.26 = (bf16[1024,512]{1,0:T(8,128)(2,1)S(1)}, bf16[1024,512]{1,0:T(8,128)(2,1)S(1)}, u32[]{:S(2)}, u32[]{:S(2)}) collective-permute-start(bf16[1024,512]{1,0:T(8,128)(2,1)S(1)} %join_places.3), channel_id=1, source_target_pairs={{0,2},{2,0},{4,6},{6,4},{8,10},{10,8},{12,14},{14,12},{16,18},{18,... | collective-permute-start | bytes 3145736 | tf_op jit(solution)/shard_map/ppermute | solution.py:136
  62.5 15.2 %collective-permute-start.27 = (bf16[256,512]{1,0:T(8,128)(2,1)S(1)}, bf16[256,512]{1,0:T(8,128)(2,1)S(1)}, u32[]{:S(2)}, u32[]{:S(2)}) collective-permute-start(bf16[256,512]{1,0:T(8,128)(2,1)S(1)} %add_round.3.refs_4_.refs_12_), channel_id=1, source_target_pairs={{0,16},{2,18},{4,20},{6,22},{8,24},{10,26},{12,28},{14,30},{16,0},... | collective-permute-start | bytes 786440 | tf_op jit(solution)/shard_map/ppermute | solution.py:136

commit v5 on v4

--- a/solution.py
+++ b/solution.py
@@ -514,16 +514,18 @@
     )(*grads, *after)
 
 
-def project_home(seq_at, normed, grads, recv, query_grads, after):
+def project_home(seq_at, normed, grads, recv, query_grads, halves, after):
     rows, share = normed[0].shape[2:]
     wide = grads[0][0].shape[1]
     chunks = len(grads)
     part = query_grads[0].shape[2]
+    ready = len(halves)
+    cols = wide // 2
 
     def body(at_ref, xa_ref, xb_ref, *refs):
         ys, refs = refs[: 4 * chunks], refs[4 * chunks :]
-        others, qs = refs[:chunks], refs[chunks : 2 * chunks]
-        out, query_out, sem = refs[-3:]
+        others, qs, half_refs = refs[:chunks], refs[chunks : 2 * chunks], refs[2 * chunks : 2 * chunks + ready]
+        out, query_out, *outs, sums, sem, sum_sem = refs[-7:]
         copies = []
         for chunk, ref in enumerate(qs):
             for j in range(2):
@@ -544,47 +546,71 @@
                     right.append(ys[chunk * 4 + place][seq * rows : (seq + 1) * rows, :])
                     low = (place * 2 + seq) * rows
                     right.append(others[chunk][low : low + rows, :])
-            out[:, chunk * wide : (chunk + 1) * wide] = tn(left, jnp.concatenate(right, axis=0))
+            total = tn(left, jnp.concatenate(right, axis=0))
+            if chunk >= ready:
+                out[:, (chunk - ready) * wide : (chunk - ready + 1) * wide] = total
+                continue
+            for number in range(2):
+                at = slice(number * cols, (number + 1) * cols)
+                sums[chunk, number] = total[:, at] + half_refs[chunk][:, at].astype(F32)
+                copy = pltpu.make_async_copy(
+                    sums.at[chunk, number],
+                    outs[number].at[:, chunk * cols : (chunk + 1) * cols],
+                    sum_sem.at[chunk, number],
+                )
+                copy.start()
+                copies.append(copy)
         for copy in copies:
             copy.wait()
 
     return pl.pallas_call(
         body,
         out_shape=[
-            pltpu.VMEM((share, chunks * wide), F32),
+            pltpu.VMEM((share, (chunks - ready) * wide), F32),
             jax.ShapeDtypeStruct((rows, 2 * chunks * part), BF),
+            pltpu.HBM((share, chunks * cols), F32),
+            pltpu.HBM((share, chunks * cols), F32),
         ],
-        in_specs=[smem()] + [vmem()] * (2 + 6 * chunks) + [hbm()] * len(after),
-        out_specs=[vmem(), hbm()],
-        scratch_shapes=[pltpu.SemaphoreType.DMA((chunks, 2))],
+        in_specs=[smem()] + [vmem()] * (2 + 6 * chunks + ready) + [hbm()] * len(after),
+        out_specs=[vmem(), hbm(), hbm(), hbm()],
+        scratch_shapes=[
+            pltpu.VMEM((ready, 2, share, cols), F32),
+            pltpu.SemaphoreType.DMA((chunks, 2)),
+            pltpu.SemaphoreType.DMA((ready, 2)),
+        ],
         compiler_params=params(),
         name="project_home",
-    )(seq_at, *normed, *[part for parts in grads for part in parts], *recv, *query_grads, *after)
-
-
-def finish(keep, recv_half):
-    rows, width = keep.shape
-    wide = width // NC
-    part = wide // 2
-
-    def body(keep_ref, *refs):
-        halves, outs = refs[:NC], refs[NC:]
-        for chunk, half_ref in enumerate(halves):
-            for number, out in enumerate(outs):
-                low = number * part
-                at = slice(chunk * wide + low, chunk * wide + low + part)
-                out[:, chunk * part : (chunk + 1) * part] = (
-                    keep_ref[:, at] + half_ref[:, low : low + part].astype(F32)
-                )
-
-    return pl.pallas_call(
-        body,
-        out_shape=[jax.ShapeDtypeStruct((rows, width // 2), F32)] * 2,
-        in_specs=[vmem()] * (1 + NC),
-        out_specs=[vmem()] * 2,
+    )(seq_at, *normed, *[part for parts in grads for part in parts], *recv, *query_grads, *halves, *after)
+
+
+def finish(keep, recv_half, sums):
+    rows, wide = keep.shape
+    cols = wide // 2
+    low = sums[0].shape[1] - cols
+
+    def body(keep_ref, half_ref, *refs):
+        outs, total, sem = refs[2:4], refs[4], refs[5]
+        copies = []
+        for number, out in enumerate(outs):
+            at = slice(number * cols, (number + 1) * cols)
+            total[number] = keep_ref[:, at] + half_ref[:, at].astype(F32)
+            copies.append(
+                pltpu.make_async_copy(total.at[number], out.at[:, low : low + cols], sem.at[number])
+            )
+            copies[-1].start()
+        for copy in copies:
+            copy.wait()
+
+    return pl.pallas_call(
+        body,
+        out_shape=[pltpu.HBM(one.shape, F32) for one in sums],
+        in_specs=[vmem()] * 2 + [hbm()] * 2,
+        out_specs=[hbm()] * 2,
+        scratch_shapes=[pltpu.VMEM((2, rows, cols), F32), pltpu.SemaphoreType.DMA((2,))],
+        input_output_aliases={2: 0, 3: 1},
         compiler_params=params(),
         name="finish",
-    )(keep, *recv_half)
+    )(keep, recv_half, *[in_hbm(one) for one in sums])
 
 
 def cube_local(queries, keys, values, out_grad, normed):
@@ -634,8 +660,10 @@
             home = join_cores(same, cross, [away_other])
             home_other = swap_seq(home)
             after, fence = recv_core[:], [home_other]
-    keep, query_grad = project_home(seq_at, (home, home_other), grads, recv_core, query_grads, [total])
-    key_weight_grad, value_weight_grad = finish(keep, recv_half)
+    keep, query_grad, *sums = project_home(
+        seq_at, (home, home_other), grads, recv_core, query_grads, recv_half[:-1], [total]
+    )
+    key_weight_grad, value_weight_grad = finish(keep, recv_half[-1], sums)
     return (query_grad, key_weight_grad, value_weight_grad)
 
 

time: 79 us -> 79 us (level)
  no operation moved by 1% of the time
where the time goes in v5:
time: 79 us; the launch traced here: 78.7 us
  waiting for transfers between devices  32.5 us (41%)
  starting transfers between devices  31.4 us (40%)
  Pallas kernels  13.8 us (17%)
  between operations  1 us (1%)
    ppermute x22, waiting for transfers between devices, flip(): return lax.ppermute(array, 'dp', [(i, i ^ mask) for i in range(16)])  20.3 us
    ppermute x22, starting transfers between devices, flip(): return lax.ppermute(array, 'dp', [(i, i ^ mask) for i in range(16)])  20.2 us
    ppermute x4, waiting for transfers between devices, swap_seq(): return lax.ppermute(array, 'seq', [(0, 1), (1, 0)])  12.2 us
    ppermute x2, starting transfers between devices, cube_local(): kv_recv = [lax.ppermute(part, 'seq', [(0, 1)]) for part in kv]  6.18 us
    ppermute x4, starting transfers between devices, swap_seq(): return lax.ppermute(array, 'seq', [(0, 1), (1, 0)])  5.01 us
    pallas_call x2, Pallas kernels, attention(): pl.pallas_call(body, out_shape=[pltpu.VMEM((2, rows, wide), BF), pltpu.VM...  4.76 us
    pallas_call x1, Pallas kernels, project_home(): pl.pallas_call(body, out_shape=[pltpu.VMEM((share, (chunks - ready) * wid...  2.08 us
    pallas_call x1, Pallas kernels, stage(): pl.pallas_call(body, out_shape=[pltpu.VMEM(one.shape, one.dtype) for one...  1.61 us
  transfers between devices with their start and end apart: 28, of which 11 were waited for; matrix products, arithmetic and copies ran while one was open for 0% of the time, Pallas kernels for 15%

profile of v5, /device:TPU:0, one launch (start us, length us, event | category | flops | bytes accessed | tf_op | source)
XLA Modules:
  0.0 78.7 jit_solution(2173157031909735307)
XLA Ops:
  0.6 1.1 %prepare_kv.1 = (bf16[128,1024]{1,0:T(8,128)(2,1)S(1)}, bf16[128,1024]{1,0:T(8,128)(2,1)S(1)}, bf16[128,1024]{1,0:T(8,128)(2,1)S(1)}, bf16[128,1024]{1,0:T(8,128)(2,1)S(1)}) custom-call(bf16[128,1024]{1,0:T(8,128)(2,1)} %k_hbm.1, bf16[128,1024]{1,0:T(8,128)(2,1)} %v_hbm.1), custom_call_target="tpu_custom_call" | custom-call | tf_op jit(solution)/shard_map/prepare_kv/pallas_call | solution.py:198
  1.7 4.9 %collective-permute-start.4 = (bf16[128,1024]{1,0:T(8,128)(2,1)S(1)}, bf16[128,1024]{1,0:T(8,128)(2,1)S(1)}, u32[]{:S(2)}, u32[]{:S(2)}) collective-permute-start(bf16[128,1024]{1,0:T(8,128)(2,1)S(1)} %get-tuple-element.41.after_ref), channel_id=1, source_target_pairs={{0,1},{2,3},{4,5},{6,7},{8,9},{10,11},{12,13},{14,15},{16,17},{18,... | collective-permute-start | bytes 786440 | tf_op jit(solution)/shard_map/ppermute | solution.py:624
  6.6 1.4 %prepare_normed.1 = (bf16[4,128,256]{2,1,0:T(8,128)(2,1)S(1)}, bf16[4,128,256]{2,1,0:T(8,128)(2,1)S(1)}, bf16[4,128,256]{2,1,0:T(8,128)(2,1)S(1)}, bf16[4,128,256]{2,1,0:T(8,128)(2,1)S(1)}) custom-call(s32[1]{0:T(128)} %bitcast.1.me_ref, bf16[128,4096]{1,0:T(8,128)(2,1)} %x_hbm.1, bf16[128,1024]{1,0:T(8,128)(2,1)S(1)} %get-tuple-element.41.after_ref), custom_call_target="tpu_custom_call" | custom-call | tf_op jit(solution)/shard_map/prepare_normed/pallas_call | solution.py:222
  8.0 1.6 %collective-permute-start = (bf16[4,128,256]{2,1,0:T(8,128)(2,1)S(1)}, bf16[4,128,256]{2,1,0:T(8,128)(2,1)S(1)}, u32[]{:S(2)}, u32[]{:S(2)}) collective-permute-start(bf16[4,128,256]{2,1,0:T(8,128)(2,1)S(1)} %get-tuple-element.43), channel_id=1, source_target_pairs={{0,4},{2,6},{4,0},{6,2},{8,12},{10,14},{12,8},{14,10},{16,20},{18,... | collective-permute-start | bytes 786440 | tf_op jit(solution)/shard_map/ppermute | solution.py:136
  9.6 1.5 %collective-permute-start.2 = (bf16[4,128,256]{2,1,0:T(8,128)(2,1)S(1)}, bf16[4,128,256]{2,1,0:T(8,128)(2,1)S(1)}, u32[]{:S(2)}, u32[]{:S(2)}) collective-permute-start(bf16[4,128,256]{2,1,0:T(8,128)(2,1)S(1)} %get-tuple-element.45), channel_id=1, source_target_pairs={{0,12},{2,14},{4,8},{6,10},{8,4},{10,6},{12,0},{14,2},{16,28},{18,... | collective-permute-start | bytes 786440 | tf_op jit(solution)/shard_map/ppermute | solution.py:136
  11.1 1.3 %collective-permute-start.3 = (bf16[128,1024]{1,0:T(8,128)(2,1)S(1)}, bf16[128,1024]{1,0:T(8,128)(2,1)S(1)}, u32[]{:S(2)}, u32[]{:S(2)}) collective-permute-start(bf16[128,1024]{1,0:T(8,128)(2,1)S(1)} %get-tuple-element.50), channel_id=1, source_target_pairs={{0,1},{2,3},{4,5},{6,7},{8,9},{10,11},{12,13},{14,15},{16,17},{18,... | collective-permute-start | bytes 786440 | tf_op jit(solution)/shard_map/ppermute | solution.py:624
  12.4 1.6 %stage.1 = (bf16[128,4096]{1,0:T(8,128)(2,1)S(1)}, bf16[128,4096]{1,0:T(8,128)(2,1)S(1)}, f32[256,128]{1,0:T(8,128)S(1)}, f32[256,128]{1,0:T(8,128)S(1)}) custom-call(bf16[128,4096]{1,0:T(8,128)(2,1)} %refs_0_.1, bf16[128,4096]{1,0:T(8,128)(2,1)} %refs_1_.1, f32[256,128]{1,0:T(8,128)} %constant.12.clone.refs_2_, f32[256,128]{1,0:T(8,128)} %constant.13.clone.refs_3_), custom_call_target="tpu_custom_call" | custom-call | tf_op jit(solution)/shard_map/stage/pallas_call | solution.py:244
  14.0 2.4 %attention.2 = (bf16[2,128,1024]{2,1,0:T(8,128)(2,1)S(1)}, f32[128,512]{1,0:T(8,128)S(1)}, bf16[128,512]{1,0:T(8,128)(2,1)S(1)}, bf16[256,512]{1,0:T(8,128)(2,1)S(1)}) custom-call(s32[1]{0:T(128)} %bitcast.at_ref, bf16[128,4096]{1,0:T(8,128)(2,1)S(1)} %get-tuple-element.46.q_ref, bf16[128,4096]{1,0:T(8,128)(2,1)S(1)} %get-tuple-element.47.g_ref, ...), custom_call_target="tpu_custom_call" | custom-call | tf_op jit(solution)/shard_map/attention/pallas_call | solution.py:434
  16.4 1.9 %collective-permute-start.8 = (bf16[256,512]{1,0:T(8,128)(2,1)S(1)}, bf16[256,512]{1,0:T(8,128)(2,1)S(1)}, u32[]{:S(2)}, u32[]{:S(2)}) collective-permute-start(bf16[256,512]{1,0:T(8,128)(2,1)S(1)} %get-tuple-element.59), channel_id=1, source_target_pairs={{0,1},{1,0},{2,3},{3,2},{4,5},{5,4},{6,7},{7,6},{8,9},{9,8},{10,11... | collective-permute-start | bytes 786440 | tf_op jit(solution)/shard_map/ppermute | solution.py:140
  18.3 2.4 %collective-permute-start.1 = (bf16[4,128,256]{2,1,0:T(8,128)(2,1)S(1)}, bf16[4,128,256]{2,1,0:T(8,128)(2,1)S(1)}, u32[]{:S(2)}, u32[]{:S(2)}) collective-permute-start(bf16[4,128,256]{2,1,0:T(8,128)(2,1)S(1)} %get-tuple-element.44), channel_id=1, source_target_pairs={{0,8},{2,10},{4,12},{6,14},{8,0},{10,2},{12,4},{14,6},{16,24},{18,... | collective-permute-start | bytes 786440 | tf_op jit(solution)/shard_map/ppermute | solution.py:136
  20.7 0.7 collective-permute-done.rest_0_.refs_1_
  21.5 2.4 %attention.3 = (bf16[2,128,1024]{2,1,0:T(8,128)(2,1)S(1)}, f32[128,512]{1,0:T(8,128)S(1)}, bf16[128,512]{1,0:T(8,128)(2,1)S(1)}, bf16[256,512]{1,0:T(8,128)(2,1)S(1)}) custom-call(s32[1]{0:T(128)} %bitcast.at_ref, bf16[128,4096]{1,0:T(8,128)(2,1)S(1)} %get-tuple-element.46.q_ref, bf16[128,4096]{1,0:T(8,128)(2,1)S(1)} %get-tuple-element.47.g_ref, ...), custom_call_target="tpu_custom_call" | custom-call | tf_op jit(solution)/shard_map/attention/pallas_call | solution.py:434
  23.8 0.7 collective-permute-start.12
  24.5 1.6 %collective-permute-start.10 = (bf16[256,512]{1,0:T(8,128)(2,1)S(1)}, bf16[256,512]{1,0:T(8,128)(2,1)S(1)}, u32[]{:S(2)}, u32[]{:S(2)}) collective-permute-start(bf16[256,512]{1,0:T(8,128)(2,1)S(1)} %combine.2.refs_0_), channel_id=1, source_target_pairs={{0,8},{2,10},{4,12},{6,14},{8,0},{10,2},{12,4},{14,6},{16,24},{18,... | collective-permute-start | bytes 786440 | tf_op jit(solution)/shard_map/ppermute | solution.py:136
  26.2 1.5 %collective-permute-start.9 = (bf16[256,512]{1,0:T(8,128)(2,1)S(1)}, bf16[256,512]{1,0:T(8,128)(2,1)S(1)}, u32[]{:S(2)}, u32[]{:S(2)}) collective-permute-start(bf16[256,512]{1,0:T(8,128)(2,1)S(1)} %combine.2.refs_0_), channel_id=1, source_target_pairs={{0,4},{2,6},{4,0},{6,2},{8,12},{10,14},{12,8},{14,10},{16,20},{18,... | collective-permute-start | bytes 786440 | tf_op jit(solution)/shard_map/ppermute | solution.py:136
  27.7 1.5 %collective-permute-start.6 = (bf16[4,2,128,256]{3,2,1,0:T(8,128)(2,1)S(1)}, bf16[4,2,128,256]{3,2,1,0:T(8,128)(2,1)S(1)}, u32[]{:S(2)}, u32[]{:S(2)}) collective-permute-start(bf16[4,2,128,256]{3,2,1,0:T(8,128)(2,1)S(1)} %pack_normed.3.xa_ref), channel_id=1, source_target_pairs={{0,1},{1,0},{2,3},{3,2},{4,5},{5,4},{6,7},{7,6},{8,9},{9,8},{10,11... | collective-permute-start | bytes 1572872 | tf_op jit(solution)/shard_map/ppermute | solution.py:140
  29.3 0.1 collective-permute-start.5
  29.3 3.7 %collective-permute-done.12.recv_ref = bf16[256,512]{1,0:T(8,128)(2,1)S(1)} collective-permute-done((bf16[256,512]{1,0:T(8,128)(2,1)S(1)}, bf16[256,512]{1,0:T(8,128)(2,1)S(1)}, u32[]{:S(2)}, u32[]{:S(2)}) %collective-permute-start.12) | collective-permute-done | bytes 262176 | tf_op jit(solution)/shard_map/ppermute | solution.py:140
  33.0 0.2 combine.3.refs_0_.refs_4_
  33.2 1.8 %collective-permute-start.14 = (bf16[256,512]{1,0:T(8,128)(2,1)S(1)}, bf16[256,512]{1,0:T(8,128)(2,1)S(1)}, u32[]{:S(2)}, u32[]{:S(2)}) collective-permute-start(bf16[256,512]{1,0:T(8,128)(2,1)S(1)} %combine.3.refs_0_.refs_4_), channel_id=1, source_target_pairs={{0,8},{2,10},{4,12},{6,14},{8,0},{10,2},{12,4},{14,6},{16,24},{18,... | collective-permute-start | bytes 786440 | tf_op jit(solution)/shard_map/ppermute | solution.py:136
  35.0 1.5 %collective-permute-start.11 = (bf16[256,512]{1,0:T(8,128)(2,1)S(1)}, bf16[256,512]{1,0:T(8,128)(2,1)S(1)}, u32[]{:S(2)}, u32[]{:S(2)}) collective-permute-start(bf16[256,512]{1,0:T(8,128)(2,1)S(1)} %collective-permute-done.10.rest_1_.refs_2_), channel_id=1, source_target_pairs={{0,4},{2,6},{4,0},{6,2},{8,12},{10,14},{12,8},{14,10},{16,20},{18,... | collective-permute-start | bytes 786440 | tf_op jit(solution)/shard_map/ppermute | solution.py:136
  36.5 0.5 collective-permute-start.13
  37.1 4.9 %collective-permute-done.6.refs_0_.xb_ref = bf16[4,2,128,256]{3,2,1,0:T(8,128)(2,1)S(1)} collective-permute-done((bf16[4,2,128,256]{3,2,1,0:T(8,128)(2,1)S(1)}, bf16[4,2,128,256]{3,2,1,0:T(8,128)(2,1)S(1)}, u32[]{:S(2)}, u32[]{:S(2)}) %collective-permute-start.6) | collective-permute-done | bytes 524320 | tf_op jit(solution)/shard_map/ppermute | solution.py:140
  42.0 0.7 project_away.2
  42.7 0.1 collective-permute-start.16
  42.8 0.5 collective-permute-start.17
  43.3 0.1 collective-permute-start.18
  43.4 0.4 collective-permute-start.19
  43.8 0.9 %collective-permute-done.13.refs_4_.refs_1_.refs_5_ = bf16[256,512]{1,0:T(8,128)(2,1)S(1)} collective-permute-done((bf16[256,512]{1,0:T(8,128)(2,1)S(1)}, bf16[256,512]{1,0:T(8,128)(2,1)S(1)}, u32[]{:S(2)}, u32[]{:S(2)}) %collective-permute-start.13) | collective-permute-done | bytes 262176 | tf_op jit(solution)/shard_map/ppermute | solution.py:136
  44.7 0.1 collective-permute-done.19.refs_3_
  45.0 0.4 collective-permute-start.20
  45.4 1.0 %collective-permute-start.7 = (bf16[4,2,128,256]{3,2,1,0:T(8,128)(2,1)S(1)}, bf16[4,2,128,256]{3,2,1,0:T(8,128)(2,1)S(1)}, u32[]{:S(2)}, u32[]{:S(2)}) collective-permute-start(bf16[4,2,128,256]{3,2,1,0:T(8,128)(2,1)S(1)} %join_cores.1.xa_ref), channel_id=1, source_target_pairs={{0,1},{1,0},{2,3},{3,2},{4,5},{5,4},{6,7},{7,6},{8,9},{9,8},{10,11... | collective-permute-start | bytes 1572872 | tf_op jit(solution)/shard_map/ppermute | solution.py:140
  46.4 1.6 %collective-permute-start.15 = (bf16[256,512]{1,0:T(8,128)(2,1)S(1)}, bf16[256,512]{1,0:T(8,128)(2,1)S(1)}, u32[]{:S(2)}, u32[]{:S(2)}) collective-permute-start(bf16[256,512]{1,0:T(8,128)(2,1)S(1)} %collective-permute-done.14.refs_4_.refs_2_.refs_6_), channel_id=1, source_target_pairs={{0,4},{2,6},{4,0},{6,2},{8,12},{10,14},{12,8},{14,10},{16,20},{18,... | collective-permute-start | bytes 786440 | tf_op jit(solution)/shard_map/ppermute | solution.py:136
  48.0 2.6 %collective-permute-start.25 = (bf16[256,512]{1,0:T(8,128)(2,1)S(1)}, bf16[256,512]{1,0:T(8,128)(2,1)S(1)}, u32[]{:S(2)}, u32[]{:S(2)}) collective-permute-start(bf16[256,512]{1,0:T(8,128)(2,1)S(1)} %add_round.2.refs_4_), channel_id=1, source_target_pairs={{0,16},{2,18},{4,20},{6,22},{8,24},{10,26},{12,28},{14,30},{16,0},... | collective-permute-start | bytes 786440 | tf_op jit(solution)/shard_map/ppermute | solution.py:136
  50.6 3.9 %collective-permute-done.15.refs_3_.refs_7_ = bf16[256,512]{1,0:T(8,128)(2,1)S(1)} collective-permute-done((bf16[256,512]{1,0:T(8,128)(2,1)S(1)}, bf16[256,512]{1,0:T(8,128)(2,1)S(1)}, u32[]{:S(2)}, u32[]{:S(2)}) %collective-permute-start.15) | collective-permute-done | bytes 262176 | tf_op jit(solution)/shard_map/ppermute | solution.py:136
  54.5 0.7 project_away.3
  55.2 0.1 collective-permute-start.21
  55.3 0.5 collective-permute-start.22
  55.8 0.1 collective-permute-start.23
  55.9 3.6 %collective-permute-done.7.refs_4_.xb_ref = bf16[4,2,128,256]{3,2,1,0:T(8,128)(2,1)S(1)} collective-permute-done((bf16[4,2,128,256]{3,2,1,0:T(8,128)(2,1)S(1)}, bf16[4,2,128,256]{3,2,1,0:T(8,128)(2,1)S(1)}, u32[]{:S(2)}, u32[]{:S(2)}) %collective-permute-start.7) | collective-permute-done | bytes 524320 | tf_op jit(solution)/shard_map/ppermute | solution.py:140
  59.5 1.3 %collective-permute-done.24.refs_3_ = f32[64,512]{1,0:T(8,128)S(1)} collective-permute-done((f32[64,512]{1,0:T(8,128)S(1)}, f32[64,512]{1,0:T(8,128)S(1)}, u32[]{:S(2)}, u32[]{:S(2)}) %collective-permute-start.24) | collective-permute-done | bytes 131104 | tf_op jit(solution)/shard_map/ppermute | solution.py:136
  60.9 1.4 %collective-permute-done.25.refs_5_.refs_12_ = bf16[256,512]{1,0:T(8,128)(2,1)S(1)} collective-permute-done((bf16[256,512]{1,0:T(8,128)(2,1)S(1)}, bf16[256,512]{1,0:T(8,128)(2,1)S(1)}, u32[]{:S(2)}, u32[]{:S(2)}) %collective-permute-start.25) | collective-permute-done | bytes 262176 | tf_op jit(solution)/shard_map/ppermute | solution.py:136
  62.4 0.1 collective-permute-start.26
  62.5 1.3 %collective-permute-start.27 = (bf16[256,512]{1,0:T(8,128)(2,1)S(1)}, bf16[256,512]{1,0:T(8,128)(2,1)S(1)}, u32[]{:S(2)}, u32[]{:S(2)}) collective-permute-start(bf16[256,512]{1,0:T(8,128)(2,1)S(1)} %add_round.3.refs_4_.refs_13_), channel_id=1, source_target_pairs={{0,16},{2,18},{4,20},{6,22},{8,24},{10,26},{12,28},{14,30},{16,0},... | collective-permute-start | bytes 786440 | tf_op jit(solution)/shard_map/ppermute | solution.py:136
  63.8 1.3 %collective-permute-done.26.refs_9_ = bf16[1024,512]{1,0:T(8,128)(2,1)S(1)} collective-permute-done((bf16[1024,512]{1,0:T(8,128)(2,1)S(1)}, bf16[1024,512]{1,0:T(8,128)(2,1)S(1)}, u32[]{:S(2)}, u32[]{:S(2)}) %collective-permute-start.26) | collective-permute-done | bytes 1048608 | tf_op jit(solution)/shard_map/ppermute | solution.py:136
  65.1 2.1 %project_home.1 = (f32[256,512]{1,0:T(8,128)S(1)}, bf16[128,4096]{1,0:T(8,128)(2,1)}, f32[256,512]{1,0:T(8,128)}, f32[256,512]{1,0:T(8,128)}) custom-call(s32[1]{0:T(128)} %bitcast.at_ref, bf16[4,2,128,256]{3,2,1,0:T(8,128)(2,1)S(1)} %join_cores.1.xa_ref, bf16[4,2,128,256]{3,2,1,0:T(8,128)(2,1)S(1)} %collective-permute-done.7.refs_4_.xb_ref, ...), custom_call_target="tpu_custom_call" | custom-call | tf_op jit(solution)/shard_map/project_home/pallas_call | solution.py:566
  67.2 10.5 %collective-permute-done.27.half_ref = bf16[256,512]{1,0:T(8,128)(2,1)S(1)} collective-permute-done((bf16[256,512]{1,0:T(8,128)(2,1)S(1)}, bf16[256,512]{1,0:T(8,128)(2,1)S(1)}, u32[]{:S(2)}, u32[]{:S(2)}) %collective-permute-start.27) | collective-permute-done | bytes 262176 | tf_op jit(solution)/shard_map/ppermute | solution.py:136
  77.7 0.8 %finish.1 = (f32[256,512]{1,0:T(8,128)}, f32[256,512]{1,0:T(8,128)}) custom-call(f32[256,512]{1,0:T(8,128)S(1)} %get-tuple-element.74.keep_ref, bf16[256,512]{1,0:T(8,128)(2,1)S(1)} %collective-permute-done.27.half_ref, f32[256,512]{1,0:T(8,128)} %get-tuple-element.75.refs_0_, ...), custom_call_target="tpu_custom_call", output_to_operand_aliasing={{0}: (2, {}), {1}: (3, {})} | custom-call | tf_op jit(solution)/shard_map/finish/pallas_call | solution.py:604
  (26 shorter events, 0.4 us)
Async XLA Ops:
  1.7 12.3 %collective-permute-start.4 = (bf16[128,1024]{1,0:T(8,128)(2,1)S(1)}, bf16[128,1024]{1,0:T(8,128)(2,1)S(1)}, u32[]{:S(2)}, u32[]{:S(2)}) collective-permute-start(bf16[128,1024]{1,0:T(8,128)(2,1)S(1)} %get-tuple-element.41.after_ref), channel_id=1, source_target_pairs={{0,1},{2,3},{4,5},{6,7},{8,9},{10,11},{12,13},{14,15},{16,17},{18,... | collective-permute-start | bytes 786440 | tf_op jit(solution)/shard_map/ppermute | solution.py:624
  8.0 13.4 %collective-permute-start = (bf16[4,128,256]{2,1,0:T(8,128)(2,1)S(1)}, bf16[4,128,256]{2,1,0:T(8,128)(2,1)S(1)}, u32[]{:S(2)}, u32[]{:S(2)}) collective-permute-start(bf16[4,128,256]{2,1,0:T(8,128)(2,1)S(1)} %get-tuple-element.43), channel_id=1, source_target_pairs={{0,4},{2,6},{4,0},{6,2},{8,12},{10,14},{12,8},{14,10},{16,20},{18,... | collective-permute-start | bytes 786440 | tf_op jit(solution)/shard_map/ppermute | solution.py:136
  9.6 11.9 %collective-permute-start.2 = (bf16[4,128,256]{2,1,0:T(8,128)(2,1)S(1)}, bf16[4,128,256]{2,1,0:T(8,128)(2,1)S(1)}, u32[]{:S(2)}, u32[]{:S(2)}) collective-permute-start(bf16[4,128,256]{2,1,0:T(8,128)(2,1)S(1)} %get-tuple-element.45), channel_id=1, source_target_pairs={{0,12},{2,14},{4,8},{6,10},{8,4},{10,6},{12,0},{14,2},{16,28},{18,... | collective-permute-start | bytes 786440 | tf_op jit(solution)/shard_map/ppermute | solution.py:136
  11.1 10.4 %collective-permute-start.3 = (bf16[128,1024]{1,0:T(8,128)(2,1)S(1)}, bf16[128,1024]{1,0:T(8,128)(2,1)S(1)}, u32[]{:S(2)}, u32[]{:S(2)}) collective-permute-start(bf16[128,1024]{1,0:T(8,128)(2,1)S(1)} %get-tuple-element.50), channel_id=1, source_target_pairs={{0,1},{2,3},{4,5},{6,7},{8,9},{10,11},{12,13},{14,15},{16,17},{18,... | collective-permute-start | bytes 786440 | tf_op jit(solution)/shard_map/ppermute | solution.py:624
  16.4 8.0 %collective-permute-start.8 = (bf16[256,512]{1,0:T(8,128)(2,1)S(1)}, bf16[256,512]{1,0:T(8,128)(2,1)S(1)}, u32[]{:S(2)}, u32[]{:S(2)}) collective-permute-start(bf16[256,512]{1,0:T(8,128)(2,1)S(1)} %get-tuple-element.59), channel_id=1, source_target_pairs={{0,1},{1,0},{2,3},{3,2},{4,5},{5,4},{6,7},{7,6},{8,9},{9,8},{10,11... | collective-permute-start | bytes 786440 | tf_op jit(solution)/shard_map/ppermute | solution.py:140
  18.3 9.4 %collective-permute-start.1 = (bf16[4,128,256]{2,1,0:T(8,128)(2,1)S(1)}, bf16[4,128,256]{2,1,0:T(8,128)(2,1)S(1)}, u32[]{:S(2)}, u32[]{:S(2)}) collective-permute-start(bf16[4,128,256]{2,1,0:T(8,128)(2,1)S(1)} %get-tuple-element.44), channel_id=1, source_target_pairs={{0,8},{2,10},{4,12},{6,14},{8,0},{10,2},{12,4},{14,6},{16,24},{18,... | collective-permute-start | bytes 786440 | tf_op jit(solution)/shard_map/ppermute | solution.py:136
  23.8 9.2 %collective-permute-start.12 = (bf16[256,512]{1,0:T(8,128)(2,1)S(1)}, bf16[256,512]{1,0:T(8,128)(2,1)S(1)}, u32[]{:S(2)}, u32[]{:S(2)}) collective-permute-start(bf16[256,512]{1,0:T(8,128)(2,1)S(1)} %get-tuple-element.61), channel_id=1, source_target_pairs={{0,1},{1,0},{2,3},{3,2},{4,5},{5,4},{6,7},{7,6},{8,9},{9,8},{10,11... | collective-permute-start | bytes 786440 | tf_op jit(solution)/shard_map/ppermute | solution.py:140
  24.5 8.5 %collective-permute-start.10 = (bf16[256,512]{1,0:T(8,128)(2,1)S(1)}, bf16[256,512]{1,0:T(8,128)(2,1)S(1)}, u32[]{:S(2)}, u32[]{:S(2)}) collective-permute-start(bf16[256,512]{1,0:T(8,128)(2,1)S(1)} %combine.2.refs_0_), channel_id=1, source_target_pairs={{0,8},{2,10},{4,12},{6,14},{8,0},{10,2},{12,4},{14,6},{16,24},{18,... | collective-permute-start | bytes 786440 | tf_op jit(solution)/shard_map/ppermute | solution.py:136
  26.2 6.8 %collective-permute-start.9 = (bf16[256,512]{1,0:T(8,128)(2,1)S(1)}, bf16[256,512]{1,0:T(8,128)(2,1)S(1)}, u32[]{:S(2)}, u32[]{:S(2)}) collective-permute-start(bf16[256,512]{1,0:T(8,128)(2,1)S(1)} %combine.2.refs_0_), channel_id=1, source_target_pairs={{0,4},{2,6},{4,0},{6,2},{8,12},{10,14},{12,8},{14,10},{16,20},{18,... | collective-permute-start | bytes 786440 | tf_op jit(solution)/shard_map/ppermute | solution.py:136
  27.7 14.3 %collective-permute-start.6 = (bf16[4,2,128,256]{3,2,1,0:T(8,128)(2,1)S(1)}, bf16[4,2,128,256]{3,2,1,0:T(8,128)(2,1)S(1)}, u32[]{:S(2)}, u32[]{:S(2)}) collective-permute-start(bf16[4,2,128,256]{3,2,1,0:T(8,128)(2,1)S(1)} %pack_normed.3.xa_ref), channel_id=1, source_target_pairs={{0,1},{1,0},{2,3},{3,2},{4,5},{5,4},{6,7},{7,6},{8,9},{9,8},{10,11... | collective-permute-start | bytes 1572872 | tf_op jit(solution)/shard_map/ppermute | solution.py:140
  29.3 7.8 %collective-permute-start.5 = (bf16[4,128,256]{2,1,0:T(8,128)(2,1)S(1)}, bf16[4,128,256]{2,1,0:T(8,128)(2,1)S(1)}, u32[]{:S(2)}, u32[]{:S(2)}) collective-permute-start(bf16[4,128,256]{2,1,0:T(8,128)(2,1)S(1)} %get-tuple-element.56), channel_id=1, source_target_pairs={{0,2},{2,0},{4,6},{6,4},{8,10},{10,8},{12,14},{14,12},{16,18},{18,... | collective-permute-start | bytes 786440 | tf_op jit(solution)/shard_map/ppermute | solution.py:136
  33.2 8.8 %collective-permute-start.14 = (bf16[256,512]{1,0:T(8,128)(2,1)S(1)}, bf16[256,512]{1,0:T(8,128)(2,1)S(1)}, u32[]{:S(2)}, u32[]{:S(2)}) collective-permute-start(bf16[256,512]{1,0:T(8,128)(2,1)S(1)} %combine.3.refs_0_.refs_4_), channel_id=1, source_target_pairs={{0,8},{2,10},{4,12},{6,14},{8,0},{10,2},{12,4},{14,6},{16,24},{18,... | collective-permute-start | bytes 786440 | tf_op jit(solution)/shard_map/ppermute | solution.py:136
  35.0 7.0 %collective-permute-start.11 = (bf16[256,512]{1,0:T(8,128)(2,1)S(1)}, bf16[256,512]{1,0:T(8,128)(2,1)S(1)}, u32[]{:S(2)}, u32[]{:S(2)}) collective-permute-start(bf16[256,512]{1,0:T(8,128)(2,1)S(1)} %collective-permute-done.10.rest_1_.refs_2_), channel_id=1, source_target_pairs={{0,4},{2,6},{4,0},{6,2},{8,12},{10,14},{12,8},{14,10},{16,20},{18,... | collective-permute-start | bytes 786440 | tf_op jit(solution)/shard_map/ppermute | solution.py:136
  36.5 8.2 %collective-permute-start.13 = (bf16[256,512]{1,0:T(8,128)(2,1)S(1)}, bf16[256,512]{1,0:T(8,128)(2,1)S(1)}, u32[]{:S(2)}, u32[]{:S(2)}) collective-permute-start(bf16[256,512]{1,0:T(8,128)(2,1)S(1)} %combine.3.refs_0_.refs_4_), channel_id=1, source_target_pairs={{0,4},{2,6},{4,0},{6,2},{8,12},{10,14},{12,8},{14,10},{16,20},{18,... | collective-permute-start | bytes 786440 | tf_op jit(solution)/shard_map/ppermute | solution.py:136
  42.7 2.0 %collective-permute-start.16 = (f32[64,512]{1,0:T(8,128)S(1)}, f32[64,512]{1,0:T(8,128)S(1)}, u32[]{:S(2)}, u32[]{:S(2)}) collective-permute-start(f32[64,512]{1,0:T(8,128)S(1)} %get-tuple-element.63), channel_id=1, source_target_pairs={{0,2},{2,0},{4,6},{6,4},{8,10},{10,8},{12,14},{14,12},{16,18},{18,... | collective-permute-start | bytes 393224 | tf_op jit(solution)/shard_map/ppermute | solution.py:136
  42.8 1.9 %collective-permute-start.17 = (f32[64,512]{1,0:T(8,128)S(1)}, f32[64,512]{1,0:T(8,128)S(1)}, u32[]{:S(2)}, u32[]{:S(2)}) collective-permute-start(f32[64,512]{1,0:T(8,128)S(1)} %get-tuple-element.64), channel_id=1, source_target_pairs={{0,2},{2,0},{4,6},{6,4},{8,10},{10,8},{12,14},{14,12},{16,18},{18,... | collective-permute-start | bytes 393224 | tf_op jit(solution)/shard_map/ppermute | solution.py:136
  43.3 1.4 %collective-permute-start.18 = (f32[64,512]{1,0:T(8,128)S(1)}, f32[64,512]{1,0:T(8,128)S(1)}, u32[]{:S(2)}, u32[]{:S(2)}) collective-permute-start(f32[64,512]{1,0:T(8,128)S(1)} %get-tuple-element.65), channel_id=1, source_target_pairs={{0,2},{2,0},{4,6},{6,4},{8,10},{10,8},{12,14},{14,12},{16,18},{18,... | collective-permute-start | bytes 393224 | tf_op jit(solution)/shard_map/ppermute | solution.py:136
  43.4 1.5 %collective-permute-start.19 = (f32[64,512]{1,0:T(8,128)S(1)}, f32[64,512]{1,0:T(8,128)S(1)}, u32[]{:S(2)}, u32[]{:S(2)}) collective-permute-start(f32[64,512]{1,0:T(8,128)S(1)} %get-tuple-element.66), channel_id=1, source_target_pairs={{0,2},{2,0},{4,6},{6,4},{8,10},{10,8},{12,14},{14,12},{16,18},{18,... | collective-permute-start | bytes 393224 | tf_op jit(solution)/shard_map/ppermute | solution.py:136
  45.0 9.5 %collective-permute-start.20 = (bf16[1024,512]{1,0:T(8,128)(2,1)S(1)}, bf16[1024,512]{1,0:T(8,128)(2,1)S(1)}, u32[]{:S(2)}, u32[]{:S(2)}) collective-permute-start(bf16[1024,512]{1,0:T(8,128)(2,1)S(1)} %join_places.2), channel_id=1, source_target_pairs={{0,2},{2,0},{4,6},{6,4},{8,10},{10,8},{12,14},{14,12},{16,18},{18,... | collective-permute-start | bytes 3145736 | tf_op jit(solution)/shard_map/ppermute | solution.py:136
  45.4 14.1 %collective-permute-start.7 = (bf16[4,2,128,256]{3,2,1,0:T(8,128)(2,1)S(1)}, bf16[4,2,128,256]{3,2,1,0:T(8,128)(2,1)S(1)}, u32[]{:S(2)}, u32[]{:S(2)}) collective-permute-start(bf16[4,2,128,256]{3,2,1,0:T(8,128)(2,1)S(1)} %join_cores.1.xa_ref), channel_id=1, source_target_pairs={{0,1},{1,0},{2,3},{3,2},{4,5},{5,4},{6,7},{7,6},{8,9},{9,8},{10,11... | collective-permute-start | bytes 1572872 | tf_op jit(solution)/shard_map/ppermute | solution.py:140
  46.4 8.1 %collective-permute-start.15 = (bf16[256,512]{1,0:T(8,128)(2,1)S(1)}, bf16[256,512]{1,0:T(8,128)(2,1)S(1)}, u32[]{:S(2)}, u32[]{:S(2)}) collective-permute-start(bf16[256,512]{1,0:T(8,128)(2,1)S(1)} %collective-permute-done.14.refs_4_.refs_2_.refs_6_), channel_id=1, source_target_pairs={{0,4},{2,6},{4,0},{6,2},{8,12},{10,14},{12,8},{14,10},{16,20},{18,... | collective-permute-start | bytes 786440 | tf_op jit(solution)/shard_map/ppermute | solution.py:136
  48.0 14.4 %collective-permute-start.25 = (bf16[256,512]{1,0:T(8,128)(2,1)S(1)}, bf16[256,512]{1,0:T(8,128)(2,1)S(1)}, u32[]{:S(2)}, u32[]{:S(2)}) collective-permute-start(bf16[256,512]{1,0:T(8,128)(2,1)S(1)} %add_round.2.refs_4_), channel_id=1, source_target_pairs={{0,16},{2,18},{4,20},{6,22},{8,24},{10,26},{12,28},{14,30},{16,0},... | collective-permute-start | bytes 786440 | tf_op jit(solution)/shard_map/ppermute | solution.py:136
  55.2 4.3 %collective-permute-start.21 = (f32[64,512]{1,0:T(8,128)S(1)}, f32[64,512]{1,0:T(8,128)S(1)}, u32[]{:S(2)}, u32[]{:S(2)}) collective-permute-start(f32[64,512]{1,0:T(8,128)S(1)} %get-tuple-element.68), channel_id=1, source_target_pairs={{0,2},{2,0},{4,6},{6,4},{8,10},{10,8},{12,14},{14,12},{16,18},{18,... | collective-permute-start | bytes 393224 | tf_op jit(solution)/shard_map/ppermute | solution.py:136
  55.3 4.2 %collective-permute-start.22 = (f32[64,512]{1,0:T(8,128)S(1)}, f32[64,512]{1,0:T(8,128)S(1)}, u32[]{:S(2)}, u32[]{:S(2)}) collective-permute-start(f32[64,512]{1,0:T(8,128)S(1)} %get-tuple-element.69), channel_id=1, source_target_pairs={{0,2},{2,0},{4,6},{6,4},{8,10},{10,8},{12,14},{14,12},{16,18},{18,... | collective-permute-start | bytes 393224 | tf_op jit(solution)/shard_map/ppermute | solution.py:136
  55.8 3.7 %collective-permute-start.23 = (f32[64,512]{1,0:T(8,128)S(1)}, f32[64,512]{1,0:T(8,128)S(1)}, u32[]{:S(2)}, u32[]{:S(2)}) collective-permute-start(f32[64,512]{1,0:T(8,128)S(1)} %get-tuple-element.70), channel_id=1, source_target_pairs={{0,2},{2,0},{4,6},{6,4},{8,10},{10,8},{12,14},{14,12},{16,18},{18,... | collective-permute-start | bytes 393224 | tf_op jit(solution)/shard_map/ppermute | solution.py:136
  59.5 1.3 %collective-permute-start.24 = (f32[64,512]{1,0:T(8,128)S(1)}, f32[64,512]{1,0:T(8,128)S(1)}, u32[]{:S(2)}, u32[]{:S(2)}) collective-permute-start(f32[64,512]{1,0:T(8,128)S(1)} %get-tuple-element.71), channel_id=1, source_target_pairs={{0,2},{2,0},{4,6},{6,4},{8,10},{10,8},{12,14},{14,12},{16,18},{18,... | collective-permute-start | bytes 393224 | tf_op jit(solution)/shard_map/ppermute | solution.py:136
  62.4 2.7 %collective-permute-start.26 = (bf16[1024,512]{1,0:T(8,128)(2,1)S(1)}, bf16[1024,512]{1,0:T(8,128)(2,1)S(1)}, u32[]{:S(2)}, u32[]{:S(2)}) collective-permute-start(bf16[1024,512]{1,0:T(8,128)(2,1)S(1)} %join_places.3), channel_id=1, source_target_pairs={{0,2},{2,0},{4,6},{6,4},{8,10},{10,8},{12,14},{14,12},{16,18},{18,... | collective-permute-start | bytes 3145736 | tf_op jit(solution)/shard_map/ppermute | solution.py:136
  62.5 15.2 %collective-permute-start.27 = (bf16[256,512]{1,0:T(8,128)(2,1)S(1)}, bf16[256,512]{1,0:T(8,128)(2,1)S(1)}, u32[]{:S(2)}, u32[]{:S(2)}) collective-permute-start(bf16[256,512]{1,0:T(8,128)(2,1)S(1)} %add_round.3.refs_4_.refs_13_), channel_id=1, source_target_pairs={{0,16},{2,18},{4,20},{6,22},{8,24},{10,26},{12,28},{14,30},{16,0},... | collective-permute-start | bytes 786440 | tf_op jit(solution)/shard_map/ppermute | solution.py:136

commit v6 on v5

--- a/solution.py
+++ b/solution.py
@@ -649,7 +649,9 @@
     cross = flip(cross, CORE)
 
     recv_half, recv_core = [], []
-    after, fence = [grads[1][2], cross], [grads[1][1]]
+    home = join_cores(same, cross, [away_other])
+    home_other = swap_seq(home)
+    after, fence = [grads[1][2], cross], [grads[1][1], home]
     for part in grads:
         own, *sends = project_away(away, away_other, part, after)
         total = add_round(own, [flip(send, CORE) for send in sends], fence)
@@ -657,8 +659,6 @@
         recv_core.append(flip(gathered, CORE))
         recv_half.append(flip(total, ZHIGH))
         if part is grads[0]:
-            home = join_cores(same, cross, [away_other])
-            home_other = swap_seq(home)
             after, fence = recv_core[:], [home_other]
     keep, query_grad, *sums = project_home(
         seq_at, (home, home_other), grads, recv_core, query_grads, recv_half[:-1], [total]

time: 79 us -> 78.8 us (level)
  no operation moved by 1% of the time
where the time goes in v6:
time: 78.8 us; the launch traced here: 78.6 us
  waiting for transfers between devices  32.4 us (41%)
  starting transfers between devices  31.4 us (40%)
  Pallas kernels  13.8 us (18%)
  between operations  1 us (1%)
    ppermute x22, waiting for transfers between devices, flip(): return lax.ppermute(array, 'dp', [(i, i ^ mask) for i in range(16)])  20.3 us
    ppermute x22, starting transfers between devices, flip(): return lax.ppermute(array, 'dp', [(i, i ^ mask) for i in range(16)])  20.2 us
    ppermute x4, waiting for transfers between devices, swap_seq(): return lax.ppermute(array, 'seq', [(0, 1), (1, 0)])  12.2 us
    ppermute x2, starting transfers between devices, cube_local(): kv_recv = [lax.ppermute(part, 'seq', [(0, 1)]) for part in kv]  6.18 us
    ppermute x4, starting transfers between devices, swap_seq(): return lax.ppermute(array, 'seq', [(0, 1), (1, 0)])  4.94 us
    pallas_call x2, Pallas kernels, attention(): pl.pallas_call(body, out_shape=[pltpu.VMEM((2, rows, wide), BF), pltpu.VM...  4.76 us
    pallas_call x1, Pallas kernels, project_home(): pl.pallas_call(body, out_shape=[pltpu.VMEM((share, (chunks - ready) * wid...  2.07 us
    pallas_call x1, Pallas kernels, stage(): pl.pallas_call(body, out_shape=[pltpu.VMEM(one.shape, one.dtype) for one...  1.61 us
  transfers between devices with their start and end apart: 28, of which 11 were waited for; matrix products, arithmetic and copies ran while one was open for 0% of the time, Pallas kernels for 15%

profile of v6, /device:TPU:0, one launch (start us, length us, event | category | flops | bytes accessed | tf_op | source)
XLA Modules:
  0.0 78.6 jit_solution(3668626089976360697)
XLA Ops:
  0.6 1.1 %prepare_kv.1 = (bf16[128,1024]{1,0:T(8,128)(2,1)S(1)}, bf16[128,1024]{1,0:T(8,128)(2,1)S(1)}, bf16[128,1024]{1,0:T(8,128)(2,1)S(1)}, bf16[128,1024]{1,0:T(8,128)(2,1)S(1)}) custom-call(bf16[128,1024]{1,0:T(8,128)(2,1)} %k_hbm.1, bf16[128,1024]{1,0:T(8,128)(2,1)} %v_hbm.1), custom_call_target="tpu_custom_call" | custom-call | tf_op jit(solution)/shard_map/prepare_kv/pallas_call | solution.py:198
  1.7 4.9 %collective-permute-start.4 = (bf16[128,1024]{1,0:T(8,128)(2,1)S(1)}, bf16[128,1024]{1,0:T(8,128)(2,1)S(1)}, u32[]{:S(2)}, u32[]{:S(2)}) collective-permute-start(bf16[128,1024]{1,0:T(8,128)(2,1)S(1)} %get-tuple-element.41.after_ref), channel_id=1, source_target_pairs={{0,1},{2,3},{4,5},{6,7},{8,9},{10,11},{12,13},{14,15},{16,17},{18,... | collective-permute-start | bytes 786440 | tf_op jit(solution)/shard_map/ppermute | solution.py:624
  6.6 1.4 %prepare_normed.1 = (bf16[4,128,256]{2,1,0:T(8,128)(2,1)S(1)}, bf16[4,128,256]{2,1,0:T(8,128)(2,1)S(1)}, bf16[4,128,256]{2,1,0:T(8,128)(2,1)S(1)}, bf16[4,128,256]{2,1,0:T(8,128)(2,1)S(1)}) custom-call(s32[1]{0:T(128)} %bitcast.1.me_ref, bf16[128,4096]{1,0:T(8,128)(2,1)} %x_hbm.1, bf16[128,1024]{1,0:T(8,128)(2,1)S(1)} %get-tuple-element.41.after_ref), custom_call_target="tpu_custom_call" | custom-call | tf_op jit(solution)/shard_map/prepare_normed/pallas_call | solution.py:222
  8.0 1.6 %collective-permute-start = (bf16[4,128,256]{2,1,0:T(8,128)(2,1)S(1)}, bf16[4,128,256]{2,1,0:T(8,128)(2,1)S(1)}, u32[]{:S(2)}, u32[]{:S(2)}) collective-permute-start(bf16[4,128,256]{2,1,0:T(8,128)(2,1)S(1)} %get-tuple-element.43), channel_id=1, source_target_pairs={{0,4},{2,6},{4,0},{6,2},{8,12},{10,14},{12,8},{14,10},{16,20},{18,... | collective-permute-start | bytes 786440 | tf_op jit(solution)/shard_map/ppermute | solution.py:136
  9.6 1.5 %collective-permute-start.2 = (bf16[4,128,256]{2,1,0:T(8,128)(2,1)S(1)}, bf16[4,128,256]{2,1,0:T(8,128)(2,1)S(1)}, u32[]{:S(2)}, u32[]{:S(2)}) collective-permute-start(bf16[4,128,256]{2,1,0:T(8,128)(2,1)S(1)} %get-tuple-element.45), channel_id=1, source_target_pairs={{0,12},{2,14},{4,8},{6,10},{8,4},{10,6},{12,0},{14,2},{16,28},{18,... | collective-permute-start | bytes 786440 | tf_op jit(solution)/shard_map/ppermute | solution.py:136
  11.1 1.3 %collective-permute-start.3 = (bf16[128,1024]{1,0:T(8,128)(2,1)S(1)}, bf16[128,1024]{1,0:T(8,128)(2,1)S(1)}, u32[]{:S(2)}, u32[]{:S(2)}) collective-permute-start(bf16[128,1024]{1,0:T(8,128)(2,1)S(1)} %get-tuple-element.50), channel_id=1, source_target_pairs={{0,1},{2,3},{4,5},{6,7},{8,9},{10,11},{12,13},{14,15},{16,17},{18,... | collective-permute-start | bytes 786440 | tf_op jit(solution)/shard_map/ppermute | solution.py:624
  12.4 1.6 %stage.1 = (bf16[128,4096]{1,0:T(8,128)(2,1)S(1)}, bf16[128,4096]{1,0:T(8,128)(2,1)S(1)}, f32[256,128]{1,0:T(8,128)S(1)}, f32[256,128]{1,0:T(8,128)S(1)}) custom-call(bf16[128,4096]{1,0:T(8,128)(2,1)} %refs_0_.1, bf16[128,4096]{1,0:T(8,128)(2,1)} %refs_1_.1, f32[256,128]{1,0:T(8,128)} %constant.12.clone.refs_2_, f32[256,128]{1,0:T(8,128)} %constant.13.clone.refs_3_), custom_call_target="tpu_custom_call" | custom-call | tf_op jit(solution)/shard_map/stage/pallas_call | solution.py:244
  14.0 2.4 %attention.2 = (bf16[2,128,1024]{2,1,0:T(8,128)(2,1)S(1)}, f32[128,512]{1,0:T(8,128)S(1)}, bf16[128,512]{1,0:T(8,128)(2,1)S(1)}, bf16[256,512]{1,0:T(8,128)(2,1)S(1)}) custom-call(s32[1]{0:T(128)} %bitcast.at_ref, bf16[128,4096]{1,0:T(8,128)(2,1)S(1)} %get-tuple-element.46.q_ref, bf16[128,4096]{1,0:T(8,128)(2,1)S(1)} %get-tuple-element.47.g_ref, ...), custom_call_target="tpu_custom_call" | custom-call | tf_op jit(solution)/shard_map/attention/pallas_call | solution.py:434
  16.4 1.9 %collective-permute-start.8 = (bf16[256,512]{1,0:T(8,128)(2,1)S(1)}, bf16[256,512]{1,0:T(8,128)(2,1)S(1)}, u32[]{:S(2)}, u32[]{:S(2)}) collective-permute-start(bf16[256,512]{1,0:T(8,128)(2,1)S(1)} %get-tuple-element.59), channel_id=1, source_target_pairs={{0,1},{1,0},{2,3},{3,2},{4,5},{5,4},{6,7},{7,6},{8,9},{9,8},{10,11... | collective-permute-start | bytes 786440 | tf_op jit(solution)/shard_map/ppermute | solution.py:140
  18.3 2.4 %collective-permute-start.1 = (bf16[4,128,256]{2,1,0:T(8,128)(2,1)S(1)}, bf16[4,128,256]{2,1,0:T(8,128)(2,1)S(1)}, u32[]{:S(2)}, u32[]{:S(2)}) collective-permute-start(bf16[4,128,256]{2,1,0:T(8,128)(2,1)S(1)} %get-tuple-element.44), channel_id=1, source_target_pairs={{0,8},{2,10},{4,12},{6,14},{8,0},{10,2},{12,4},{14,6},{16,24},{18,... | collective-permute-start | bytes 786440 | tf_op jit(solution)/shard_map/ppermute | solution.py:136
  20.7 0.7 collective-permute-done.rest_0_.refs_1_
  21.5 2.4 %attention.3 = (bf16[2,128,1024]{2,1,0:T(8,128)(2,1)S(1)}, f32[128,512]{1,0:T(8,128)S(1)}, bf16[128,512]{1,0:T(8,128)(2,1)S(1)}, bf16[256,512]{1,0:T(8,128)(2,1)S(1)}) custom-call(s32[1]{0:T(128)} %bitcast.at_ref, bf16[128,4096]{1,0:T(8,128)(2,1)S(1)} %get-tuple-element.46.q_ref, bf16[128,4096]{1,0:T(8,128)(2,1)S(1)} %get-tuple-element.47.g_ref, ...), custom_call_target="tpu_custom_call" | custom-call | tf_op jit(solution)/shard_map/attention/pallas_call | solution.py:434
  23.8 0.7 collective-permute-start.12
  24.5 1.6 %collective-permute-start.10 = (bf16[256,512]{1,0:T(8,128)(2,1)S(1)}, bf16[256,512]{1,0:T(8,128)(2,1)S(1)}, u32[]{:S(2)}, u32[]{:S(2)}) collective-permute-start(bf16[256,512]{1,0:T(8,128)(2,1)S(1)} %combine.2.refs_0_), channel_id=1, source_target_pairs={{0,8},{2,10},{4,12},{6,14},{8,0},{10,2},{12,4},{14,6},{16,24},{18,... | collective-permute-start | bytes 786440 | tf_op jit(solution)/shard_map/ppermute | solution.py:136
  26.2 1.5 %collective-permute-start.9 = (bf16[256,512]{1,0:T(8,128)(2,1)S(1)}, bf16[256,512]{1,0:T(8,128)(2,1)S(1)}, u32[]{:S(2)}, u32[]{:S(2)}) collective-permute-start(bf16[256,512]{1,0:T(8,128)(2,1)S(1)} %combine.2.refs_0_), channel_id=1, source_target_pairs={{0,4},{2,6},{4,0},{6,2},{8,12},{10,14},{12,8},{14,10},{16,20},{18,... | collective-permute-start | bytes 786440 | tf_op jit(solution)/shard_map/ppermute | solution.py:136
  27.7 1.5 %collective-permute-start.6 = (bf16[4,2,128,256]{3,2,1,0:T(8,128)(2,1)S(1)}, bf16[4,2,128,256]{3,2,1,0:T(8,128)(2,1)S(1)}, u32[]{:S(2)}, u32[]{:S(2)}) collective-permute-start(bf16[4,2,128,256]{3,2,1,0:T(8,128)(2,1)S(1)} %pack_normed.3.xa_ref), channel_id=1, source_target_pairs={{0,1},{1,0},{2,3},{3,2},{4,5},{5,4},{6,7},{7,6},{8,9},{9,8},{10,11... | collective-permute-start | bytes 1572872 | tf_op jit(solution)/shard_map/ppermute | solution.py:140
  29.3 0.1 collective-permute-start.5
  29.3 3.7 %collective-permute-done.12.recv_ref = bf16[256,512]{1,0:T(8,128)(2,1)S(1)} collective-permute-done((bf16[256,512]{1,0:T(8,128)(2,1)S(1)}, bf16[256,512]{1,0:T(8,128)(2,1)S(1)}, u32[]{:S(2)}, u32[]{:S(2)}) %collective-permute-start.12) | collective-permute-done | bytes 262176 | tf_op jit(solution)/shard_map/ppermute | solution.py:140
  33.0 0.2 combine.3.refs_0_.refs_4_
  33.2 1.8 %collective-permute-start.14 = (bf16[256,512]{1,0:T(8,128)(2,1)S(1)}, bf16[256,512]{1,0:T(8,128)(2,1)S(1)}, u32[]{:S(2)}, u32[]{:S(2)}) collective-permute-start(bf16[256,512]{1,0:T(8,128)(2,1)S(1)} %combine.3.refs_0_.refs_4_), channel_id=1, source_target_pairs={{0,8},{2,10},{4,12},{6,14},{8,0},{10,2},{12,4},{14,6},{16,24},{18,... | collective-permute-start | bytes 786440 | tf_op jit(solution)/shard_map/ppermute | solution.py:136
  35.0 1.5 %collective-permute-start.11 = (bf16[256,512]{1,0:T(8,128)(2,1)S(1)}, bf16[256,512]{1,0:T(8,128)(2,1)S(1)}, u32[]{:S(2)}, u32[]{:S(2)}) collective-permute-start(bf16[256,512]{1,0:T(8,128)(2,1)S(1)} %collective-permute-done.10.rest_1_.refs_2_), channel_id=1, source_target_pairs={{0,4},{2,6},{4,0},{6,2},{8,12},{10,14},{12,8},{14,10},{16,20},{18,... | collective-permute-start | bytes 786440 | tf_op jit(solution)/shard_map/ppermute | solution.py:136
  36.5 0.5 collective-permute-start.13
  37.1 4.9 %collective-permute-done.6.refs_0_.xb_ref = bf16[4,2,128,256]{3,2,1,0:T(8,128)(2,1)S(1)} collective-permute-done((bf16[4,2,128,256]{3,2,1,0:T(8,128)(2,1)S(1)}, bf16[4,2,128,256]{3,2,1,0:T(8,128)(2,1)S(1)}, u32[]{:S(2)}, u32[]{:S(2)}) %collective-permute-start.6) | collective-permute-done | bytes 524320 | tf_op jit(solution)/shard_map/ppermute | solution.py:140
  42.0 0.7 project_away.2
  42.7 0.1 collective-permute-start.16
  42.8 0.5 collective-permute-start.17
  43.3 0.1 collective-permute-start.18
  43.4 0.4 collective-permute-start.19
  43.9 0.8 %collective-permute-done.13.refs_4_.refs_1_.refs_5_ = bf16[256,512]{1,0:T(8,128)(2,1)S(1)} collective-permute-done((bf16[256,512]{1,0:T(8,128)(2,1)S(1)}, bf16[256,512]{1,0:T(8,128)(2,1)S(1)}, u32[]{:S(2)}, u32[]{:S(2)}) %collective-permute-start.13) | collective-permute-done | bytes 262176 | tf_op jit(solution)/shard_map/ppermute | solution.py:136
  44.7 0.1 collective-permute-done.19.refs_3_
  45.0 0.4 collective-permute-start.20
  45.4 0.9 %collective-permute-start.7 = (bf16[4,2,128,256]{3,2,1,0:T(8,128)(2,1)S(1)}, bf16[4,2,128,256]{3,2,1,0:T(8,128)(2,1)S(1)}, u32[]{:S(2)}, u32[]{:S(2)}) collective-permute-start(bf16[4,2,128,256]{3,2,1,0:T(8,128)(2,1)S(1)} %join_cores.1.refs_5_.xa_ref), channel_id=1, source_target_pairs={{0,1},{1,0},{2,3},{3,2},{4,5},{5,4},{6,7},{7,6},{8,9},{9,8},{10,11... | collective-permute-start | bytes 1572872 | tf_op jit(solution)/shard_map/ppermute | solution.py:140
  46.3 1.6 %collective-permute-start.15 = (bf16[256,512]{1,0:T(8,128)(2,1)S(1)}, bf16[256,512]{1,0:T(8,128)(2,1)S(1)}, u32[]{:S(2)}, u32[]{:S(2)}) collective-permute-start(bf16[256,512]{1,0:T(8,128)(2,1)S(1)} %collective-permute-done.14.refs_4_.refs_2_.refs_6_), channel_id=1, source_target_pairs={{0,4},{2,6},{4,0},{6,2},{8,12},{10,14},{12,8},{14,10},{16,20},{18,... | collective-permute-start | bytes 786440 | tf_op jit(solution)/shard_map/ppermute | solution.py:136
  47.9 2.6 %collective-permute-start.25 = (bf16[256,512]{1,0:T(8,128)(2,1)S(1)}, bf16[256,512]{1,0:T(8,128)(2,1)S(1)}, u32[]{:S(2)}, u32[]{:S(2)}) collective-permute-start(bf16[256,512]{1,0:T(8,128)(2,1)S(1)} %add_round.2.refs_4_), channel_id=1, source_target_pairs={{0,16},{2,18},{4,20},{6,22},{8,24},{10,26},{12,28},{14,30},{16,0},... | collective-permute-start | bytes 786440 | tf_op jit(solution)/shard_map/ppermute | solution.py:136
  50.5 3.9 %collective-permute-done.15.refs_3_.refs_7_ = bf16[256,512]{1,0:T(8,128)(2,1)S(1)} collective-permute-done((bf16[256,512]{1,0:T(8,128)(2,1)S(1)}, bf16[256,512]{1,0:T(8,128)(2,1)S(1)}, u32[]{:S(2)}, u32[]{:S(2)}) %collective-permute-start.15) | collective-permute-done | bytes 262176 | tf_op jit(solution)/shard_map/ppermute | solution.py:136
  54.4 0.7 project_away.3
  55.1 0.1 collective-permute-start.21
  55.2 0.5 collective-permute-start.22
  55.7 0.1 collective-permute-start.23
  55.8 3.6 %collective-permute-done.7.refs_4_.xb_ref = bf16[4,2,128,256]{3,2,1,0:T(8,128)(2,1)S(1)} collective-permute-done((bf16[4,2,128,256]{3,2,1,0:T(8,128)(2,1)S(1)}, bf16[4,2,128,256]{3,2,1,0:T(8,128)(2,1)S(1)}, u32[]{:S(2)}, u32[]{:S(2)}) %collective-permute-start.7) | collective-permute-done | bytes 524320 | tf_op jit(solution)/shard_map/ppermute | solution.py:140
  59.4 1.3 %collective-permute-done.24.refs_3_ = f32[64,512]{1,0:T(8,128)S(1)} collective-permute-done((f32[64,512]{1,0:T(8,128)S(1)}, f32[64,512]{1,0:T(8,128)S(1)}, u32[]{:S(2)}, u32[]{:S(2)}) %collective-permute-start.24) | collective-permute-done | bytes 131104 | tf_op jit(solution)/shard_map/ppermute | solution.py:136
  60.8 1.4 %collective-permute-done.25.refs_5_.refs_12_ = bf16[256,512]{1,0:T(8,128)(2,1)S(1)} collective-permute-done((bf16[256,512]{1,0:T(8,128)(2,1)S(1)}, bf16[256,512]{1,0:T(8,128)(2,1)S(1)}, u32[]{:S(2)}, u32[]{:S(2)}) %collective-permute-start.25) | collective-permute-done | bytes 262176 | tf_op jit(solution)/shard_map/ppermute | solution.py:136
  62.3 0.1 collective-permute-start.26
  62.4 1.3 %collective-permute-start.27 = (bf16[256,512]{1,0:T(8,128)(2,1)S(1)}, bf16[256,512]{1,0:T(8,128)(2,1)S(1)}, u32[]{:S(2)}, u32[]{:S(2)}) collective-permute-start(bf16[256,512]{1,0:T(8,128)(2,1)S(1)} %add_round.3.refs_4_.refs_13_), channel_id=1, source_target_pairs={{0,16},{2,18},{4,20},{6,22},{8,24},{10,26},{12,28},{14,30},{16,0},... | collective-permute-start | bytes 786440 | tf_op jit(solution)/shard_map/ppermute | solution.py:136
  63.7 1.3 %collective-permute-done.26.refs_9_ = bf16[1024,512]{1,0:T(8,128)(2,1)S(1)} collective-permute-done((bf16[1024,512]{1,0:T(8,128)(2,1)S(1)}, bf16[1024,512]{1,0:T(8,128)(2,1)S(1)}, u32[]{:S(2)}, u32[]{:S(2)}) %collective-permute-start.26) | collective-permute-done | bytes 1048608 | tf_op jit(solution)/shard_map/ppermute | solution.py:136
  65.0 2.1 %project_home.1 = (f32[256,512]{1,0:T(8,128)S(1)}, bf16[128,4096]{1,0:T(8,128)(2,1)}, f32[256,512]{1,0:T(8,128)}, f32[256,512]{1,0:T(8,128)}) custom-call(s32[1]{0:T(128)} %bitcast.at_ref, bf16[4,2,128,256]{3,2,1,0:T(8,128)(2,1)S(1)} %join_cores.1.refs_5_.xa_ref, bf16[4,2,128,256]{3,2,1,0:T(8,128)(2,1)S(1)} %collective-permute-done.7.refs_4_.xb_ref, ...), custom_call_target="tpu_custom_call" | custom-call | tf_op jit(solution)/shard_map/project_home/pallas_call | solution.py:566
  67.1 10.5 %collective-permute-done.27.half_ref = bf16[256,512]{1,0:T(8,128)(2,1)S(1)} collective-permute-done((bf16[256,512]{1,0:T(8,128)(2,1)S(1)}, bf16[256,512]{1,0:T(8,128)(2,1)S(1)}, u32[]{:S(2)}, u32[]{:S(2)}) %collective-permute-start.27) | collective-permute-done | bytes 262176 | tf_op jit(solution)/shard_map/ppermute | solution.py:136
  77.6 0.8 %finish.1 = (f32[256,512]{1,0:T(8,128)}, f32[256,512]{1,0:T(8,128)}) custom-call(f32[256,512]{1,0:T(8,128)S(1)} %get-tuple-element.74.keep_ref, bf16[256,512]{1,0:T(8,128)(2,1)S(1)} %collective-permute-done.27.half_ref, f32[256,512]{1,0:T(8,128)} %get-tuple-element.75.refs_0_, ...), custom_call_target="tpu_custom_call", output_to_operand_aliasing={{0}: (2, {}), {1}: (3, {})} | custom-call | tf_op jit(solution)/shard_map/finish/pallas_call | solution.py:604
  (26 shorter events, 0.4 us)
Async XLA Ops:
  1.7 12.3 %collective-permute-start.4 = (bf16[128,1024]{1,0:T(8,128)(2,1)S(1)}, bf16[128,1024]{1,0:T(8,128)(2,1)S(1)}, u32[]{:S(2)}, u32[]{:S(2)}) collective-permute-start(bf16[128,1024]{1,0:T(8,128)(2,1)S(1)} %get-tuple-element.41.after_ref), channel_id=1, source_target_pairs={{0,1},{2,3},{4,5},{6,7},{8,9},{10,11},{12,13},{14,15},{16,17},{18,... | collective-permute-start | bytes 786440 | tf_op jit(solution)/shard_map/ppermute | solution.py:624
  8.0 13.4 %collective-permute-start = (bf16[4,128,256]{2,1,0:T(8,128)(2,1)S(1)}, bf16[4,128,256]{2,1,0:T(8,128)(2,1)S(1)}, u32[]{:S(2)}, u32[]{:S(2)}) collective-permute-start(bf16[4,128,256]{2,1,0:T(8,128)(2,1)S(1)} %get-tuple-element.43), channel_id=1, source_target_pairs={{0,4},{2,6},{4,0},{6,2},{8,12},{10,14},{12,8},{14,10},{16,20},{18,... | collective-permute-start | bytes 786440 | tf_op jit(solution)/shard_map/ppermute | solution.py:136
  9.6 11.9 %collective-permute-start.2 = (bf16[4,128,256]{2,1,0:T(8,128)(2,1)S(1)}, bf16[4,128,256]{2,1,0:T(8,128)(2,1)S(1)}, u32[]{:S(2)}, u32[]{:S(2)}) collective-permute-start(bf16[4,128,256]{2,1,0:T(8,128)(2,1)S(1)} %get-tuple-element.45), channel_id=1, source_target_pairs={{0,12},{2,14},{4,8},{6,10},{8,4},{10,6},{12,0},{14,2},{16,28},{18,... | collective-permute-start | bytes 786440 | tf_op jit(solution)/shard_map/ppermute | solution.py:136
  11.1 10.4 %collective-permute-start.3 = (bf16[128,1024]{1,0:T(8,128)(2,1)S(1)}, bf16[128,1024]{1,0:T(8,128)(2,1)S(1)}, u32[]{:S(2)}, u32[]{:S(2)}) collective-permute-start(bf16[128,1024]{1,0:T(8,128)(2,1)S(1)} %get-tuple-element.50), channel_id=1, source_target_pairs={{0,1},{2,3},{4,5},{6,7},{8,9},{10,11},{12,13},{14,15},{16,17},{18,... | collective-permute-start | bytes 786440 | tf_op jit(solution)/shard_map/ppermute | solution.py:624
  16.4 8.0 %collective-permute-start.8 = (bf16[256,512]{1,0:T(8,128)(2,1)S(1)}, bf16[256,512]{1,0:T(8,128)(2,1)S(1)}, u32[]{:S(2)}, u32[]{:S(2)}) collective-permute-start(bf16[256,512]{1,0:T(8,128)(2,1)S(1)} %get-tuple-element.59), channel_id=1, source_target_pairs={{0,1},{1,0},{2,3},{3,2},{4,5},{5,4},{6,7},{7,6},{8,9},{9,8},{10,11... | collective-permute-start | bytes 786440 | tf_op jit(solution)/shard_map/ppermute | solution.py:140
  18.3 9.4 %collective-permute-start.1 = (bf16[4,128,256]{2,1,0:T(8,128)(2,1)S(1)}, bf16[4,128,256]{2,1,0:T(8,128)(2,1)S(1)}, u32[]{:S(2)}, u32[]{:S(2)}) collective-permute-start(bf16[4,128,256]{2,1,0:T(8,128)(2,1)S(1)} %get-tuple-element.44), channel_id=1, source_target_pairs={{0,8},{2,10},{4,12},{6,14},{8,0},{10,2},{12,4},{14,6},{16,24},{18,... | collective-permute-start | bytes 786440 | tf_op jit(solution)/shard_map/ppermute | solution.py:136
  23.8 9.2 %collective-permute-start.12 = (bf16[256,512]{1,0:T(8,128)(2,1)S(1)}, bf16[256,512]{1,0:T(8,128)(2,1)S(1)}, u32[]{:S(2)}, u32[]{:S(2)}) collective-permute-start(bf16[256,512]{1,0:T(8,128)(2,1)S(1)} %get-tuple-element.61), channel_id=1, source_target_pairs={{0,1},{1,0},{2,3},{3,2},{4,5},{5,4},{6,7},{7,6},{8,9},{9,8},{10,11... | collective-permute-start | bytes 786440 | tf_op jit(solution)/shard_map/ppermute | solution.py:140
  24.5 8.5 %collective-permute-start.10 = (bf16[256,512]{1,0:T(8,128)(2,1)S(1)}, bf16[256,512]{1,0:T(8,128)(2,1)S(1)}, u32[]{:S(2)}, u32[]{:S(2)}) collective-permute-start(bf16[256,512]{1,0:T(8,128)(2,1)S(1)} %combine.2.refs_0_), channel_id=1, source_target_pairs={{0,8},{2,10},{4,12},{6,14},{8,0},{10,2},{12,4},{14,6},{16,24},{18,... | collective-permute-start | bytes 786440 | tf_op jit(solution)/shard_map/ppermute | solution.py:136
  26.2 6.8 %collective-permute-start.9 = (bf16[256,512]{1,0:T(8,128)(2,1)S(1)}, bf16[256,512]{1,0:T(8,128)(2,1)S(1)}, u32[]{:S(2)}, u32[]{:S(2)}) collective-permute-start(bf16[256,512]{1,0:T(8,128)(2,1)S(1)} %combine.2.refs_0_), channel_id=1, source_target_pairs={{0,4},{2,6},{4,0},{6,2},{8,12},{10,14},{12,8},{14,10},{16,20},{18,... | collective-permute-start | bytes 786440 | tf_op jit(solution)/shard_map/ppermute | solution.py:136
  27.7 14.3 %collective-permute-start.6 = (bf16[4,2,128,256]{3,2,1,0:T(8,128)(2,1)S(1)}, bf16[4,2,128,256]{3,2,1,0:T(8,128)(2,1)S(1)}, u32[]{:S(2)}, u32[]{:S(2)}) collective-permute-start(bf16[4,2,128,256]{3,2,1,0:T(8,128)(2,1)S(1)} %pack_normed.3.xa_ref), channel_id=1, source_target_pairs={{0,1},{1,0},{2,3},{3,2},{4,5},{5,4},{6,7},{7,6},{8,9},{9,8},{10,11... | collective-permute-start | bytes 1572872 | tf_op jit(solution)/shard_map/ppermute | solution.py:140
  29.3 7.8 %collective-permute-start.5 = (bf16[4,128,256]{2,1,0:T(8,128)(2,1)S(1)}, bf16[4,128,256]{2,1,0:T(8,128)(2,1)S(1)}, u32[]{:S(2)}, u32[]{:S(2)}) collective-permute-start(bf16[4,128,256]{2,1,0:T(8,128)(2,1)S(1)} %get-tuple-element.56), channel_id=1, source_target_pairs={{0,2},{2,0},{4,6},{6,4},{8,10},{10,8},{12,14},{14,12},{16,18},{18,... | collective-permute-start | bytes 786440 | tf_op jit(solution)/shard_map/ppermute | solution.py:136
  33.2 8.7 %collective-permute-start.14 = (bf16[256,512]{1,0:T(8,128)(2,1)S(1)}, bf16[256,512]{1,0:T(8,128)(2,1)S(1)}, u32[]{:S(2)}, u32[]{:S(2)}) collective-permute-start(bf16[256,512]{1,0:T(8,128)(2,1)S(1)} %combine.3.refs_0_.refs_4_), channel_id=1, source_target_pairs={{0,8},{2,10},{4,12},{6,14},{8,0},{10,2},{12,4},{14,6},{16,24},{18,... | collective-permute-start | bytes 786440 | tf_op jit(solution)/shard_map/ppermute | solution.py:136
  35.0 7.0 %collective-permute-start.11 = (bf16[256,512]{1,0:T(8,128)(2,1)S(1)}, bf16[256,512]{1,0:T(8,128)(2,1)S(1)}, u32[]{:S(2)}, u32[]{:S(2)}) collective-permute-start(bf16[256,512]{1,0:T(8,128)(2,1)S(1)} %collective-permute-done.10.rest_1_.refs_2_), channel_id=1, source_target_pairs={{0,4},{2,6},{4,0},{6,2},{8,12},{10,14},{12,8},{14,10},{16,20},{18,... | collective-permute-start | bytes 786440 | tf_op jit(solution)/shard_map/ppermute | solution.py:136
  36.5 8.2 %collective-permute-start.13 = (bf16[256,512]{1,0:T(8,128)(2,1)S(1)}, bf16[256,512]{1,0:T(8,128)(2,1)S(1)}, u32[]{:S(2)}, u32[]{:S(2)}) collective-permute-start(bf16[256,512]{1,0:T(8,128)(2,1)S(1)} %combine.3.refs_0_.refs_4_), channel_id=1, source_target_pairs={{0,4},{2,6},{4,0},{6,2},{8,12},{10,14},{12,8},{14,10},{16,20},{18,... | collective-permute-start | bytes 786440 | tf_op jit(solution)/shard_map/ppermute | solution.py:136
  42.7 2.0 %collective-permute-start.16 = (f32[64,512]{1,0:T(8,128)S(1)}, f32[64,512]{1,0:T(8,128)S(1)}, u32[]{:S(2)}, u32[]{:S(2)}) collective-permute-start(f32[64,512]{1,0:T(8,128)S(1)} %get-tuple-element.63), channel_id=1, source_target_pairs={{0,2},{2,0},{4,6},{6,4},{8,10},{10,8},{12,14},{14,12},{16,18},{18,... | collective-permute-start | bytes 393224 | tf_op jit(solution)/shard_map/ppermute | solution.py:136
  42.8 1.9 %collective-permute-start.17 = (f32[64,512]{1,0:T(8,128)S(1)}, f32[64,512]{1,0:T(8,128)S(1)}, u32[]{:S(2)}, u32[]{:S(2)}) collective-permute-start(f32[64,512]{1,0:T(8,128)S(1)} %get-tuple-element.64), channel_id=1, source_target_pairs={{0,2},{2,0},{4,6},{6,4},{8,10},{10,8},{12,14},{14,12},{16,18},{18,... | collective-permute-start | bytes 393224 | tf_op jit(solution)/shard_map/ppermute | solution.py:136
  43.3 1.4 %collective-permute-start.18 = (f32[64,512]{1,0:T(8,128)S(1)}, f32[64,512]{1,0:T(8,128)S(1)}, u32[]{:S(2)}, u32[]{:S(2)}) collective-permute-start(f32[64,512]{1,0:T(8,128)S(1)} %get-tuple-element.65), channel_id=1, source_target_pairs={{0,2},{2,0},{4,6},{6,4},{8,10},{10,8},{12,14},{14,12},{16,18},{18,... | collective-permute-start | bytes 393224 | tf_op jit(solution)/shard_map/ppermute | solution.py:136
  43.4 1.5 %collective-permute-start.19 = (f32[64,512]{1,0:T(8,128)S(1)}, f32[64,512]{1,0:T(8,128)S(1)}, u32[]{:S(2)}, u32[]{:S(2)}) collective-permute-start(f32[64,512]{1,0:T(8,128)S(1)} %get-tuple-element.66), channel_id=1, source_target_pairs={{0,2},{2,0},{4,6},{6,4},{8,10},{10,8},{12,14},{14,12},{16,18},{18,... | collective-permute-start | bytes 393224 | tf_op jit(solution)/shard_map/ppermute | solution.py:136
  45.0 9.4 %collective-permute-start.20 = (bf16[1024,512]{1,0:T(8,128)(2,1)S(1)}, bf16[1024,512]{1,0:T(8,128)(2,1)S(1)}, u32[]{:S(2)}, u32[]{:S(2)}) collective-permute-start(bf16[1024,512]{1,0:T(8,128)(2,1)S(1)} %join_places.2), channel_id=1, source_target_pairs={{0,2},{2,0},{4,6},{6,4},{8,10},{10,8},{12,14},{14,12},{16,18},{18,... | collective-permute-start | bytes 3145736 | tf_op jit(solution)/shard_map/ppermute | solution.py:136
  45.4 14.0 %collective-permute-start.7 = (bf16[4,2,128,256]{3,2,1,0:T(8,128)(2,1)S(1)}, bf16[4,2,128,256]{3,2,1,0:T(8,128)(2,1)S(1)}, u32[]{:S(2)}, u32[]{:S(2)}) collective-permute-start(bf16[4,2,128,256]{3,2,1,0:T(8,128)(2,1)S(1)} %join_cores.1.refs_5_.xa_ref), channel_id=1, source_target_pairs={{0,1},{1,0},{2,3},{3,2},{4,5},{5,4},{6,7},{7,6},{8,9},{9,8},{10,11... | collective-permute-start | bytes 1572872 | tf_op jit(solution)/shard_map/ppermute | solution.py:140
  46.3 8.1 %collective-permute-start.15 = (bf16[256,512]{1,0:T(8,128)(2,1)S(1)}, bf16[256,512]{1,0:T(8,128)(2,1)S(1)}, u32[]{:S(2)}, u32[]{:S(2)}) collective-permute-start(bf16[256,512]{1,0:T(8,128)(2,1)S(1)} %collective-permute-done.14.refs_4_.refs_2_.refs_6_), channel_id=1, source_target_pairs={{0,4},{2,6},{4,0},{6,2},{8,12},{10,14},{12,8},{14,10},{16,20},{18,... | collective-permute-start | bytes 786440 | tf_op jit(solution)/shard_map/ppermute | solution.py:136
  47.9 14.4 %collective-permute-start.25 = (bf16[256,512]{1,0:T(8,128)(2,1)S(1)}, bf16[256,512]{1,0:T(8,128)(2,1)S(1)}, u32[]{:S(2)}, u32[]{:S(2)}) collective-permute-start(bf16[256,512]{1,0:T(8,128)(2,1)S(1)} %add_round.2.refs_4_), channel_id=1, source_target_pairs={{0,16},{2,18},{4,20},{6,22},{8,24},{10,26},{12,28},{14,30},{16,0},... | collective-permute-start | bytes 786440 | tf_op jit(solution)/shard_map/ppermute | solution.py:136
  55.1 4.3 %collective-permute-start.21 = (f32[64,512]{1,0:T(8,128)S(1)}, f32[64,512]{1,0:T(8,128)S(1)}, u32[]{:S(2)}, u32[]{:S(2)}) collective-permute-start(f32[64,512]{1,0:T(8,128)S(1)} %get-tuple-element.68), channel_id=1, source_target_pairs={{0,2},{2,0},{4,6},{6,4},{8,10},{10,8},{12,14},{14,12},{16,18},{18,... | collective-permute-start | bytes 393224 | tf_op jit(solution)/shard_map/ppermute | solution.py:136
  55.2 4.2 %collective-permute-start.22 = (f32[64,512]{1,0:T(8,128)S(1)}, f32[64,512]{1,0:T(8,128)S(1)}, u32[]{:S(2)}, u32[]{:S(2)}) collective-permute-start(f32[64,512]{1,0:T(8,128)S(1)} %get-tuple-element.69), channel_id=1, source_target_pairs={{0,2},{2,0},{4,6},{6,4},{8,10},{10,8},{12,14},{14,12},{16,18},{18,... | collective-permute-start | bytes 393224 | tf_op jit(solution)/shard_map/ppermute | solution.py:136
  55.7 3.7 %collective-permute-start.23 = (f32[64,512]{1,0:T(8,128)S(1)}, f32[64,512]{1,0:T(8,128)S(1)}, u32[]{:S(2)}, u32[]{:S(2)}) collective-permute-start(f32[64,512]{1,0:T(8,128)S(1)} %get-tuple-element.70), channel_id=1, source_target_pairs={{0,2},{2,0},{4,6},{6,4},{8,10},{10,8},{12,14},{14,12},{16,18},{18,... | collective-permute-start | bytes 393224 | tf_op jit(solution)/shard_map/ppermute | solution.py:136
  59.4 1.3 %collective-permute-start.24 = (f32[64,512]{1,0:T(8,128)S(1)}, f32[64,512]{1,0:T(8,128)S(1)}, u32[]{:S(2)}, u32[]{:S(2)}) collective-permute-start(f32[64,512]{1,0:T(8,128)S(1)} %get-tuple-element.71), channel_id=1, source_target_pairs={{0,2},{2,0},{4,6},{6,4},{8,10},{10,8},{12,14},{14,12},{16,18},{18,... | collective-permute-start | bytes 393224 | tf_op jit(solution)/shard_map/ppermute | solution.py:136
  62.3 2.7 %collective-permute-start.26 = (bf16[1024,512]{1,0:T(8,128)(2,1)S(1)}, bf16[1024,512]{1,0:T(8,128)(2,1)S(1)}, u32[]{:S(2)}, u32[]{:S(2)}) collective-permute-start(bf16[1024,512]{1,0:T(8,128)(2,1)S(1)} %join_places.3), channel_id=1, source_target_pairs={{0,2},{2,0},{4,6},{6,4},{8,10},{10,8},{12,14},{14,12},{16,18},{18,... | collective-permute-start | bytes 3145736 | tf_op jit(solution)/shard_map/ppermute | solution.py:136
  62.4 15.2 %collective-permute-start.27 = (bf16[256,512]{1,0:T(8,128)(2,1)S(1)}, bf16[256,512]{1,0:T(8,128)(2,1)S(1)}, u32[]{:S(2)}, u32[]{:S(2)}) collective-permute-start(bf16[256,512]{1,0:T(8,128)(2,1)S(1)} %add_round.3.refs_4_.refs_13_), channel_id=1, source_target_pairs={{0,16},{2,18},{4,20},{6,22},{8,24},{10,26},{12,28},{14,30},{16,0},... | collective-permute-start | bytes 786440 | tf_op jit(solution)/shard_map/ppermute | solution.py:136
